TPU v7x, 32 devices: a whole 2x2x4 slice. The times are simulated.
32 devices in a mesh: dp: 4 (over y, x), fetch: 8 (over z, core).
Axes of the slice: x: 2, y: 2, z: 4, core: 2. Of those that a mesh axis runs over, the one named last changes fastest.
Arguments:
- tokens: bfloat16 [4096, 6144], P(('dp', 'fetch')), may hold values from -6 to 6
- routes: int32 [4096, 2], P(('dp', 'fetch')), may hold values from 0 to 7, as said below
- route_probs: float32 [4096, 2], P(('dp', 'fetch')), may hold values from 0.1 to 1
- gate_weight: bfloat16 [6144, 8192], P(None, 'fetch'), may hold values from -0.078125 to 0.078125
- up_weight: bfloat16 [6144, 8192], P(None, 'fetch'), may hold values from -0.078125 to 0.078125
- down_weight: bfloat16 [8192, 6144], P('fetch'), may hold values from -0.0625 to 0.0625
- out_grad: bfloat16 [4096, 6144], P(('dp', 'fetch')), may hold values from -6 to 6
Outputs:
- token_grad: bfloat16 [4096, 6144], P(('dp', 'fetch'))
- gate_grad: bfloat16 [6144, 8192], P('dp', 'fetch')
- up_grad: bfloat16 [6144, 8192], P('dp', 'fetch')
- down_grad: bfloat16 [8192, 6144], P('fetch', 'dp')
Inputs may be any that keep to these rules, and one draw needn't show every extreme that they name: `routes`: the two numbers of a row differ. In every aligned block of 128 rows (the rows of one device) between 16 and 32 rows name expert 0, and one block in every draw has exactly 32 of them.
All inputs are finite; a program needn't handle non-finite values.
Results may differ from a plain program's by a relative error of at most 0.023.
Values may be sent and summed in bfloat16 or wider, within the bound.
No kernel may reach another device: no remote copies, remote signals or barrier semaphores. Data moves between devices by JAX's collectives and lax.ppermute only.
A program may use at most 192 MiB of HBM per device.

v0:
```python
import jax
import jax.numpy as jnp
from jax import lax
from jax.sharding import PartitionSpec as P

CAP = 32


def on_device(tokens, routes, route_probs, gate_weight, up_weight, down_weight, out_grad):
    hits = routes == 0
    coef = jnp.sum(jnp.where(hits, route_probs, jnp.float32(0.0)), axis=1)
    keyed = jnp.where(jnp.any(hits, axis=1), 0, 1).astype(jnp.int32)
    slots = jnp.argsort(keyed, stable=True)[:CAP]
    picked = jnp.take(tokens, slots, axis=0)
    scaled = (coef[slots][:, None] * jnp.take(out_grad, slots, axis=0).astype(jnp.float32)).astype(
        jnp.bfloat16
    )
    gathered = lax.all_gather(picked, "fetch", axis=0, tiled=True)
    gate = jnp.dot(gathered, gate_weight, preferred_element_type=jnp.float32)
    up = jnp.dot(gathered, up_weight, preferred_element_type=jnp.float32)
    sig = jax.nn.sigmoid(gate)
    act = gate * sig
    hidden = (act * up).astype(jnp.bfloat16)
    scaled_all = lax.all_gather(scaled, "fetch", axis=0, tiled=True)
    contract = (((1,), (1,)), ((), ()))
    hidden_grad = lax.dot_general(
        scaled_all, down_weight, contract, preferred_element_type=jnp.float32
    )
    up_rows = (hidden_grad * act).astype(jnp.bfloat16)
    gate_rows = (hidden_grad * up * sig * (1.0 + gate * (1.0 - sig))).astype(jnp.bfloat16)
    term = lax.dot_general(gate_rows, gate_weight, contract, preferred_element_type=jnp.float32)
    input_rows = lax.psum_scatter(
        (
            term + lax.dot_general(up_rows, up_weight, contract, preferred_element_type=jnp.float32)
        ).astype(jnp.bfloat16),
        "fetch",
        scatter_dimension=0,
        tiled=True,
    )
    token_grad = jnp.zeros(tokens.shape, jnp.bfloat16).at[slots].set(input_rows)
    rows_contract = (((0,), (0,)), ((), ()))
    gate_term = lax.dot_general(
        gathered, gate_rows, rows_contract, preferred_element_type=jnp.float32
    )
    up_term = lax.dot_general(gathered, up_rows, rows_contract, preferred_element_type=jnp.float32)
    down_term = lax.dot_general(
        hidden, scaled_all, rows_contract, preferred_element_type=jnp.float32
    )
    gate_sum, up_sum, down_sum = (
        lax.psum_scatter(
            gate_term.astype(jnp.bfloat16), "dp", scatter_dimension=0, tiled=True
        ).astype(jnp.float32),
        lax.psum_scatter(
            up_term.astype(jnp.bfloat16), "dp", scatter_dimension=0, tiled=True
        ).astype(jnp.float32),
        lax.psum_scatter(
            down_term.astype(jnp.bfloat16), "dp", scatter_dimension=1, tiled=True
        ).astype(jnp.float32),
    )
    gate_grad = gate_sum.astype(jnp.bfloat16)
    up_grad = up_sum.astype(jnp.bfloat16)
    down_grad = down_sum.astype(jnp.bfloat16)
    return (token_grad, gate_grad, up_grad, down_grad)


def solution(mesh):
    return jax.shard_map(
        on_device,
        mesh=mesh,
        in_specs=(
            P(("dp", "fetch"), None),
            P(("dp", "fetch"), None),
            P(("dp", "fetch"), None),
            P(None, "fetch"),
            P(None, "fetch"),
            P("fetch", None),
            P(("dp", "fetch"), None),
        ),
        out_specs=(P(("dp", "fetch"), None), P("dp", "fetch"), P("dp", "fetch"), P("fetch", "dp")),
        check_vma=False,
    )
```

profile of v0, /device:TPU:0, one launch (start us, length us, event | category | flops | bytes accessed | tf_op | source)
XLA Modules:
  0.0 550.8 jit_solution(8273724187620284688)
XLA Ops:
  7.2 0.0 copy-start
  7.2 0.0 copy-start.4
  7.2 0.0 copy-start.5
  7.2 0.0 copy-start.3
  7.2 0.0 all-gather.5.cloned.1.call-start
  7.3 0.8 fusion.5
  8.1 2.5 sort.17
  10.7 0.0 copy-start.6
  10.7 0.5 copy-done.6
  11.2 0.0 copy-done
  11.2 0.8 gather_fusion.2
  12.0 0.8 broadcast_select_fusion
  12.8 0.0 all-gather.5.cloned.1.call-update
  12.9 0.0 all-gather.3.cloned.1.call-start
  12.9 0.0 copy-done.4
  12.9 0.0 copy-done.5
  13.0 0.7 gather_fusion
  13.7 0.0 copy-done.3
  13.7 0.8 gather_fusion.1
  14.5 0.9 multiply_convert_fusion.3
  15.4 0.0 all-gather.3.cloned.1.call-update
  15.4 0.0 reduce-scatter.5.cloned.1.call-start
  15.4 38.6 %all-gather.5.cloned.1.call-done = bf16[256,6144]{1,0:T(8,128)(2,1)} async-done(((bf16[32,6144]{1,0:T(8,128)(2,1)}), bf16[256,6144]{1,0:T(8,128)(2,1)}) %all-gather.5.cloned.1.call-update) | async-done | bytes 3145744 | tf_op jit(solution)/shard_map/all_gather | solution.py:18
  54.0 0.0 copy-start.2
  54.0 9.2 %fusion.8 = f32[256,1024]{1,0:T(8,128)S(1)} fusion(bf16[256,6144]{1,0:T(8,128)(2,1)} %all-gather.5.cloned.1.call-done, bf16[6144,1024]{1,0:T(8,128)(2,1)} %param.12), kind=kOutput, calls=%fused_computation.27 | convolution fusion | flops 3221225472 | bytes 16777216 | tf_op jit(solution)/shard_map/dot_general | solution.py:19
  63.2 0.0 copy-done.2
  63.2 6.6 %fusion.7 = f32[256,1024]{1,0:T(8,128)S(1)} fusion(bf16[256,6144]{1,0:T(8,128)(2,1)S(1)} %copy-done.2, bf16[6144,1024]{1,0:T(8,128)(2,1)} %param.13), kind=kOutput, calls=%fused_computation.26 | convolution fusion | flops 3221225472 | bytes 16777216 | tf_op jit(solution)/shard_map/dot_general | solution.py:20
  69.8 23.6 %all-gather.3.cloned.1.call-done = bf16[256,6144]{1,0:T(8,128)(2,1)} async-done(((bf16[32,6144]{1,0:T(8,128)(2,1)}), bf16[256,6144]{1,0:T(8,128)(2,1)}) %all-gather.3.cloned.1.call-update) | async-done | bytes 3145744 | tf_op jit(solution)/shard_map/all_gather | solution.py:24
  93.4 9.2 %multiply_convert_fusion.1 = (bf16[256,1024]{1,0:T(8,128)(2,1)S(1)}, bf16[256,1024]{1,0:T(8,128)(2,1)S(1)}) fusion(f32[256,1024]{1,0:T(8,128)S(1)} %fusion.8, f32[256,1024]{1,0:T(8,128)S(1)} %fusion.7, bf16[256,6144]{1,0:T(8,128)(2,1)} %all-gather.3.cloned.1.call-done, bf16[1024,6144]{1,0:T(8,128)(2,1)} %param.14), kind=kOutput, calls=%fused_computation.10 | convolution fusion | flops 3224633344 | bytes 18874368 | tf_op jit(solution)/shard_map/dot_general | solution.py:26
  102.6 14.7 %fusion.9 = f32[256,6144]{1,0:T(8,128)} fusion(bf16[256,1024]{1,0:T(8,128)(2,1)S(1)} %get-tuple-element.10, bf16[6144,1024]{1,0:T(8,128)(2,1)} %param.12), kind=kOutput, calls=%fused_computation.28 | convolution fusion | flops 3221225472 | bytes 19398656 | tf_op jit(solution)/shard_map/dot_general | solution.py:31
  117.3 15.2 %fusion = bf16[256,6144]{1,0:T(8,128)(2,1)} fusion(f32[256,6144]{1,0:T(8,128)} %fusion.9, bf16[256,1024]{1,0:T(8,128)(2,1)S(1)} %get-tuple-element.9, bf16[6144,1024]{1,0:T(8,128)(2,1)} %param.13), kind=kOutput, calls=%fused_computation.8 | convolution fusion | flops 3224371200 | bytes 22544384 | tf_op jit(solution)/shard_map/dot_general | solution.py:34
  132.6 0.0 reduce-scatter.5.cloned.1.call-update
  132.6 0.2 reduce-scatter.11.cloned.1.call-start
  132.8 8.4 %convolution_convert_fusion = bf16[1024,6144]{1,0:T(8,128)(2,1)} fusion(bf16[256,6144]{1,0:T(8,128)(2,1)} %all-gather.3.cloned.1.call-done, f32[256,1024]{1,0:T(8,128)S(1)} %fusion.7, f32[256,1024]{1,0:T(8,128)S(1)} %fusion.8), kind=kOutput, calls=%fused_computation.4 | convolution fusion | flops 3229089792 | bytes 17825792 | tf_op jit(solution)/shard_map/dot_general | solution.py:46
  141.2 0.0 reduce-scatter.11.cloned.1.call-update
  141.2 0.0 reduce-scatter.9.cloned.1.call-start
  141.3 8.6 %convolution_convert_fusion.1 = bf16[6144,1024]{1,0:T(8,128)(2,1)} fusion(bf16[256,6144]{1,0:T(8,128)(2,1)} %all-gather.5.cloned.1.call-done, bf16[256,1024]{1,0:T(8,128)(2,1)S(1)} %get-tuple-element.9), kind=kOutput, calls=%fused_computation.5 | convolution fusion | flops 3227516928 | bytes 16252928 | tf_op jit(solution)/shard_map/dot_general | solution.py:45
  149.8 0.0 reduce-scatter.9.cloned.1.call-update
  149.9 0.0 reduce-scatter.7.cloned.1.call-start
  149.9 8.5 %convolution_convert_fusion.2 = bf16[6144,1024]{1,0:T(8,128)(2,1)} fusion(bf16[256,6144]{1,0:T(8,128)(2,1)} %all-gather.5.cloned.1.call-done, bf16[256,1024]{1,0:T(8,128)(2,1)S(1)} %get-tuple-element.10), kind=kOutput, calls=%fused_computation.6 | convolution fusion | flops 3227516928 | bytes 16252928 | tf_op jit(solution)/shard_map/dot_general | solution.py:42
  158.4 0.0 reduce-scatter.7.cloned.1.call-update
  158.4 0.0 copy-start.1
  158.4 13.5 %reduce-scatter.5.cloned.1.call-done = bf16[32,6144]{1,0:T(8,128)(2,1)} async-done(((bf16[256,6144]{1,0:T(8,128)(2,1)}), bf16[32,6144]{1,0:T(8,128)(2,1)}) %reduce-scatter.5.cloned.1.call-update) | async-done | bytes 393232 | tf_op jit(solution)/shard_map/reduce_scatter | solution.py:32
  172.0 3.0 scatter_custom_fusion
  174.9 120.4 %reduce-scatter.11.cloned.1.call-done = bf16[1024,1536]{1,0:T(8,128)(2,1)} async-done(((bf16[1024,6144]{1,0:T(8,128)(2,1)}), bf16[1024,1536]{1,0:T(8,128)(2,1)}) %reduce-scatter.11.cloned.1.call-update) | async-done | bytes 3145744 | tf_op jit(solution)/shard_map/reduce_scatter | solution.py:56
  295.4 124.3 %reduce-scatter.9.cloned.1.call-done = bf16[1536,1024]{1,0:T(8,128)(2,1)} async-done(((bf16[6144,1024]{1,0:T(8,128)(2,1)}), bf16[1536,1024]{1,0:T(8,128)(2,1)}) %reduce-scatter.9.cloned.1.call-update) | async-done | bytes 3145744 | tf_op jit(solution)/shard_map/reduce_scatter | solution.py:53
  419.7 124.3 %reduce-scatter.7.cloned.1.call-done = bf16[1536,1024]{1,0:T(8,128)(2,1)} async-done(((bf16[6144,1024]{1,0:T(8,128)(2,1)}), bf16[1536,1024]{1,0:T(8,128)(2,1)}) %reduce-scatter.7.cloned.1.call-update) | async-done | bytes 3145744 | tf_op jit(solution)/shard_map/reduce_scatter | solution.py:50
  543.9 0.0 copy-done.1
  (5 shorter events, 0.0 us)
Async XLA Ops:
  7.2 4.0 copy-start
  7.2 5.7 %copy-start.4 = (s32[128,2]{0,1:T(2,128)S(1)}, s32[128,2]{0,1:T(2,128)}, u32[]{:S(2)}) copy-start(s32[128,2]{0,1:T(2,128)} %param.10) | copy-start | bytes 3076
  7.2 5.7 %copy-start.5 = (f32[128,2]{0,1:T(2,128)S(1)}, f32[128,2]{0,1:T(2,128)}, u32[]{:S(2)}) copy-start(f32[128,2]{0,1:T(2,128)} %param.11) | copy-start | bytes 3076
  7.2 6.5 %copy-start.3 = (bf16[128,6144]{1,0:T(8,128)(2,1)S(1)}, bf16[128,6144]{1,0:T(8,128)(2,1)}, u32[]{:S(2)}) copy-start(bf16[128,6144]{1,0:T(8,128)(2,1)} %param.15) | copy-start | bytes 4718596
  7.2 46.8 %all-gather.5.cloned.1.call-start = ((), (), s32[]{:S(2)}) async-start(), calls=%async_computation.5 | async-start | bytes 3538944 | tf_op jit(solution)/shard_map/all_gather | solution.py:18
  10.7 0.5 copy-start.6
  12.9 80.5 %all-gather.3.cloned.1.call-start = ((), (), s32[]{:S(2)}) async-start(), calls=%async_computation.4 | async-start | bytes 3538944 | tf_op jit(solution)/shard_map/all_gather | solution.py:24
  15.4 156.6 %reduce-scatter.5.cloned.1.call-start = ((), (), s32[]{:S(2)}) async-start(), calls=%async_computation.6 | async-start | bytes 3538944 | tf_op jit(solution)/shard_map/reduce_scatter | solution.py:32
  54.0 9.2 %copy-start.2 = (bf16[256,6144]{1,0:T(8,128)(2,1)S(1)}, bf16[256,6144]{1,0:T(8,128)(2,1)}, u32[]{:S(2)}) copy-start(bf16[256,6144]{1,0:T(8,128)(2,1)} %all-gather.5.cloned.1.call-done) | copy-start | bytes 9437188
  132.6 162.8 %reduce-scatter.11.cloned.1.call-start = ((), (), s32[]{:S(2)}) async-start(), calls=%async_computation.9 | async-start | bytes 15728640 | tf_op jit(solution)/shard_map/reduce_scatter | solution.py:56
  141.2 278.4 %reduce-scatter.9.cloned.1.call-start = ((), (), s32[]{:S(2)}) async-start(), calls=%async_computation.8 | async-start | bytes 15728640 | tf_op jit(solution)/shard_map/reduce_scatter | solution.py:53
  149.9 394.1 %reduce-scatter.7.cloned.1.call-start = ((), (), s32[]{:S(2)}) async-start(), calls=%async_computation.7 | async-start | bytes 15728640 | tf_op jit(solution)/shard_map/reduce_scatter | solution.py:50
  158.4 385.6 %copy-start.1 = (bf16[128,6144]{1,0:T(8,128)(2,1)S(1)}, bf16[128,6144]{1,0:T(8,128)(2,1)}, u32[]{:S(2)}) copy-start(bf16[128,6144]{1,0:T(8,128)(2,1)} %param.9) | copy-start | bytes 4718596
Sparse Core Ops, SparseCore 0:
  13.0 40.9 all-gather.4
  56.2 37.1 all-gather.2
  132.7 39.1 reduce-scatter.4
  175.5 119.8 reduce-scatter.10
  298.9 120.7 reduce-scatter.8
  423.2 120.7 reduce-scatter.6
where the time goes:
time: 551 us
  waiting for transfers between devices  445 us (81%)
  matrix products  80.3 us (15%)
  between operations  14.2 us (3%)
  local copies, waits for them, and re-layouts  5.81 us (1%)
    reduce_scatter x1, waiting for transfers between devices, on_device(): lax.psum_scatter(gate_term.astype(jnp.bfloat16), 'dp', scatter_dimension=...  124 us
    reduce_scatter x1, waiting for transfers between devices, on_device(): lax.psum_scatter(up_term.astype(jnp.bfloat16), 'dp', scatter_dimension=0,...  124 us
    reduce_scatter x1, waiting for transfers between devices, on_device(): lax.psum_scatter(down_term.astype(jnp.bfloat16), 'dp', scatter_dimension=...  120 us
    all_gather x1, waiting for transfers between devices, on_device(): gathered = lax.all_gather(picked, 'fetch', axis=0, tiled=True)  38.6 us
    all_gather x1, waiting for transfers between devices, on_device(): scaled_all = lax.all_gather(scaled, 'fetch', axis=0, tiled=True)  23.6 us
    dot_general x1, matrix products, on_device(): lax.dot_general(up_rows, up_weight, contract, preferred_element_type=jnp....  15.2 us
    dot_general x1, matrix products, on_device(): lax.dot_general(gate_rows, gate_weight, contract, preferred_element_type=...  14.7 us
    reduce_scatter x1, waiting for transfers between devices, on_device(): lax.psum_scatter((term + lax.dot_general(up_rows, up_weight, contract, pr...  13.5 us
  transfers between devices with their start and end apart: 6, of which 6 were waited for; matrix products, arithmetic and copies ran while one was open for 8% of the time, Pallas kernels for 0%

commit v1 on v0

v1 whole, which is shorter than its diff:
```python
import functools

import jax
import jax.numpy as jnp
from jax import lax
from jax.experimental import pallas as pl
from jax.experimental.pallas import tpu as pltpu
from jax.sharding import PartitionSpec as P

CAP = 32
F32, BF16 = jnp.float32, jnp.bfloat16
ROWS = (((0,), (0,)), ((), ()))
LAST = (((1,), (1,)), ((), ()))
VMEM = pl.BlockSpec(memory_space=pltpu.VMEM)


def mm(a, b, dims=(((1,), (0,)), ((), ()))):
    return lax.dot_general(a, b, dims, preferred_element_type=F32)


def pick_kernel(routes, probs, tokens, out_grad, sel_out, picked, scaled):
    n = tokens.shape[0]
    hits = routes[...] == 0
    coef = jnp.sum(jnp.where(hits, probs[...], 0.0), axis=0, keepdims=True)
    routed = jnp.sum(jnp.where(hits, 1.0, 0.0), axis=0, keepdims=True) > 0.5
    flags = jnp.broadcast_to(jnp.where(routed, 1.0, 0.0), (8, n))
    before = lax.broadcasted_iota(jnp.int32, (n, n), 0) <= lax.broadcasted_iota(jnp.int32, (n, n), 1)
    upto = mm(flags.astype(BF16), jnp.where(before, 1.0, 0.0).astype(BF16))[:1]
    count = jnp.sum(flags[:1], axis=1, keepdims=True)
    lane = lax.broadcasted_iota(jnp.int32, (1, n), 1).astype(F32)
    rank = jnp.where(routed, upto - 1.0, count + lane - upto)
    sel = rank == lax.broadcasted_iota(jnp.int32, (CAP, n), 0).astype(F32)
    scale = jnp.sum(jnp.where(sel, coef, 0.0), axis=1, keepdims=True)
    sel = jnp.where(sel, 1.0, 0.0).astype(BF16)
    sel_out[...] = sel
    picked[...] = mm(sel, tokens[...]).astype(BF16)
    scaled[...] = (scale * mm(sel, out_grad[...])).astype(BF16)


def pick(tokens, routes, probs, out_grad):
    d = tokens.shape[1]
    rows = jax.ShapeDtypeStruct((CAP, d), BF16)
    return pl.pallas_call(
        pick_kernel,
        out_shape=(jax.ShapeDtypeStruct((CAP, tokens.shape[0]), BF16), rows, rows),
        in_specs=[VMEM] * 4,
        out_specs=(VMEM,) * 3,
        compiler_params=pltpu.CompilerParams(vmem_limit_bytes=32 << 20),
    )(routes.T, probs.T, tokens, out_grad)


def put_kernel(sel, *refs):
    *parts, out = refs
    total = parts[0][...].astype(F32)
    for part in parts[1:]:
        total = total + part[...].astype(F32)
    out[...] = mm(sel[...], total.astype(BF16), ROWS).astype(BF16)


def put(sel, parts):
    d = parts[0].shape[1]
    return pl.pallas_call(
        put_kernel,
        out_shape=jax.ShapeDtypeStruct((sel.shape[1], d), BF16),
        in_specs=[VMEM] * (1 + len(parts)),
        out_specs=VMEM,
        compiler_params=pltpu.CompilerParams(vmem_limit_bytes=32 << 20),
    )(sel, *parts)


def on_device(tokens, routes, route_probs, gate_weight, up_weight, down_weight, out_grad):
    n_dp, n_fetch = lax.axis_size("dp"), lax.axis_size("fetch")
    chips = n_fetch // 2

    def move(x, hop):
        pairs = [(2 * z + c, 2 * ((z + hop) % chips) + c) for z in range(chips) for c in range(2)]
        return lax.ppermute(x, "fetch", pairs)

    def swap(x):
        return lax.ppermute(x, "fetch", [(k, k ^ 1) for k in range(n_fetch)])

    def across(x, bits):
        return lax.ppermute(x, "dp", [(k, k ^ bits) for k in range(n_dp)])

    offsets = [0]
    for s in range(1, chips // 2 + 1):
        offsets += [-s] if 2 * s == chips else [-s, s]

    def ring(x):
        blocks = {0: x}
        for s in range(1, chips // 2 + 1):
            blocks[-s] = move(blocks[1 - s], 1)
            if 2 * s != chips:
                blocks[s] = move(blocks[s - 1], -1)
        mine = jnp.concatenate([blocks[o] for o in offsets])
        return mine, swap(mine)

    def spread(x):
        if n_dp != 4:
            return lax.all_gather(x, "dp", axis=0, tiled=True)
        half = x.shape[0] // 2
        by_x, by_y = across(x, 1), across(x, 2)
        far = [across(by_x[:half], 2), across(by_y[half:], 1)]
        return jnp.concatenate([x, by_x, by_y] + far)

    def slices(x):
        width = x.shape[1] // n_dp
        if n_dp != 4:
            got = lax.all_to_all(x, "dp", 1, 0, tiled=True)
            got = got.reshape(n_dp, -1, width)
        else:
            me = lax.axis_index("dp")
            cut = [lax.dynamic_slice_in_dim(x, (me ^ k) * width, width, 1) for k in range(4)]
            got = jnp.stack([cut[0]] + [across(cut[k], k) for k in range(1, 4)])
        return jnp.concatenate([got, swap(got)], axis=1).reshape(-1, width)

    sel, picked, scaled = pick(tokens, routes, route_probs, out_grad)
    picked_mine, picked_theirs = ring(picked)
    scaled_mine, scaled_theirs = ring(scaled)
    rows = jnp.concatenate([picked_mine, picked_theirs])
    grads = jnp.concatenate([scaled_mine, scaled_theirs])
    picked_slices = slices(picked_mine)
    scaled_slices = slices(scaled_mine)

    gate = mm(rows, gate_weight)
    up = mm(rows, up_weight)
    sig = jax.nn.sigmoid(gate)
    act = gate * sig
    hidden = spread((act * up).astype(BF16))
    hidden_grad = mm(grads, down_weight, LAST)
    up_rows = (hidden_grad * act).astype(BF16)
    gate_rows = (hidden_grad * up * sig * (1.0 + gate * (1.0 - sig))).astype(BF16)
    gate_all, up_all = spread(gate_rows), spread(up_rows)

    term = (mm(gate_rows, gate_weight, LAST) + mm(up_rows, up_weight, LAST)).astype(BF16)
    half = CAP * chips
    term = (term[:half].astype(F32) + swap(term[half:]).astype(F32)).astype(BF16)
    parts = [term[:CAP]]
    for k, o in enumerate(offsets[1:], 1):
        parts.append(move(term[k * CAP : (k + 1) * CAP], o))
    token_grad = put(sel, parts)

    down_grad = mm(hidden, scaled_slices, ROWS).astype(BF16)
    gate_grad = mm(picked_slices, gate_all, ROWS).astype(BF16)
    up_grad = mm(picked_slices, up_all, ROWS).astype(BF16)
    return token_grad, gate_grad, up_grad, down_grad


def solution(mesh):
    return jax.shard_map(
        on_device,
        mesh=mesh,
        in_specs=(
            P(("dp", "fetch"), None),
            P(("dp", "fetch"), None),
            P(("dp", "fetch"), None),
            P(None, "fetch"),
            P(None, "fetch"),
            P("fetch", None),
            P(("dp", "fetch"), None),
        ),
        out_specs=(P(("dp", "fetch"), None), P("dp", "fetch"), P("dp", "fetch"), P("fetch", "dp")),
        check_vma=False,
    )
```

time: 551 us -> 233 us (0.42)
  the two profiles are of different devices: /device:TPU:0 before, /device:TPU:8 now
where the time goes in v1:
time: 233 us; the launch traced here: 232 us
  waiting for transfers between devices  117 us (50%)
  matrix products  56.5 us (24%)
  starting transfers between devices  29.8 us (13%)
  local copies, waits for them, and re-layouts  18.9 us (8%)
  other arithmetic  6.48 us (3%)
  Pallas kernels  2.43 us (1%)
    ppermute x9, waiting for transfers between devices, move(): return lax.ppermute(x, 'fetch', pairs)  70 us
    dot_general x8, matrix products, mm(): return lax.dot_general(a, b, dims, preferred_element_type=F32)  56.5 us
    ppermute x18, waiting for transfers between devices, across(): return lax.ppermute(x, 'dp', [(k, k ^ bits) for k in range(n_dp)])  47 us
    ppermute x18, starting transfers between devices, across(): return lax.ppermute(x, 'dp', [(k, k ^ bits) for k in range(n_dp)])  21.7 us
    unnamed x38, local copies, waits for them, and re-layouts  11.7 us
    ppermute x9, starting transfers between devices, move(): return lax.ppermute(x, 'fetch', pairs)  8.02 us
  transfers between devices with their start and end apart: 32, of which 18 were waited for; matrix products, arithmetic and copies ran while one was open for 33% of the time, Pallas kernels for 0%

profile of v1, /device:TPU:8, one launch (start us, length us, event | category | flops | bytes accessed | tf_op | source)
XLA Modules:
  0.0 232.1 jit_solution(4543483985479799436)
XLA Ops:
  0.6 1.4 copy-done
  2.0 1.4 copy-done.1
  5.5 2.0 collective-permute-start
  7.6 2.0 collective-permute-start.5
  10.5 17.5 %collective-permute-done = bf16[32,6144]{1,0:T(8,128)(2,1)S(1)} collective-permute-done((bf16[32,6144]{1,0:T(8,128)(2,1)S(1)}, bf16[32,6144]{1,0:T(8,128)(2,1)S(1)}, u32[]{:S(2)}, u32[]{:S(2)}) %collective-permute-start) | collective-permute-done | bytes 393248 | tf_op jit(solution)/shard_map/ppermute | solution.py:77
  28.8 16.1 %collective-permute-done.4 = bf16[32,6144]{1,0:T(8,128)(2,1)S(1)} collective-permute-done((bf16[32,6144]{1,0:T(8,128)(2,1)S(1)}, bf16[32,6144]{1,0:T(8,128)(2,1)S(1)}, u32[]{:S(2)}, u32[]{:S(2)}) %collective-permute-start.4) | collective-permute-done | bytes 393248 | tf_op jit(solution)/shard_map/ppermute | solution.py:77
  46.6 6.7 %collective-permute-done.2 = bf16[32,6144]{1,0:T(8,128)(2,1)S(1)} collective-permute-done((bf16[32,6144]{1,0:T(8,128)(2,1)S(1)}, bf16[32,6144]{1,0:T(8,128)(2,1)S(1)}, u32[]{:S(2)}, u32[]{:S(2)}) %collective-permute-start.2) | collective-permute-done | bytes 393248 | tf_op jit(solution)/shard_map/ppermute | solution.py:77
  54.2 2.5 %collective-permute-start.30 = (bf16[128,1536]{1,0:T(8,128)(2,1)S(1)}, bf16[128,1536]{1,0:T(8,128)(2,1)S(1)}, u32[]{:S(2)}, u32[]{:S(2)}) collective-permute-start(bf16[128,1536]{1,0:T(8,128)(2,1)S(1)} %get-tuple-element.21), channel_id=1, source_target_pairs={{0,24},{8,16},{16,8},{24,0},{1,25},{9,17},{17,9},{25,1},{2,26},{10... | collective-permute-start | bytes 1179656 | tf_op jit(solution)/shard_map/ppermute | solution.py:83
  57.8 2.9 %collective-permute-done.6 = bf16[32,6144]{1,0:T(8,128)(2,1)S(1)} collective-permute-done((bf16[32,6144]{1,0:T(8,128)(2,1)S(1)}, bf16[32,6144]{1,0:T(8,128)(2,1)S(1)}, u32[]{:S(2)}, u32[]{:S(2)}) %collective-permute-start.6) | collective-permute-done | bytes 393248 | tf_op jit(solution)/shard_map/ppermute | solution.py:77
  60.8 2.5 %collective-permute-start.14 = (bf16[128,1536]{1,0:T(8,128)(2,1)S(1)}, bf16[128,1536]{1,0:T(8,128)(2,1)S(1)}, u32[]{:S(2)}, u32[]{:S(2)}) collective-permute-start(bf16[128,1536]{1,0:T(8,128)(2,1)S(1)} %get-tuple-element.25), channel_id=1, source_target_pairs={{0,24},{8,16},{16,8},{24,0},{1,25},{9,17},{17,9},{25,1},{2,26},{10... | collective-permute-start | bytes 1179656 | tf_op jit(solution)/shard_map/ppermute | solution.py:83
  63.3 3.8 %collective-permute-done.30 = bf16[128,1536]{1,0:T(8,128)(2,1)S(1)} collective-permute-done((bf16[128,1536]{1,0:T(8,128)(2,1)S(1)}, bf16[128,1536]{1,0:T(8,128)(2,1)S(1)}, u32[]{:S(2)}, u32[]{:S(2)}) %collective-permute-start.30) | collective-permute-done | bytes 393248 | tf_op jit(solution)/shard_map/ppermute | solution.py:83
  67.1 1.5 collective-permute-start.13
  68.7 6.9 %collective-permute-done.29 = bf16[128,1536]{1,0:T(8,128)(2,1)S(1)} collective-permute-done((bf16[128,1536]{1,0:T(8,128)(2,1)S(1)}, bf16[128,1536]{1,0:T(8,128)(2,1)S(1)}, u32[]{:S(2)}, u32[]{:S(2)}) %collective-permute-start.29) | collective-permute-done | bytes 393248 | tf_op jit(solution)/shard_map/ppermute | solution.py:83
  75.6 1.5 collective-permute-start.12
  77.1 1.3 pad_maximum_fusion.3
  78.4 5.6 %collective-permute-done.14 = bf16[128,1536]{1,0:T(8,128)(2,1)S(1)} collective-permute-done((bf16[128,1536]{1,0:T(8,128)(2,1)S(1)}, bf16[128,1536]{1,0:T(8,128)(2,1)S(1)}, u32[]{:S(2)}, u32[]{:S(2)}) %collective-permute-start.14) | collective-permute-done | bytes 393248 | tf_op jit(solution)/shard_map/ppermute | solution.py:83
  84.0 8.0 %collective-permute-done.13 = bf16[128,1536]{1,0:T(8,128)(2,1)S(1)} collective-permute-done((bf16[128,1536]{1,0:T(8,128)(2,1)S(1)}, bf16[128,1536]{1,0:T(8,128)(2,1)S(1)}, u32[]{:S(2)}, u32[]{:S(2)}) %collective-permute-start.13) | collective-permute-done | bytes 393248 | tf_op jit(solution)/shard_map/ppermute | solution.py:83
  92.1 1.3 pad_maximum_fusion.2
  93.5 1.3 constant_dynamic-update-slice_fusion.4
  94.7 7.4 %fusion.3 = f32[256,1024]{1,0:T(8,128)S(1)} fusion(bf16[256,6144]{1,0:T(8,128)(2,1)} %constant_dynamic-update-slice_fusion.4, bf16[1024,6144]{1,0:T(8,128)(2,1)} %param.12), kind=kOutput, calls=%fused_computation.57 | convolution fusion | flops 3221225472 | bytes 16777216 | tf_op jit(solution)/shard_map/dot_general | solution.py:18
  102.3 6.6 %fusion.4 = f32[256,1024]{1,0:T(8,128)S(1)} fusion(bf16[256,6144]{1,0:T(8,128)(2,1)S(1)} %constant_dynamic-update-slice_fusion.13, bf16[6144,1024]{1,0:T(8,128)(2,1)} %param.10), kind=kOutput, calls=%fused_computation.58 | convolution fusion | flops 3221225472 | bytes 16777216 | tf_op jit(solution)/shard_map/dot_general | solution.py:18
  109.3 1.2 slice-done.2
  110.5 5.2 %constant_dynamic-update-slice_fusion.32 = (bf16[1024,1024]{1,0:T(8,128)(2,1)}, bf16[256,1024]{1,0:T(8,128)(2,1)}, bf16[1024,1024]{1,0:T(8,128)(2,1)}, bf16[256,...) fusion(f32[256,1024]{1,0:T(8,128)S(1)} %fusion.4, f32[256,1024]{1,0:T(8,128)S(1)} %fusion.3, ...), kind=kOutput, calls=%fused_computation.49 | convolution fusion | flops 3225157632 | bytes 20971520 | tf_op jit(solution)/shard_map/dot_general | solution.py:18
  115.7 1.4 collective-permute-start.25
  117.9 1.3 collective-permute-start.16
  119.2 10.9 %fusion.5 = f32[256,6144]{1,0:T(8,128)} fusion(bf16[256,1024]{1,0:T(8,128)(2,1)} %get-tuple-element.17, bf16[6144,1024]{1,0:T(8,128)(2,1)} %param.10), kind=kOutput, calls=%fused_computation.59 | convolution fusion | flops 3221225472 | bytes 19398656 | tf_op jit(solution)/shard_map/dot_general | solution.py:18
  130.0 11.6 %fusion = bf16[256,6144]{1,0:T(8,128)(2,1)} fusion(f32[256,6144]{1,0:T(8,128)} %fusion.5, bf16[256,1024]{1,0:T(8,128)(2,1)} %get-tuple-element.19, bf16[6144,1024]{1,0:T(8,128)(2,1)} %param.11), kind=kOutput, calls=%fused_computation.1 | convolution fusion | flops 3224371200 | bytes 22544384 | tf_op jit(solution)/shard_map/dot_general | solution.py:18
  141.7 1.5 slice.49
  143.9 1.5 pad_maximum_fusion.1
  145.5 1.5 collective-permute-start.20
  147.0 1.9 pad_maximum_fusion
  152.8 1.1 constant_dynamic-update-slice_fusion.30
  153.9 1.3 collective-permute-start.27
  156.3 2.0 collective-permute-done.17
  160.4 1.4 collective-permute-start.18
  161.9 7.7 %collective-permute-done.21 = bf16[256,1024]{1,0:T(8,128)(2,1)S(1)} collective-permute-done((bf16[256,1024]{1,0:T(8,128)(2,1)S(1)}, bf16[256,1024]{1,0:T(8,128)(2,1)S(1)}, u32[]{:S(2)}, u32[]{:S(2)}) %collective-permute-start.21) | collective-permute-done | bytes 524320 | tf_op jit(solution)/shard_map/ppermute | solution.py:83
  170.4 4.8 %collective-permute-done.26 = bf16[128,1024]{1,0:T(8,128)(2,1)S(1)} collective-permute-done((bf16[128,1024]{1,0:T(8,128)(2,1)S(1)}, bf16[128,1024]{1,0:T(8,128)(2,1)S(1)}, u32[]{:S(2)}, u32[]{:S(2)}) %collective-permute-start.26) | collective-permute-done | bytes 262176 | tf_op jit(solution)/shard_map/ppermute | solution.py:83
  175.8 1.5 collective-permute-start.23
  177.4 3.4 %collective-permute-done.18 = bf16[128,1024]{1,0:T(8,128)(2,1)S(1)} collective-permute-done((bf16[128,1024]{1,0:T(8,128)(2,1)S(1)}, bf16[128,1024]{1,0:T(8,128)(2,1)S(1)}, u32[]{:S(2)}, u32[]{:S(2)}) %collective-permute-start.18) | collective-permute-done | bytes 262176 | tf_op jit(solution)/shard_map/ppermute | solution.py:83
  180.9 4.2 %collective-permute-done.22 = bf16[128,1024]{1,0:T(8,128)(2,1)S(1)} collective-permute-done((bf16[128,1024]{1,0:T(8,128)(2,1)S(1)}, bf16[128,1024]{1,0:T(8,128)(2,1)S(1)}, u32[]{:S(2)}, u32[]{:S(2)}) %collective-permute-start.22) | collective-permute-done | bytes 262176 | tf_op jit(solution)/shard_map/ppermute | solution.py:83
  185.1 4.9 %convolution_convert_fusion.1 = bf16[1536,1024]{1,0:T(8,128)(2,1)} fusion(bf16[1024,1536]{1,0:T(8,128)(2,1)S(1)} %bitcast.33, bf16[1024,1024]{1,0:T(8,128)(2,1)S(1)} %constant_dynamic-update-slice_fusion.23), kind=kOutput, calls=%fused_computation.3 | convolution fusion | flops 3222798336 | bytes 8388608 | tf_op jit(solution)/shard_map/dot_general | solution.py:18
  190.0 4.9 %convolution_convert_fusion.2 = bf16[1536,1024]{1,0:T(8,128)(2,1)} fusion(bf16[1024,1536]{1,0:T(8,128)(2,1)S(1)} %bitcast.34, bf16[1024,1024]{1,0:T(8,128)(2,1)S(1)} %constant_dynamic-update-slice_fusion.18), kind=kOutput, calls=%fused_computation.4 | convolution fusion | flops 3222798336 | bytes 8388608 | tf_op jit(solution)/shard_map/dot_general | solution.py:18
  197.3 1.1 collective-permute-start.9
  198.5 5.0 %convolution_convert_fusion = bf16[1024,1536]{1,0:T(8,128)(2,1)} fusion(bf16[1024,1024]{1,0:T(8,128)(2,1)S(1)} %constant_dynamic-update-slice_fusion.28, bf16[1024,1536]{1,0:T(8,128)(2,1)S(1)} %bitcast.32), kind=kOutput, calls=%fused_computation.2 | convolution fusion | flops 3222798336 | bytes 8388608 | tf_op jit(solution)/shard_map/dot_general | solution.py:18
  203.5 10.7 %collective-permute-done.11.refs_3_ = bf16[32,6144]{1,0:T(8,128)(2,1)S(1)} collective-permute-done((bf16[32,6144]{1,0:T(8,128)(2,1)S(1)}, bf16[32,6144]{1,0:T(8,128)(2,1)S(1)}, u32[]{:S(2)}, u32[]{:S(2)}) %collective-permute-start.11) | collective-permute-done | bytes 393248 | tf_op jit(solution)/shard_map/ppermute | solution.py:77
  214.2 14.7 %collective-permute-done.10.refs_2_ = bf16[32,6144]{1,0:T(8,128)(2,1)S(1)} collective-permute-done((bf16[32,6144]{1,0:T(8,128)(2,1)S(1)}, bf16[32,6144]{1,0:T(8,128)(2,1)S(1)}, u32[]{:S(2)}, u32[]{:S(2)}) %collective-permute-start.10) | collective-permute-done | bytes 393248 | tf_op jit(solution)/shard_map/ppermute | solution.py:77
  228.9 1.4 collective-permute-done.9.refs_1_
  230.3 1.7 shard_map.103
  (87 shorter events, 20.8 us)
Async XLA Ops:
  0.6 1.4 copy-start
  2.0 1.4 copy-start.1
  3.4 0.7 copy-start.2
  4.1 0.7 copy-start.3
  5.5 40.3 %collective-permute-start.1 = (bf16[32,6144]{1,0:T(8,128)(2,1)S(1)}, bf16[32,6144]{1,0:T(8,128)(2,1)S(1)}, u32[]{:S(2)}, u32[]{:S(2)}) collective-permute-start(bf16[32,6144]{1,0:T(8,128)(2,1)S(1)} %get-tuple-element.8), channel_id=1, source_target_pairs={{0,6},{1,7},{2,0},{3,1},{4,2},{5,3},{6,4},{7,5},{8,14},{9,15},{10,... | collective-permute-start | bytes 1179656 | tf_op jit(solution)/shard_map/ppermute | solution.py:77
  5.5 22.4 %collective-permute-start = (bf16[32,6144]{1,0:T(8,128)(2,1)S(1)}, bf16[32,6144]{1,0:T(8,128)(2,1)S(1)}, u32[]{:S(2)}, u32[]{:S(2)}) collective-permute-start(bf16[32,6144]{1,0:T(8,128)(2,1)S(1)} %get-tuple-element.8), channel_id=1, source_target_pairs={{0,2},{1,3},{2,4},{3,5},{4,6},{5,7},{6,0},{7,1},{8,10},{9,11},{10,... | collective-permute-start | bytes 1179656 | tf_op jit(solution)/shard_map/ppermute | solution.py:77
  7.6 39.0 %collective-permute-start.5 = (bf16[32,6144]{1,0:T(8,128)(2,1)S(1)}, bf16[32,6144]{1,0:T(8,128)(2,1)S(1)}, u32[]{:S(2)}, u32[]{:S(2)}) collective-permute-start(bf16[32,6144]{1,0:T(8,128)(2,1)S(1)} %get-tuple-element.9), channel_id=1, source_target_pairs={{0,6},{1,7},{2,0},{3,1},{4,2},{5,3},{6,4},{7,5},{8,14},{9,15},{10,... | collective-permute-start | bytes 1179656 | tf_op jit(solution)/shard_map/ppermute | solution.py:77
  9.6 35.3 %collective-permute-start.4 = (bf16[32,6144]{1,0:T(8,128)(2,1)S(1)}, bf16[32,6144]{1,0:T(8,128)(2,1)S(1)}, u32[]{:S(2)}, u32[]{:S(2)}) collective-permute-start(bf16[32,6144]{1,0:T(8,128)(2,1)S(1)} %get-tuple-element.9), channel_id=1, source_target_pairs={{0,2},{1,3},{2,4},{3,5},{4,6},{5,7},{6,0},{7,1},{8,10},{9,11},{10,... | collective-permute-start | bytes 1179656 | tf_op jit(solution)/shard_map/ppermute | solution.py:77
  28.0 25.3 %collective-permute-start.2 = (bf16[32,6144]{1,0:T(8,128)(2,1)S(1)}, bf16[32,6144]{1,0:T(8,128)(2,1)S(1)}, u32[]{:S(2)}, u32[]{:S(2)}) collective-permute-start(bf16[32,6144]{1,0:T(8,128)(2,1)S(1)} %collective-permute-done), channel_id=1, source_target_pairs={{0,2},{1,3},{2,4},{3,5},{4,6},{5,7},{6,0},{7,1},{8,10},{9,11},{10,... | collective-permute-start | bytes 1179656 | tf_op jit(solution)/shard_map/ppermute | solution.py:77
  44.9 15.8 %collective-permute-start.6 = (bf16[32,6144]{1,0:T(8,128)(2,1)S(1)}, bf16[32,6144]{1,0:T(8,128)(2,1)S(1)}, u32[]{:S(2)}, u32[]{:S(2)}) collective-permute-start(bf16[32,6144]{1,0:T(8,128)(2,1)S(1)} %collective-permute-done.4), channel_id=1, source_target_pairs={{0,2},{1,3},{2,4},{3,5},{4,6},{5,7},{6,0},{7,1},{8,10},{9,11},{10,... | collective-permute-start | bytes 1179656 | tf_op jit(solution)/shard_map/ppermute | solution.py:77
  54.1 39.4 %collective-permute-start.3 = (bf16[128,6144]{1,0:T(8,128)(2,1)S(1)}, bf16[128,6144]{1,0:T(8,128)(2,1)S(1)}, u32[]{:S(2)}, u32[]{:S(2)}) collective-permute-start(bf16[128,6144]{1,0:T(8,128)(2,1)S(1)} %get-tuple-element.32), channel_id=1, source_target_pairs={{0,1},{1,0},{2,3},{3,2},{4,5},{5,4},{6,7},{7,6},{8,9},{9,8},{10,11... | collective-permute-start | bytes 4718600 | tf_op jit(solution)/shard_map/ppermute | solution.py:80
  54.2 12.9 %collective-permute-start.30 = (bf16[128,1536]{1,0:T(8,128)(2,1)S(1)}, bf16[128,1536]{1,0:T(8,128)(2,1)S(1)}, u32[]{:S(2)}, u32[]{:S(2)}) collective-permute-start(bf16[128,1536]{1,0:T(8,128)(2,1)S(1)} %get-tuple-element.21), channel_id=1, source_target_pairs={{0,24},{8,16},{16,8},{24,0},{1,25},{9,17},{17,9},{25,1},{2,26},{10... | collective-permute-start | bytes 1179656 | tf_op jit(solution)/shard_map/ppermute | solution.py:83
  56.7 18.9 %collective-permute-start.29 = (bf16[128,1536]{1,0:T(8,128)(2,1)S(1)}, bf16[128,1536]{1,0:T(8,128)(2,1)S(1)}, u32[]{:S(2)}, u32[]{:S(2)}) collective-permute-start(bf16[128,1536]{1,0:T(8,128)(2,1)S(1)} %get-tuple-element.22), channel_id=1, source_target_pairs={{0,16},{8,24},{16,0},{24,8},{1,17},{9,25},{17,1},{25,9},{2,18},{10... | collective-permute-start | bytes 1179656 | tf_op jit(solution)/shard_map/ppermute | solution.py:83
  57.2 19.9 %collective-permute-start.28 = (bf16[128,1536]{1,0:T(8,128)(2,1)S(1)}, bf16[128,1536]{1,0:T(8,128)(2,1)S(1)}, u32[]{:S(2)}, u32[]{:S(2)}) collective-permute-start(bf16[128,1536]{1,0:T(8,128)(2,1)S(1)} %get-tuple-element.23), channel_id=1, source_target_pairs={{0,8},{8,0},{16,24},{24,16},{1,9},{9,1},{17,25},{25,17},{2,10},{10... | collective-permute-start | bytes 1179656 | tf_op jit(solution)/shard_map/ppermute | solution.py:83
  60.8 23.2 %collective-permute-start.14 = (bf16[128,1536]{1,0:T(8,128)(2,1)S(1)}, bf16[128,1536]{1,0:T(8,128)(2,1)S(1)}, u32[]{:S(2)}, u32[]{:S(2)}) collective-permute-start(bf16[128,1536]{1,0:T(8,128)(2,1)S(1)} %get-tuple-element.25), channel_id=1, source_target_pairs={{0,24},{8,16},{16,8},{24,0},{1,25},{9,17},{17,9},{25,1},{2,26},{10... | collective-permute-start | bytes 1179656 | tf_op jit(solution)/shard_map/ppermute | solution.py:83
  67.1 24.9 %collective-permute-start.13 = (bf16[128,1536]{1,0:T(8,128)(2,1)S(1)}, bf16[128,1536]{1,0:T(8,128)(2,1)S(1)}, u32[]{:S(2)}, u32[]{:S(2)}) collective-permute-start(bf16[128,1536]{1,0:T(8,128)(2,1)S(1)} %get-tuple-element.26), channel_id=1, source_target_pairs={{0,16},{8,24},{16,0},{24,8},{1,17},{9,25},{17,1},{25,9},{2,18},{10... | collective-permute-start | bytes 1179656 | tf_op jit(solution)/shard_map/ppermute | solution.py:83
  75.6 16.5 %collective-permute-start.12 = (bf16[128,1536]{1,0:T(8,128)(2,1)S(1)}, bf16[128,1536]{1,0:T(8,128)(2,1)S(1)}, u32[]{:S(2)}, u32[]{:S(2)}) collective-permute-start(bf16[128,1536]{1,0:T(8,128)(2,1)S(1)} %get-tuple-element.27), channel_id=1, source_target_pairs={{0,8},{8,0},{16,24},{24,16},{1,9},{9,1},{17,25},{25,17},{2,10},{10... | collective-permute-start | bytes 1179656 | tf_op jit(solution)/shard_map/ppermute | solution.py:83
  77.1 25.1 %collective-permute-start.7 = (bf16[128,6144]{1,0:T(8,128)(2,1)S(1)}, bf16[128,6144]{1,0:T(8,128)(2,1)S(1)}, u32[]{:S(2)}, u32[]{:S(2)}) collective-permute-start(bf16[128,6144]{1,0:T(8,128)(2,1)S(1)} %get-tuple-element.40), channel_id=1, source_target_pairs={{0,1},{1,0},{2,3},{3,2},{4,5},{5,4},{6,7},{7,6},{8,9},{9,8},{10,11... | collective-permute-start | bytes 4718600 | tf_op jit(solution)/shard_map/ppermute | solution.py:80
  84.0 59.2 %collective-permute-start.31 = (bf16[4,128,1536]{2,1,0:T(8,128)(2,1)}, bf16[4,128,1536]{2,1,0:T(8,128)(2,1)}, u32[]{:S(2)}, u32[]{:S(2)}) collective-permute-start(bf16[4,128,1536]{2,1,0:T(8,128)(2,1)} %pad_maximum_fusion.3), channel_id=1, source_target_pairs={{0,1},{1,0},{2,3},{3,2},{4,5},{5,4},{6,7},{7,6},{8,9},{9,8},{10,11... | collective-permute-start | bytes 4718600 | tf_op jit(solution)/shard_map/ppermute | solution.py:80
  93.5 52.0 %collective-permute-start.15 = (bf16[4,128,1536]{2,1,0:T(8,128)(2,1)}, bf16[4,128,1536]{2,1,0:T(8,128)(2,1)}, u32[]{:S(2)}, u32[]{:S(2)}) collective-permute-start(bf16[4,128,1536]{2,1,0:T(8,128)(2,1)} %pad_maximum_fusion.2), channel_id=1, source_target_pairs={{0,1},{1,0},{2,3},{3,2},{4,5},{5,4},{6,7},{7,6},{8,9},{9,8},{10,11... | collective-permute-start | bytes 4718600 | tf_op jit(solution)/shard_map/ppermute | solution.py:80
  102.2 6.8 %slice-start = ((s8[12582912]{0:T(1024)(128)(4,1)}), s8[4194304]{0:T(1024)(128)(4,1)S(1)}, s32[]{:S(2)}) async-start(s8[12582912]{0:T(1024)(128)(4,1)} %bitcast.47), calls=%async_computation | async-start | bytes 8388608
  102.3 7.0 %slice-start.1 = ((s8[12582912]{0:T(1024)(128)(4,1)}), s8[4194304]{0:T(1024)(128)(4,1)S(1)}, s32[]{:S(2)}) async-start(s8[12582912]{0:T(1024)(128)(4,1)} %bitcast.47), calls=%async_computation.1 | async-start | bytes 8388608
  102.3 8.1 %slice-start.2 = ((s8[12582912]{0:T(1024)(128)(4,1)}), s8[4194304]{0:T(1024)(128)(4,1)S(1)}, s32[]{:S(2)}) async-start(s8[12582912]{0:T(1024)(128)(4,1)} %bitcast.47), calls=%async_computation.2 | async-start | bytes 8388608
  115.7 36.0 %collective-permute-start.25 = (bf16[256,1024]{1,0:T(8,128)(2,1)}, bf16[256,1024]{1,0:T(8,128)(2,1)}, u32[]{:S(2)}, u32[]{:S(2)}) collective-permute-start(bf16[256,1024]{1,0:T(8,128)(2,1)} %get-tuple-element.11), channel_id=1, source_target_pairs={{0,16},{8,24},{16,0},{24,8},{1,17},{9,25},{17,1},{25,9},{2,18},{10... | collective-permute-start | bytes 1572872 | tf_op jit(solution)/shard_map/ppermute | solution.py:83
  117.1 31.8 %collective-permute-start.24 = (bf16[256,1024]{1,0:T(8,128)(2,1)}, bf16[256,1024]{1,0:T(8,128)(2,1)}, u32[]{:S(2)}, u32[]{:S(2)}) collective-permute-start(bf16[256,1024]{1,0:T(8,128)(2,1)} %get-tuple-element.11), channel_id=1, source_target_pairs={{0,8},{8,0},{16,24},{24,16},{1,9},{9,1},{17,25},{25,17},{2,10},{10... | collective-permute-start | bytes 1572872 | tf_op jit(solution)/shard_map/ppermute | solution.py:83
  117.9 36.0 %collective-permute-start.16 = (bf16[256,1024]{1,0:T(8,128)(2,1)}, bf16[256,1024]{1,0:T(8,128)(2,1)}, u32[]{:S(2)}, u32[]{:S(2)}) collective-permute-start(bf16[256,1024]{1,0:T(8,128)(2,1)} %get-tuple-element.17), channel_id=1, source_target_pairs={{0,8},{8,0},{16,24},{24,16},{1,9},{9,1},{17,25},{25,17},{2,10},{10... | collective-permute-start | bytes 1572872 | tf_op jit(solution)/shard_map/ppermute | solution.py:83
  143.2 2.3 copy-start.8
  143.2 15.1 %collective-permute-start.17 = (bf16[256,1024]{1,0:T(8,128)(2,1)}, bf16[256,1024]{1,0:T(8,128)(2,1)S(1)}, u32[]{:S(2)}, u32[]{:S(2)}) collective-permute-start(bf16[256,1024]{1,0:T(8,128)(2,1)} %get-tuple-element.17), channel_id=1, source_target_pairs={{0,16},{8,24},{16,0},{24,8},{1,17},{9,25},{17,1},{25,9},{2,18},{10... | collective-permute-start | bytes 1572872 | tf_op jit(solution)/shard_map/ppermute | solution.py:83
  145.4 4.3 %copy-start.7 = (bf16[1024,1024]{1,0:T(8,128)(2,1)S(1)}, bf16[1024,1024]{1,0:T(8,128)(2,1)}, u32[]{:S(2)}) copy-start(bf16[1024,1024]{1,0:T(8,128)(2,1)} %get-tuple-element.10) | copy-start | bytes 6291460
  145.5 14.9 %collective-permute-start.20 = (bf16[256,1024]{1,0:T(8,128)(2,1)S(1)}, bf16[256,1024]{1,0:T(8,128)(2,1)S(1)}, u32[]{:S(2)}, u32[]{:S(2)}) collective-permute-start(bf16[256,1024]{1,0:T(8,128)(2,1)S(1)} %copy-done.8), channel_id=1, source_target_pairs={{0,8},{8,0},{16,24},{24,16},{1,9},{9,1},{17,25},{25,17},{2,10},{10... | collective-permute-start | bytes 1572872 | tf_op jit(solution)/shard_map/ppermute | solution.py:83
  147.0 8.2 %copy-start.6 = (bf16[1024,1024]{1,0:T(8,128)(2,1)S(1)}, bf16[1024,1024]{1,0:T(8,128)(2,1)}, u32[]{:S(2)}) copy-start(bf16[1024,1024]{1,0:T(8,128)(2,1)} %get-tuple-element.16) | copy-start | bytes 6291460
  148.9 12.9 %copy-start.5 = (bf16[1024,1024]{1,0:T(8,128)(2,1)S(1)}, bf16[1024,1024]{1,0:T(8,128)(2,1)}, u32[]{:S(2)}) copy-start(bf16[1024,1024]{1,0:T(8,128)(2,1)} %get-tuple-element.18) | copy-start | bytes 6291460
  149.0 20.6 %collective-permute-start.21 = (bf16[256,1024]{1,0:T(8,128)(2,1)S(1)}, bf16[256,1024]{1,0:T(8,128)(2,1)S(1)}, u32[]{:S(2)}, u32[]{:S(2)}) collective-permute-start(bf16[256,1024]{1,0:T(8,128)(2,1)S(1)} %copy-done.8), channel_id=1, source_target_pairs={{0,16},{8,24},{16,0},{24,8},{1,17},{9,25},{17,1},{25,9},{2,18},{10... | collective-permute-start | bytes 1572872 | tf_op jit(solution)/shard_map/ppermute | solution.py:83
  151.8 43.1 %collective-permute-start.8 = (bf16[128,6144]{1,0:T(8,128)(2,1)S(1)}, bf16[128,6144]{1,0:T(8,128)(2,1)S(1)}, u32[]{:S(2)}, u32[]{:S(2)}) collective-permute-start(bf16[128,6144]{1,0:T(8,128)(2,1)S(1)} %slice.49), channel_id=1, source_target_pairs={{0,1},{1,0},{2,3},{3,2},{4,5},{5,4},{6,7},{7,6},{8,9},{9,8},{10,11... | collective-permute-start | bytes 4718600 | tf_op jit(solution)/shard_map/ppermute | solution.py:80
  153.9 21.9 %collective-permute-start.27 = (bf16[128,1024]{1,0:T(8,128)(2,1)S(1)}, bf16[128,1024]{1,0:T(8,128)(2,1)S(1)}, u32[]{:S(2)}, u32[]{:S(2)}) collective-permute-start(bf16[128,1024]{1,0:T(8,128)(2,1)S(1)} %slice.59), channel_id=1, source_target_pairs={{0,8},{8,0},{16,24},{24,16},{1,9},{9,1},{17,25},{25,17},{2,10},{10... | collective-permute-start | bytes 786440 | tf_op jit(solution)/shard_map/ppermute | solution.py:83
  158.3 16.9 %collective-permute-start.26 = (bf16[128,1024]{1,0:T(8,128)(2,1)S(1)}, bf16[128,1024]{1,0:T(8,128)(2,1)S(1)}, u32[]{:S(2)}, u32[]{:S(2)}) collective-permute-start(bf16[128,1024]{1,0:T(8,128)(2,1)S(1)} %slice.58), channel_id=1, source_target_pairs={{0,16},{8,24},{16,0},{24,8},{1,17},{9,25},{17,1},{25,9},{2,18},{10... | collective-permute-start | bytes 786440 | tf_op jit(solution)/shard_map/ppermute | solution.py:83
  160.4 20.4 %collective-permute-start.18 = (bf16[128,1024]{1,0:T(8,128)(2,1)S(1)}, bf16[128,1024]{1,0:T(8,128)(2,1)S(1)}, u32[]{:S(2)}, u32[]{:S(2)}) collective-permute-start(bf16[128,1024]{1,0:T(8,128)(2,1)S(1)} %slice.54), channel_id=1, source_target_pairs={{0,16},{8,24},{16,0},{24,8},{1,17},{9,25},{17,1},{25,9},{2,18},{10... | collective-permute-start | bytes 786440 | tf_op jit(solution)/shard_map/ppermute | solution.py:83
  169.6 11.3 %collective-permute-start.19 = (bf16[128,1024]{1,0:T(8,128)(2,1)S(1)}, bf16[128,1024]{1,0:T(8,128)(2,1)S(1)}, u32[]{:S(2)}, u32[]{:S(2)}) collective-permute-start(bf16[128,1024]{1,0:T(8,128)(2,1)S(1)} %slice.55), channel_id=1, source_target_pairs={{0,8},{8,0},{16,24},{24,16},{1,9},{9,1},{17,25},{25,17},{2,10},{10... | collective-permute-start | bytes 786440 | tf_op jit(solution)/shard_map/ppermute | solution.py:83
  175.2 9.9 %collective-permute-start.22 = (bf16[128,1024]{1,0:T(8,128)(2,1)S(1)}, bf16[128,1024]{1,0:T(8,128)(2,1)S(1)}, u32[]{:S(2)}, u32[]{:S(2)}) collective-permute-start(bf16[128,1024]{1,0:T(8,128)(2,1)S(1)} %slice.56), channel_id=1, source_target_pairs={{0,16},{8,24},{16,0},{24,8},{1,17},{9,25},{17,1},{25,9},{2,18},{10... | collective-permute-start | bytes 786440 | tf_op jit(solution)/shard_map/ppermute | solution.py:83
  175.8 9.2 %collective-permute-start.23 = (bf16[128,1024]{1,0:T(8,128)(2,1)S(1)}, bf16[128,1024]{1,0:T(8,128)(2,1)S(1)}, u32[]{:S(2)}, u32[]{:S(2)}) collective-permute-start(bf16[128,1024]{1,0:T(8,128)(2,1)S(1)} %slice.57), channel_id=1, source_target_pairs={{0,8},{8,0},{16,24},{24,16},{1,9},{9,1},{17,25},{25,17},{2,10},{10... | collective-permute-start | bytes 786440 | tf_op jit(solution)/shard_map/ppermute | solution.py:83
  190.0 4.9 %copy-start.4 = (bf16[256,6144]{1,0:T(8,128)(2,1)S(1)}, bf16[256,6144]{1,0:T(8,128)(2,1)}, u32[]{:S(2)}) copy-start(bf16[256,6144]{1,0:T(8,128)(2,1)} %fusion) | copy-start | bytes 9437188
  195.4 18.8 %collective-permute-start.11 = (bf16[32,6144]{1,0:T(8,128)(2,1)S(1)}, bf16[32,6144]{1,0:T(8,128)(2,1)S(1)}, u32[]{:S(2)}, u32[]{:S(2)}) collective-permute-start(bf16[32,6144]{1,0:T(8,128)(2,1)S(1)} %get-tuple-element.28), channel_id=1, source_target_pairs={{0,4},{1,5},{2,6},{3,7},{4,0},{5,1},{6,2},{7,3},{8,12},{9,13},{10,... | collective-permute-start | bytes 1179656 | tf_op jit(solution)/shard_map/ppermute | solution.py:77
  196.4 32.5 %collective-permute-start.10 = (bf16[32,6144]{1,0:T(8,128)(2,1)S(1)}, bf16[32,6144]{1,0:T(8,128)(2,1)S(1)}, u32[]{:S(2)}, u32[]{:S(2)}) collective-permute-start(bf16[32,6144]{1,0:T(8,128)(2,1)S(1)} %get-tuple-element.29), channel_id=1, source_target_pairs={{0,2},{1,3},{2,4},{3,5},{4,6},{5,7},{6,0},{7,1},{8,10},{9,11},{10,... | collective-permute-start | bytes 1179656 | tf_op jit(solution)/shard_map/ppermute | solution.py:77
  197.3 33.0 %collective-permute-start.9 = (bf16[32,6144]{1,0:T(8,128)(2,1)S(1)}, bf16[32,6144]{1,0:T(8,128)(2,1)S(1)}, u32[]{:S(2)}, u32[]{:S(2)}) collective-permute-start(bf16[32,6144]{1,0:T(8,128)(2,1)S(1)} %get-tuple-element.30), channel_id=1, source_target_pairs={{0,6},{1,7},{2,0},{3,1},{4,2},{5,3},{6,4},{7,5},{8,14},{9,15},{10,... | collective-permute-start | bytes 1179656 | tf_op jit(solution)/shard_map/ppermute | solution.py:77

commit v2 on v1

v2 whole, which is shorter than its diff:
```python
import functools

import jax
import jax.numpy as jnp
from jax import lax
from jax.experimental import pallas as pl
from jax.experimental.pallas import tpu as pltpu
from jax.sharding import PartitionSpec as P

CAP = 32
F32, BF16 = jnp.float32, jnp.bfloat16
ROWS = (((0,), (0,)), ((), ()))
LAST = (((1,), (1,)), ((), ()))
VMEM = pl.BlockSpec(memory_space=pltpu.VMEM)
SMEM = pl.BlockSpec(memory_space=pltpu.SMEM)
ANY = pl.BlockSpec(memory_space=pl.ANY)
LIMIT = 40 << 20


def mm(a, b, dims=(((1,), (0,)), ((), ()))):
    return lax.dot_general(a, b, dims, preferred_element_type=F32)


def shape(dims, kind=BF16):
    return jax.ShapeDtypeStruct(tuple(dims), kind)


def params(limit=LIMIT):
    return pltpu.CompilerParams(vmem_limit_bytes=limit)


def cost(flops, nbytes, weigh=64):
    return pl.CostEstimate(flops=int(flops) // weigh, bytes_accessed=int(nbytes) // weigh, transcendentals=0)


def fetch(source, held, sem, parts):
    width = source.shape[1] // parts
    copies = []
    for i in range(parts):
        cols = pl.ds(i * width, width)
        copies.append(pltpu.make_async_copy(source.at[:, cols], held.at[:, cols], sem.at[i]))
        copies[-1].start()
    return copies


def pick_kernel(me, routes, probs, tokens, out_grad, sel_out, both, held, sem):
    _, n_dp, _, width = both.shape
    copies = fetch(tokens, held.at[0], sem.at[0], n_dp) + fetch(out_grad, held.at[1], sem.at[1], n_dp)
    n = tokens.shape[0]
    hits = routes[...] == 0
    coef = jnp.sum(jnp.where(hits, probs[...], 0.0), axis=0, keepdims=True)
    routed = jnp.sum(jnp.where(hits, 1.0, 0.0), axis=0, keepdims=True) > 0.5
    flags = jnp.broadcast_to(jnp.where(routed, 1.0, 0.0), (8, n))
    before = lax.broadcasted_iota(jnp.int32, (n, n), 0) <= lax.broadcasted_iota(jnp.int32, (n, n), 1)
    upto = mm(flags.astype(BF16), jnp.where(before, 1.0, 0.0).astype(BF16))[:1]
    count = jnp.sum(flags[:1], axis=1, keepdims=True)
    lane = lax.broadcasted_iota(jnp.int32, (1, n), 1).astype(F32)
    rank = jnp.where(routed, upto - 1.0, count + lane - upto)
    sel = rank == lax.broadcasted_iota(jnp.int32, (CAP, n), 0).astype(F32)
    scale = jnp.sum(jnp.where(sel, coef, 0.0), axis=1, keepdims=True)
    sel = jnp.where(sel, 1.0, 0.0).astype(BF16)
    sel_out[...] = sel
    for copy in copies:
        copy.wait()
    for k in range(n_dp):
        cols = pl.ds(pl.multiple_of((me[0] ^ k) * width, 128), width)
        both[0, k] = mm(sel, held[0, :, cols]).astype(BF16)
        both[1, k] = (scale * mm(sel, held[1, :, cols])).astype(BF16)


def pick(me, tokens, routes, probs, out_grad, n_dp):
    n, d = tokens.shape
    return pl.pallas_call(
        pick_kernel,
        out_shape=(shape((CAP, n)), shape((2, n_dp, CAP, d // n_dp))),
        in_specs=[SMEM, VMEM, VMEM, ANY, ANY],
        out_specs=(VMEM,) * 2,
        scratch_shapes=[pltpu.VMEM((2, n, d), BF16), pltpu.SemaphoreType.DMA((2, n_dp))],
        compiler_params=params(60 << 20),
        cost_estimate=cost(4 * CAP * n * d, 5 * n * d),
    )(me, routes.T, probs.T, tokens, out_grad)


def after(x, *deps):
    def kernel(*refs):
        del refs

    return pl.pallas_call(
        kernel,
        out_shape=shape(x.shape, x.dtype),
        in_specs=[ANY] * (1 + len(deps)),
        out_specs=ANY,
        input_output_aliases={0: 0},
        compiler_params=params(1 << 20),
        cost_estimate=cost(0, 0),
    )(x, *deps)


def lay_kernel(count, deps, whole, *refs):
    blocks, rest, sem = refs[:count], list(refs[count + deps : -1]), refs[-1]
    copies = []
    at = 0
    for b in blocks:
        rows = pl.ds(at, b.shape[2])
        at += b.shape[2]
        if whole:
            copies.append((b, rest[0].at[:, :, rows]))
        for k, out in enumerate(rest[whole:], 1):
            copies.append((b.at[:, k], out.at[:, rows]))
    copies = [pltpu.make_async_copy(a, b, sem.at[i]) for i, (a, b) in enumerate(copies)]
    for copy in copies:
        copy.start()
    for copy in copies:
        copy.wait()


def lay(blocks, whole, deps=()):
    arrays, slices, _, width = blocks[0].shape
    rows = sum(b.shape[2] for b in blocks)
    outs = [shape((arrays, slices, rows, width))] * whole + [shape((arrays, rows, width))] * (slices - 1)
    return pl.pallas_call(
        functools.partial(lay_kernel, len(blocks), len(deps), whole),
        out_shape=outs,
        in_specs=[ANY] * (len(blocks) + len(deps)),
        out_specs=[ANY] * len(outs),
        scratch_shapes=[pltpu.SemaphoreType.DMA((len(blocks) * (whole + slices - 1),))],
        compiler_params=params(1 << 20),
        cost_estimate=cost(0, 4 * arrays * slices * rows * width),
    )(*blocks, *deps)


def pile_kernel(count, *refs):
    blocks, out, sem = refs[:count], refs[-2], refs[-1]
    copies = [pltpu.make_async_copy(b, out.at[i], sem.at[i]) for i, b in enumerate(blocks)]
    for copy in copies:
        copy.start()
    for copy in copies:
        copy.wait()


def pile(blocks, *deps):
    return pl.pallas_call(
        functools.partial(pile_kernel, len(blocks)),
        out_shape=shape((len(blocks),) + blocks[0].shape),
        in_specs=[ANY] * (len(blocks) + len(deps)),
        out_specs=ANY,
        scratch_shapes=[pltpu.SemaphoreType.DMA((len(blocks),))],
        compiler_params=params(1 << 20),
        cost_estimate=cost(0, 4 * len(blocks) * blocks[0].size),
    )(*blocks, *deps)


def gather_rows(me, i, parts, rows):
    at = 0
    for part in parts:
        _, n_dp, count, width = part.shape
        for k in range(n_dp):
            cols = pl.ds(pl.multiple_of((me[0] ^ k) * width, 128), width)
            rows[at : at + count, cols] = part[i, k]
        at += count


class Stream:
    def __init__(self, copies):
        self.copies = copies
        self.started = 0

    def start(self, upto):
        while self.started < min(upto, len(self.copies)):
            for copy in self.copies[self.started]:
                copy.start()
            self.started += 1

    def take(self, i):
        for copy in self.copies[i]:
            copy.wait()


def slab_kernel(count, me, *refs):
    parts, (gw, uw, dw, out, rows, gate, up, wide, tall, wide_sem, tall_sem) = refs[:count], refs[count:]
    ff, piece = gw.shape[1], tall.shape[1]
    _, n_dp, _, width = parts[0].shape
    sub = wide.shape[2]
    forth = []
    for k in range(n_dp):
        for s in range(width // sub):
            source = pl.ds(pl.multiple_of((me[0] ^ k) * width + s * sub, 128), sub)
            slot = len(forth) % 3
            forth.append([
                pltpu.make_async_copy(w.at[source], wide.at[slot, j], wide_sem.at[slot, j])
                for j, w in enumerate((gw, uw))
            ])
    back = Stream([
        [pltpu.make_async_copy(dw.at[pl.ds(i * piece, piece)], tall.at[i % 3], tall_sem.at[i % 3])]
        for i in range(ff // piece)
    ])
    forth = Stream(forth)
    forth.start(2)
    total = len(forth.copies)
    for i in range(total):
        k, s = i // (width // sub), i % (width // sub)
        forth.take(i)
        forth.start(i + 3)
        if i >= total - 2:
            back.start(i + 3 - total)
        some = jnp.concatenate([p[0, k, :, s * sub : (s + 1) * sub] for p in parts])
        for acc, j in ((gate, 0), (up, 1)):
            more = mm(some, wide[i % 3, j])
            acc[...] = more if i == 0 else acc[...] + more
    gather_rows(me, 1, parts, rows)
    g, u = gate[...], up[...]
    sig = jax.nn.sigmoid(g)
    act = g * sig
    gate[...] = act
    out[:, :ff] = (act * u).astype(BF16)
    up[...] = u * sig * (1.0 + g * (1.0 - sig))
    for i in range(ff // piece):
        at = i * piece
        cols = slice(at, at + piece)
        back.take(i)
        back.start(i + 3)
        grad = mm(rows[...], tall[i % 3], LAST)
        out[:, ff + at : ff + at + piece] = (grad * up[:, cols]).astype(BF16)
        out[:, 2 * ff + at : 2 * ff + at + piece] = (grad * gate[:, cols]).astype(BF16)


def slab(me, parts, gw, uw, dw):
    rows, (d, ff) = sum(p.shape[2] for p in parts), gw.shape
    width = parts[0].shape[3]
    sub = 768 if width % 768 == 0 else width
    return pl.pallas_call(
        functools.partial(slab_kernel, len(parts)),
        out_shape=shape((rows, 3 * ff)),
        in_specs=[SMEM] + [VMEM] * len(parts) + [ANY] * 3,
        out_specs=VMEM,
        scratch_shapes=[
            pltpu.VMEM((rows, d), BF16),
            pltpu.VMEM((rows, ff), F32),
            pltpu.VMEM((rows, ff), F32),
            pltpu.VMEM((3, 2, sub, ff), BF16),
            pltpu.VMEM((3, 256, d), BF16),
            pltpu.SemaphoreType.DMA((3, 2)),
            pltpu.SemaphoreType.DMA((3,)),
        ],
        compiler_params=params(50 << 20),
        cost_estimate=cost(6 * rows * gw.size, 6 * gw.size, 1),
    )(me, *parts, gw, uw, dw)


def term_kernel(grads, gw, uw, *refs):
    mine, left, right, held, sem = refs[-5:]
    ff, half, width = gw.shape[1], mine.shape[0], mine.shape[1]
    tile = held.shape[2]
    copies = []
    for i in range(width // tile):
        rows, slot = pl.ds(i * tile, tile), i % 4
        copies.append([
            pltpu.make_async_copy(w.at[rows], held.at[slot, j], sem.at[slot, j]) for j, w in enumerate((gw, uw))
        ])
    stream = Stream(copies)
    stream.start(3)
    for i in range(width // tile):
        cols = slice(i * tile, (i + 1) * tile)
        stream.take(i)
        stream.start(i + 4)
        held_gate, held_up = held[i % 4, 0], held[i % 4, 1]
        term = mm(grads[:, ff : 2 * ff], held_gate, LAST) + mm(grads[:, 2 * ff :], held_up, LAST)
        mine[:, cols] = term[:half].astype(BF16)
        theirs = left if i * tile < width // 2 else right
        theirs[:, i * tile % (width // 2) : i * tile % (width // 2) + tile] = term[half:].astype(BF16)


def term(grads, gw, uw, deps):
    rows, (d, ff) = grads.shape[0], gw.shape
    return pl.pallas_call(
        term_kernel,
        out_shape=(shape((rows // 2, d)), shape((rows // 2, d // 2)), shape((rows // 2, d // 2))),
        in_specs=[VMEM, ANY, ANY] + [ANY] * len(deps),
        out_specs=(VMEM,) * 3,
        scratch_shapes=[pltpu.VMEM((4, 2, 512, ff), BF16), pltpu.SemaphoreType.DMA((4, 2))],
        compiler_params=params(50 << 20),
        cost_estimate=cost(4 * rows * gw.size, 4 * gw.size),
    )(grads, gw, uw, *deps)


def fold_kernel(mine, left, right, *outs):
    half = left.shape[1]
    for i, out in enumerate(outs):
        rows = slice(i * CAP, (i + 1) * CAP)
        for cols, theirs in ((slice(0, half), left), (slice(half, 2 * half), right)):
            out[:, cols] = (mine[rows, cols].astype(F32) + theirs[rows].astype(F32)).astype(BF16)


def fold(mine, left, right):
    rows, d = mine.shape
    return pl.pallas_call(
        fold_kernel,
        out_shape=[shape((CAP, d))] * (rows // CAP),
        in_specs=[VMEM] * 3,
        out_specs=[VMEM] * (rows // CAP),
        compiler_params=params(16 << 20),
        cost_estimate=cost(0, 6 * rows * d),
    )(mine, left, right)


def put_kernel(groups, sel, *refs):
    *parts, out = refs
    each = len(parts) // groups
    for g in range(groups):
        total = parts[g * each][...].astype(F32)
        for part in parts[g * each + 1 : (g + 1) * each]:
            total = total + part[...].astype(F32)
        width = total.shape[1]
        out[:, g * width : (g + 1) * width] = mm(sel[...], total.astype(BF16), ROWS).astype(BF16)


def put(sel, groups):
    parts = [p for group in groups for p in group]
    d = sum(group[0].shape[1] for group in groups)
    return pl.pallas_call(
        functools.partial(put_kernel, len(groups)),
        out_shape=shape((sel.shape[1], d)),
        in_specs=[VMEM] * (1 + len(parts)),
        out_specs=VMEM,
        compiler_params=params(32 << 20),
        cost_estimate=cost(2 * sel.size * d, 4 * sel.size * d),
    )(sel, *parts)


def contract_kernel(n_slices, n_grads, n_totals, *refs):
    slices, refs = refs[:n_slices], refs[n_slices:]
    grads, refs = refs[:n_grads], refs[n_grads:]
    totals, refs = refs[:n_totals], refs[n_totals:]
    outs, (picked, scaled, rows) = refs[:3], refs[3:]

    @pl.when(pl.program_id(0) == 0)
    def _():
        at = 0
        for block in slices:
            size = block.shape[-2]
            whole = len(block.shape) == 4
            picked[at : at + size] = block[0, 0] if whole else block[0]
            scaled[at : at + size] = block[1, 0] if whole else block[1]
            at += size
        at = 0
        for block in grads:
            size = block.shape[0]
            rows[at : at + size] = block[...]
            at += size

    ff, tile = rows.shape[1] // 3, outs[0].shape[0]
    cols = pl.ds(pl.multiple_of(pl.program_id(0) * tile, tile), tile)

    def put_tile(n, value):
        if n_totals:
            value = value + totals[n][...].astype(F32)
        outs[n][...] = value.astype(outs[n].dtype)

    put_tile(0, mm(picked[:, cols], rows[:, ff : 2 * ff], ROWS))
    put_tile(1, mm(picked[:, cols], rows[:, 2 * ff :], ROWS))
    put_tile(2, mm(rows[:, :ff], scaled[:, cols], ROWS))


def contract(slices, grads, totals, tile=256):
    rows = sum(b.shape[0] for b in grads)
    width, ff = slices[0].shape[-1], grads[0].shape[1] // 3
    tall = pl.BlockSpec((tile, ff), lambda i: (i, 0))
    wide = pl.BlockSpec((ff, tile), lambda i: (0, i))
    return pl.pallas_call(
        functools.partial(contract_kernel, len(slices), len(grads), len(totals)),
        out_shape=(shape((width, ff)), shape((width, ff)), shape((ff, width))),
        grid=(width // tile,),
        in_specs=[VMEM] * (len(slices) + len(grads)) + [tall, tall, wide][: len(totals)],
        out_specs=(tall, tall, wide),
        scratch_shapes=[pltpu.VMEM((rows, width), BF16)] * 2 + [pltpu.VMEM((rows, 3 * ff), BF16)],
        compiler_params=params(56 << 20),
        cost_estimate=cost(6 * rows * width * ff, 2 * rows * (2 * width + 3 * ff) + 12 * width * ff, 1),
    )(*slices, *grads, *totals)


def on_device(tokens, routes, route_probs, gate_weight, up_weight, down_weight, out_grad):
    n_dp, n_fetch = lax.axis_size("dp"), lax.axis_size("fetch")
    chips = n_fetch // 2
    me = lax.axis_index("dp").astype(jnp.int32).reshape(1)

    def move(x, hop):
        pairs = [(2 * z + c, 2 * ((z + hop) % chips) + c) for z in range(chips) for c in range(2)]
        return lax.ppermute(x, "fetch", pairs)

    def swap(x):
        return lax.ppermute(x, "fetch", [(k, k ^ 1) for k in range(n_fetch)])

    def across(x, bits):
        return lax.ppermute(x, "dp", [(k, k ^ bits) for k in range(n_dp)])

    offsets = [0]
    for s in range(1, chips // 2 + 1):
        offsets += [-s] if 2 * s == chips else [-s, s]

    sel, both = pick(me, tokens, routes, route_probs, out_grad, n_dp)
    blocks = {0: both, -1: move(both, 1)}
    blocks[0] = own = after(both, blocks[-1])
    for s in range(2, chips // 2 + 1):
        blocks[-s] = move(blocks[1 - s], 1)
    for s in range(1, chips // 2):
        blocks[s] = move(blocks[s - 1], -1)
    here, beside = [own, blocks[-1]], [blocks[o] for o in offsets[2:]]
    here_theirs = [swap(own), swap(blocks[-1])]
    near_cuts = lay(here, False, here_theirs[:1])
    near_got = [across(cut, k) for k, cut in enumerate(near_cuts, 1)]
    far, *far_cuts = lay(beside, True, near_got + here_theirs[1:])
    far_theirs = swap(far)
    far_got = [across(cut, k) for k, cut in enumerate(far_cuts, 1)]

    parts = here + [far] + here_theirs + [far_theirs]
    rows = slab(me, parts, gate_weight, up_weight, down_weight)
    mine, left, right = term(rows, gate_weight, up_weight, far_got)
    near_theirs = swap(pile(near_got, mine))
    far_got_theirs = swap(pile(far_got, mine))
    summed, *others = fold(mine, swap(left), swap(right))
    slices = [parts]
    for k in range(n_dp - 1):
        slices.append([near_got[k], far_got[k], near_theirs[k], far_got_theirs[k]])
    if n_dp == 4:
        half = rows.shape[0] // 2
        by_x, by_y = after(across(rows, 1), summed), after(across(rows, 2), summed)
        first = [rows, by_x, by_y]
        last = [across(by_x[:half], 2), across(by_y[half:], 1)]
    else:
        got = [across(rows, k) for k in range(1, n_dp)]
        first, last = [rows] + got[:-1], got[-1:]
    totals = contract(sum(slices[:-1], []), first, [])
    gate_grad, up_grad, down_grad = contract(slices[-1], last, totals)
    token_grad = put(sel, [[summed] + [move(x, o) for x, o in zip(others, offsets[1:])]])
    return token_grad, gate_grad, up_grad, down_grad


def solution(mesh):
    return jax.shard_map(
        on_device,
        mesh=mesh,
        in_specs=(
            P(("dp", "fetch"), None),
            P(("dp", "fetch"), None),
            P(("dp", "fetch"), None),
            P(None, "fetch"),
            P(None, "fetch"),
            P("fetch", None),
            P(("dp", "fetch"), None),
        ),
        out_specs=(P(("dp", "fetch"), None), P("dp", "fetch"), P("dp", "fetch"), P("fetch", "dp")),
        check_vma=False,
    )
```

time: 233 us -> 197 us (0.85)
  the two profiles are of different devices: /device:TPU:8 before, /device:TPU:0 now
where the time goes in v2:
time: 197 us; the launch traced here: 196 us
  waiting for transfers between devices  90.6 us (46%)
  Pallas kernels  69.8 us (35%)
  starting transfers between devices  25.3 us (13%)
  local copies, waits for them, and re-layouts  9.42 us (5%)
    ppermute x6, waiting for transfers between devices, move(): return lax.ppermute(x, 'fetch', pairs)  61.3 us
    ppermute x10, waiting for transfers between devices, across(): return lax.ppermute(x, 'dp', [(k, k ^ bits) for k in range(n_dp)])  28 us
    pallas_call x2, Pallas kernels, contract(): pl.pallas_call(functools.partial(contract_kernel, len(slices), len(grads)...  26.4 us
    pallas_call x1, Pallas kernels, slab(): pl.pallas_call(functools.partial(slab_kernel, len(parts)), out_shape=shap...  20.7 us
    ppermute x10, starting transfers between devices, across(): return lax.ppermute(x, 'dp', [(k, k ^ bits) for k in range(n_dp)])  15.2 us
    pallas_call x1, Pallas kernels, term(): pl.pallas_call(term_kernel, out_shape=(shape((rows // 2, d)), shape((rows...  13.6 us
    ppermute x6, starting transfers between devices, move(): return lax.ppermute(x, 'fetch', pairs)  8.55 us
    unnamed x46, local copies, waits for them, and re-layouts  7.2 us
  transfers between devices with their start and end apart: 23, of which 7 were waited for; matrix products, arithmetic and copies ran while one was open for 1% of the time, Pallas kernels for 21%

profile of v2, /device:TPU:0, one launch (start us, length us, event | category | flops | bytes accessed | tf_op | source)
XLA Modules:
  0.0 196.1 jit_solution(9412531919793189772)
XLA Ops:
  0.6 4.0 %shard_map.102 = (bf16[32,128]{1,0:T(8,128)(2,1)}, bf16[2,4,32,1536]{3,2,1,0:T(8,128)(2,1)}) custom-call(s32[1]{0:T(128)} %bitcast.me, s32[2,128]{1,0:T(2,128)} %bitcast.15, f32[2,128]{1,0:T(2,128)} %bitcast.16, bf16[128,6144]{1,0:T(8,128)(2,1)} %tokens.1, bf16[128,6144]{1,0:T(8,128)(2,1)} %out_grad.1), custom_call_target="tpu_custom_call" | custom-call | flops 1572864 | bytes 61440 | tf_op jit(solution)/shard_map/pallas_call | solution.py:73
  4.7 3.1 %collective-permute-start = (bf16[2,4,32,1536]{3,2,1,0:T(8,128)(2,1)}, bf16[2,4,32,1536]{3,2,1,0:T(8,128)(2,1)S(1)}, u32[]{:S(2)}, u32[]{:S(2)}) collective-permute-start(bf16[2,4,32,1536]{3,2,1,0:T(8,128)(2,1)} %get-tuple-element.27.refs_0_), channel_id=1, source_target_pairs={{0,2},{1,3},{2,4},{3,5},{4,6},{5,7},{6,0},{7,1},{8,10},{9,11},{10,... | collective-permute-start | bytes 2359304 | tf_op jit(solution)/shard_map/ppermute | solution.py:388
  7.8 19.8 %collective-permute-done.refs_1_ = bf16[2,4,32,1536]{3,2,1,0:T(8,128)(2,1)S(1)} collective-permute-done((bf16[2,4,32,1536]{3,2,1,0:T(8,128)(2,1)}, bf16[2,4,32,1536]{3,2,1,0:T(8,128)(2,1)S(1)}, u32[]{:S(2)}, u32[]{:S(2)}) %collective-permute-start) | collective-permute-done | bytes 786464 | tf_op jit(solution)/shard_map/ppermute | solution.py:388
  27.5 1.1 copy-done.3
  28.7 0.9 copy-done.4
  29.6 1.7 collective-permute-start.1
  31.3 0.2 collective-permute-start.7
  31.6 0.3 collective-permute-start.2
  31.8 0.2 collective-permute-done.3.refs_2_.refs_3_
  32.1 1.1 copy-done.5
  33.2 0.8 shard_map.104
  34.0 1.6 collective-permute-start.4
  35.6 1.5 collective-permute-start.5
  37.1 12.9 %collective-permute-done.1.refs_0_ = bf16[2,4,32,1536]{3,2,1,0:T(8,128)(2,1)S(1)} collective-permute-done((bf16[2,4,32,1536]{3,2,1,0:T(8,128)(2,1)}, bf16[2,4,32,1536]{3,2,1,0:T(8,128)(2,1)S(1)}, u32[]{:S(2)}, u32[]{:S(2)}) %collective-permute-start.1) | collective-permute-done | bytes 786464 | tf_op jit(solution)/shard_map/ppermute | solution.py:388
  50.0 2.4 %collective-permute-start.6 = (bf16[2,64,1536]{2,1,0:T(8,128)(2,1)S(1)}, bf16[2,64,1536]{2,1,0:T(8,128)(2,1)S(1)}, u32[]{:S(2)}, u32[]{:S(2)}) collective-permute-start(bf16[2,64,1536]{2,1,0:T(8,128)(2,1)S(1)} %get-tuple-element.30), channel_id=1, source_target_pairs={{0,24},{8,16},{16,8},{24,0},{1,25},{9,17},{17,9},{25,1},{2,26},{10... | collective-permute-start | bytes 1179656 | tf_op jit(solution)/shard_map/ppermute | solution.py:394
  52.4 14.3 %collective-permute-done.2.refs_1_ = bf16[2,4,32,1536]{3,2,1,0:T(8,128)(2,1)S(1)} collective-permute-done((bf16[2,4,32,1536]{3,2,1,0:T(8,128)(2,1)S(1)}, bf16[2,4,32,1536]{3,2,1,0:T(8,128)(2,1)S(1)}, u32[]{:S(2)}, u32[]{:S(2)}) %collective-permute-start.2) | collective-permute-done | bytes 786464 | tf_op jit(solution)/shard_map/ppermute | solution.py:388
  66.8 1.0 shard_map.105
  67.8 0.1 collective-permute-start.8
  67.9 1.6 collective-permute-start.10
  69.4 1.4 collective-permute-start.11
  70.9 0.5 collective-permute-start.9
  71.5 1.1 copy-done.20
  72.6 20.7 %shard_map.106.grads.refs_14_ = bf16[256,3072]{1,0:T(8,128)(2,1)} custom-call(s32[1]{0:T(128)} %bitcast.me, bf16[2,4,32,1536]{3,2,1,0:T(8,128)(2,1)S(1)} %copy-done.6, bf16[2,4,32,1536]{3,2,1,0:T(8,128)(2,1)S(1)} %collective-permute-done.refs_1_, bf16[2,4,64,1536]{3,2,1,0:T(8,128)(2,1)} %copy-done.13, ...), custom_call_target="tpu_custom_call" | custom-call | flops 9663676416 | bytes 37748736 | tf_op jit(solution)/shard_map/pallas_call | solution.py:231
  93.3 13.6 %shard_map.107 = (bf16[128,6144]{1,0:T(8,128)(2,1)}, bf16[128,3072]{1,0:T(8,128)(2,1)S(1)}, bf16[128,3072]{1,0:T(8,128)(2,1)S(1)}) custom-call(bf16[256,3072]{1,0:T(8,128)(2,1)} %shard_map.106.grads.refs_14_, bf16[6144,1024]{1,0:T(8,128)(2,1)} %gw.1, bf16[6144,1024]{1,0:T(8,128)(2,1)} %uw.1, bf16[2,64,1536]{2,1,0:T(8,128)(2,1)S(1)} %collective-permute-done.9.refs_0_.refs_7_, ...), custom_call_target="tpu_custom_call" | custom-call | flops 100663296 | bytes 393216 | tf_op jit(solution)/shard_map/pallas_call | solution.py:275
  107.1 1.4 copy-done
  108.5 0.6 shard_map.111
  109.1 0.5 collective-permute-start.18
  109.6 0.3 copy-done.19
  109.9 1.5 collective-permute-start.21
  111.4 1.5 collective-permute-start.19
  112.9 0.6 shard_map.110
  113.5 0.6 collective-permute-start.17
  114.1 1.1 collective-permute-done.13.right
  115.2 0.4 shard_map.108
  115.6 1.9 collective-permute-start.14
  117.4 0.2 collective-permute-start.15
  117.6 1.1 slice_bitcast_fusion
  118.7 27.9 %collective-permute-done.21.refs_0_ = bf16[256,3072]{1,0:T(8,128)(2,1)S(1)} collective-permute-done((bf16[256,3072]{1,0:T(8,128)(2,1)S(1)}, bf16[256,3072]{1,0:T(8,128)(2,1)S(1)}, u32[]{:S(2)}, u32[]{:S(2)}) %collective-permute-start.21) | collective-permute-done | bytes 1572896 | tf_op jit(solution)/shard_map/ppermute | solution.py:394
  146.7 1.4 collective-permute-start.16
  148.1 1.6 collective-permute-start.22
  149.7 1.6 collective-permute-start.20
  151.3 1.0 slice_bitcast_fusion.1
  152.4 14.3 %collective-permute-done.16.refs_3_ = bf16[32,6144]{1,0:T(8,128)(2,1)S(1)} collective-permute-done((bf16[32,6144]{1,0:T(8,128)(2,1)S(1)}, bf16[32,6144]{1,0:T(8,128)(2,1)S(1)}, u32[]{:S(2)}, u32[]{:S(2)}) %collective-permute-start.16) | collective-permute-done | bytes 393248 | tf_op jit(solution)/shard_map/ppermute | solution.py:388
  166.7 1.7 shard_map.109
  168.4 15.5 %shard_map.114 = (bf16[1536,1024]{1,0:T(8,128)(2,1)}, bf16[1536,1024]{1,0:T(8,128)(2,1)}, bf16[1024,1536]{1,0:T(8,128)(2,1)}) custom-call(bf16[2,4,32,1536]{3,2,1,0:T(8,128)(2,1)} %copy-done.4, bf16[2,4,32,1536]{3,2,1,0:T(8,128)(2,1)} %copy-done.2, bf16[2,4,64,1536]{3,2,1,0:T(8,128)(2,1)} %copy-done.13, bf16[2,4,32,1536]{3,2,1,0:T(8,128)(2,1)} %copy-done.12, ...), custom_call_target="tpu_custom_call" | custom-call | flops 7247757312 | bytes 28311552 | tf_op jit(solution)/shard_map/pallas_call | solution.py:369
  184.0 0.9 copy-done.21
  184.9 0.3 copy-done.22
  185.2 10.9 %shard_map.115 = (bf16[1536,1024]{1,0:T(8,128)(2,1)}, bf16[1536,1024]{1,0:T(8,128)(2,1)}, bf16[1024,1536]{1,0:T(8,128)(2,1)}) custom-call(bf16[2,64,1536]{2,1,0:T(8,128)(2,1)} %copy-done.7, bf16[2,64,1536]{2,1,0:T(8,128)(2,1)} %copy-done.10, bf16[2,64,1536]{2,1,0:T(8,128)(2,1)} %get-tuple-element.53.refs_2_, bf16[2,64,1536]{2,1,0:T(8,128)(2,1)} %get-tuple-element.50.refs_3_, ...), custom_call_target="tpu_custom_call" | custom-call | flops 2415919104 | bytes 22020096 | tf_op jit(solution)/shard_map/pallas_call | solution.py:369
  (62 shorter events, 0.3 us)
Async XLA Ops:
  4.7 22.8 %collective-permute-start = (bf16[2,4,32,1536]{3,2,1,0:T(8,128)(2,1)}, bf16[2,4,32,1536]{3,2,1,0:T(8,128)(2,1)S(1)}, u32[]{:S(2)}, u32[]{:S(2)}) collective-permute-start(bf16[2,4,32,1536]{3,2,1,0:T(8,128)(2,1)} %get-tuple-element.27.refs_0_), channel_id=1, source_target_pairs={{0,2},{1,3},{2,4},{3,5},{4,6},{5,7},{6,0},{7,1},{8,10},{9,11},{10,... | collective-permute-start | bytes 2359304 | tf_op jit(solution)/shard_map/ppermute | solution.py:388
  27.5 1.1 copy-start.3
  28.7 42.7 %copy-start.2 = (bf16[2,4,32,1536]{3,2,1,0:T(8,128)(2,1)}, bf16[2,4,32,1536]{3,2,1,0:T(8,128)(2,1)S(1)}, u32[]{:S(2)}) copy-start(bf16[2,4,32,1536]{3,2,1,0:T(8,128)(2,1)S(1)} %collective-permute-done.refs_1_) | copy-start | bytes 2359300
  28.7 0.9 copy-start.4
  29.6 2.5 %collective-permute-start.3 = (bf16[2,4,32,1536]{3,2,1,0:T(8,128)(2,1)}, bf16[2,4,32,1536]{3,2,1,0:T(8,128)(2,1)S(1)}, u32[]{:S(2)}, u32[]{:S(2)}) collective-permute-start(bf16[2,4,32,1536]{3,2,1,0:T(8,128)(2,1)} %copy-done.4), channel_id=1, source_target_pairs={{0,1},{1,0},{2,3},{3,2},{4,5},{5,4},{6,7},{7,6},{8,9},{9,8},{10,11... | collective-permute-start | bytes 2359304 | tf_op jit(solution)/shard_map/ppermute | solution.py:391
  29.6 20.4 %collective-permute-start.1 = (bf16[2,4,32,1536]{3,2,1,0:T(8,128)(2,1)}, bf16[2,4,32,1536]{3,2,1,0:T(8,128)(2,1)S(1)}, u32[]{:S(2)}, u32[]{:S(2)}) collective-permute-start(bf16[2,4,32,1536]{3,2,1,0:T(8,128)(2,1)} %copy-done.4), channel_id=1, source_target_pairs={{0,6},{1,7},{2,0},{3,1},{4,2},{5,3},{6,4},{7,5},{8,14},{9,15},{10,... | collective-permute-start | bytes 2359304 | tf_op jit(solution)/shard_map/ppermute | solution.py:388
  31.3 21.1 %collective-permute-start.7 = (bf16[2,4,32,1536]{3,2,1,0:T(8,128)(2,1)S(1)}, bf16[2,4,32,1536]{3,2,1,0:T(8,128)(2,1)S(1)}, u32[]{:S(2)}, u32[]{:S(2)}) collective-permute-start(bf16[2,4,32,1536]{3,2,1,0:T(8,128)(2,1)S(1)} %collective-permute-done.refs_1_), channel_id=1, source_target_pairs={{0,1},{1,0},{2,3},{3,2},{4,5},{5,4},{6,7},{7,6},{8,9},{9,8},{10,11... | collective-permute-start | bytes 2359304 | tf_op jit(solution)/shard_map/ppermute | solution.py:391
  31.6 35.2 %collective-permute-start.2 = (bf16[2,4,32,1536]{3,2,1,0:T(8,128)(2,1)S(1)}, bf16[2,4,32,1536]{3,2,1,0:T(8,128)(2,1)S(1)}, u32[]{:S(2)}, u32[]{:S(2)}) collective-permute-start(bf16[2,4,32,1536]{3,2,1,0:T(8,128)(2,1)S(1)} %collective-permute-done.refs_1_), channel_id=1, source_target_pairs={{0,2},{1,3},{2,4},{3,5},{4,6},{5,7},{6,0},{7,1},{8,10},{9,11},{10,... | collective-permute-start | bytes 2359304 | tf_op jit(solution)/shard_map/ppermute | solution.py:388
  32.1 1.1 copy-start.5
  33.2 38.2 %copy-start.12 = (bf16[2,4,32,1536]{3,2,1,0:T(8,128)(2,1)}, bf16[2,4,32,1536]{3,2,1,0:T(8,128)(2,1)S(1)}, u32[]{:S(2)}) copy-start(bf16[2,4,32,1536]{3,2,1,0:T(8,128)(2,1)S(1)} %collective-permute-done.3.refs_2_.refs_3_) | copy-start | bytes 2359300
  34.0 32.7 %collective-permute-start.4 = (bf16[2,64,1536]{2,1,0:T(8,128)(2,1)S(1)}, bf16[2,64,1536]{2,1,0:T(8,128)(2,1)S(1)}, u32[]{:S(2)}, u32[]{:S(2)}) collective-permute-start(bf16[2,64,1536]{2,1,0:T(8,128)(2,1)S(1)} %get-tuple-element.28), channel_id=1, source_target_pairs={{0,8},{8,0},{16,24},{24,16},{1,9},{9,1},{17,25},{25,17},{2,10},{10... | collective-permute-start | bytes 1179656 | tf_op jit(solution)/shard_map/ppermute | solution.py:394
  35.6 31.2 %collective-permute-start.5 = (bf16[2,64,1536]{2,1,0:T(8,128)(2,1)S(1)}, bf16[2,64,1536]{2,1,0:T(8,128)(2,1)S(1)}, u32[]{:S(2)}, u32[]{:S(2)}) collective-permute-start(bf16[2,64,1536]{2,1,0:T(8,128)(2,1)S(1)} %get-tuple-element.29), channel_id=1, source_target_pairs={{0,16},{8,24},{16,0},{24,8},{1,17},{9,25},{17,1},{25,9},{2,18},{10... | collective-permute-start | bytes 1179656 | tf_op jit(solution)/shard_map/ppermute | solution.py:394
  50.0 22.6 %copy-start.6 = (bf16[2,4,32,1536]{3,2,1,0:T(8,128)(2,1)S(1)}, bf16[2,4,32,1536]{3,2,1,0:T(8,128)(2,1)}, u32[]{:S(2)}) copy-start(bf16[2,4,32,1536]{3,2,1,0:T(8,128)(2,1)} %copy-done.4) | copy-start | bytes 2359300
  50.0 16.8 %collective-permute-start.6 = (bf16[2,64,1536]{2,1,0:T(8,128)(2,1)S(1)}, bf16[2,64,1536]{2,1,0:T(8,128)(2,1)S(1)}, u32[]{:S(2)}, u32[]{:S(2)}) collective-permute-start(bf16[2,64,1536]{2,1,0:T(8,128)(2,1)S(1)} %get-tuple-element.30), channel_id=1, source_target_pairs={{0,24},{8,16},{16,8},{24,0},{1,25},{9,17},{17,9},{25,1},{2,26},{10... | collective-permute-start | bytes 1179656 | tf_op jit(solution)/shard_map/ppermute | solution.py:394
  52.4 19.0 %copy-start.11 = (bf16[2,4,32,1536]{3,2,1,0:T(8,128)(2,1)}, bf16[2,4,32,1536]{3,2,1,0:T(8,128)(2,1)S(1)}, u32[]{:S(2)}) copy-start(bf16[2,4,32,1536]{3,2,1,0:T(8,128)(2,1)S(1)} %collective-permute-done.7.refs_5_.refs_4_) | copy-start | bytes 2359300
  66.8 46.1 %copy-start.14 = (bf16[2,64,1536]{2,1,0:T(8,128)(2,1)}, bf16[2,64,1536]{2,1,0:T(8,128)(2,1)S(1)}, u32[]{:S(2)}) copy-start(bf16[2,64,1536]{2,1,0:T(8,128)(2,1)S(1)} %collective-permute-done.4.refs_2_.refs_0_.refs_6_) | copy-start | bytes 1179652
  66.8 46.1 %copy-start.15 = (bf16[2,64,1536]{2,1,0:T(8,128)(2,1)}, bf16[2,64,1536]{2,1,0:T(8,128)(2,1)S(1)}, u32[]{:S(2)}) copy-start(bf16[2,64,1536]{2,1,0:T(8,128)(2,1)S(1)} %collective-permute-done.5.refs_3_.refs_1_.refs_10_) | copy-start | bytes 1179652
  66.8 46.1 %copy-start.7 = (bf16[2,64,1536]{2,1,0:T(8,128)(2,1)}, bf16[2,64,1536]{2,1,0:T(8,128)(2,1)S(1)}, u32[]{:S(2)}) copy-start(bf16[2,64,1536]{2,1,0:T(8,128)(2,1)S(1)} %collective-permute-done.6.refs_4_.refs_2_.refs_0_) | copy-start | bytes 1179652
  67.8 3.7 %copy-start.13 = (bf16[2,4,64,1536]{3,2,1,0:T(8,128)(2,1)}, bf16[2,4,64,1536]{3,2,1,0:T(8,128)(2,1)S(1)}, u32[]{:S(2)}) copy-start(bf16[2,4,64,1536]{3,2,1,0:T(8,128)(2,1)S(1)} %get-tuple-element.31.refs_2_) | copy-start | bytes 4718596
  67.8 3.6 %collective-permute-start.8 = (bf16[2,4,64,1536]{3,2,1,0:T(8,128)(2,1)S(1)}, bf16[2,4,64,1536]{3,2,1,0:T(8,128)(2,1)S(1)}, u32[]{:S(2)}, u32[]{:S(2)}) collective-permute-start(bf16[2,4,64,1536]{3,2,1,0:T(8,128)(2,1)S(1)} %get-tuple-element.31.refs_2_), channel_id=1, source_target_pairs={{0,1},{1,0},{2,3},{3,2},{4,5},{5,4},{6,7},{7,6},{8,9},{9,8},{10,11... | collective-permute-start | bytes 4718600 | tf_op jit(solution)/shard_map/ppermute | solution.py:391
  67.9 25.4 %collective-permute-start.10 = (bf16[2,64,1536]{2,1,0:T(8,128)(2,1)S(1)}, bf16[2,64,1536]{2,1,0:T(8,128)(2,1)S(1)}, u32[]{:S(2)}, u32[]{:S(2)}) collective-permute-start(bf16[2,64,1536]{2,1,0:T(8,128)(2,1)S(1)} %get-tuple-element.33), channel_id=1, source_target_pairs={{0,16},{8,24},{16,0},{24,8},{1,17},{9,25},{17,1},{25,9},{2,18},{10... | collective-permute-start | bytes 1179656 | tf_op jit(solution)/shard_map/ppermute | solution.py:394
  69.4 23.8 %collective-permute-start.11 = (bf16[2,64,1536]{2,1,0:T(8,128)(2,1)S(1)}, bf16[2,64,1536]{2,1,0:T(8,128)(2,1)S(1)}, u32[]{:S(2)}, u32[]{:S(2)}) collective-permute-start(bf16[2,64,1536]{2,1,0:T(8,128)(2,1)S(1)} %get-tuple-element.34), channel_id=1, source_target_pairs={{0,24},{8,16},{16,8},{24,0},{1,25},{9,17},{17,9},{25,1},{2,26},{10... | collective-permute-start | bytes 1179656 | tf_op jit(solution)/shard_map/ppermute | solution.py:394
  70.9 22.4 %collective-permute-start.9 = (bf16[2,64,1536]{2,1,0:T(8,128)(2,1)S(1)}, bf16[2,64,1536]{2,1,0:T(8,128)(2,1)S(1)}, u32[]{:S(2)}, u32[]{:S(2)}) collective-permute-start(bf16[2,64,1536]{2,1,0:T(8,128)(2,1)S(1)} %get-tuple-element.32), channel_id=1, source_target_pairs={{0,8},{8,0},{16,24},{24,16},{1,9},{9,1},{17,25},{25,17},{2,10},{10... | collective-permute-start | bytes 1179656 | tf_op jit(solution)/shard_map/ppermute | solution.py:394
  71.4 1.1 copy-start.20
  93.3 13.8 %copy-start.16 = (bf16[2,64,1536]{2,1,0:T(8,128)(2,1)}, bf16[2,64,1536]{2,1,0:T(8,128)(2,1)S(1)}, u32[]{:S(2)}) copy-start(bf16[2,64,1536]{2,1,0:T(8,128)(2,1)S(1)} %collective-permute-done.10.refs_1_.refs_11_) | copy-start | bytes 1179652
  93.3 13.8 %copy-start.10 = (bf16[2,64,1536]{2,1,0:T(8,128)(2,1)}, bf16[2,64,1536]{2,1,0:T(8,128)(2,1)S(1)}, u32[]{:S(2)}) copy-start(bf16[2,64,1536]{2,1,0:T(8,128)(2,1)S(1)} %collective-permute-done.11.refs_2_.refs_1_) | copy-start | bytes 1179652
  93.3 13.8 %copy-start.17 = (bf16[2,64,1536]{2,1,0:T(8,128)(2,1)}, bf16[2,64,1536]{2,1,0:T(8,128)(2,1)S(1)}, u32[]{:S(2)}) copy-start(bf16[2,64,1536]{2,1,0:T(8,128)(2,1)S(1)} %collective-permute-done.9.refs_0_.refs_7_) | copy-start | bytes 1179652
  107.0 6.6 %collective-permute-start.12 = (bf16[128,3072]{1,0:T(8,128)(2,1)S(1)}, bf16[128,3072]{1,0:T(8,128)(2,1)S(1)}, u32[]{:S(2)}, u32[]{:S(2)}) collective-permute-start(bf16[128,3072]{1,0:T(8,128)(2,1)S(1)} %get-tuple-element.36), channel_id=1, source_target_pairs={{0,1},{1,0},{2,3},{3,2},{4,5},{5,4},{6,7},{7,6},{8,9},{9,8},{10,11... | collective-permute-start | bytes 2359304 | tf_op jit(solution)/shard_map/ppermute | solution.py:391
  107.1 1.4 copy-start
  108.5 1.4 copy-start.19
  109.1 8.4 %collective-permute-start.18 = (bf16[3,2,64,1536]{3,2,1,0:T(8,128)(2,1)S(1)}, bf16[3,2,64,1536]{3,2,1,0:T(8,128)(2,1)S(1)}, u32[]{:S(2)}, u32[]{:S(2)}) collective-permute-start(bf16[3,2,64,1536]{3,2,1,0:T(8,128)(2,1)S(1)} %shard_map.111), channel_id=1, source_target_pairs={{0,1},{1,0},{2,3},{3,2},{4,5},{5,4},{6,7},{7,6},{8,9},{9,8},{10,11... | collective-permute-start | bytes 3538952 | tf_op jit(solution)/shard_map/ppermute | solution.py:391
  109.9 36.8 %collective-permute-start.21 = (bf16[256,3072]{1,0:T(8,128)(2,1)S(1)}, bf16[256,3072]{1,0:T(8,128)(2,1)S(1)}, u32[]{:S(2)}, u32[]{:S(2)}) collective-permute-start(bf16[256,3072]{1,0:T(8,128)(2,1)S(1)} %copy-done.19), channel_id=1, source_target_pairs={{0,16},{8,24},{16,0},{24,8},{1,17},{9,25},{17,1},{25,9},{2,18},{10... | collective-permute-start | bytes 4718600 | tf_op jit(solution)/shard_map/ppermute | solution.py:394
  111.4 36.7 %collective-permute-start.19 = (bf16[256,3072]{1,0:T(8,128)(2,1)S(1)}, bf16[256,3072]{1,0:T(8,128)(2,1)S(1)}, u32[]{:S(2)}, u32[]{:S(2)}) collective-permute-start(bf16[256,3072]{1,0:T(8,128)(2,1)S(1)} %copy-done.19), channel_id=1, source_target_pairs={{0,8},{8,0},{16,24},{24,16},{1,9},{9,1},{17,25},{25,17},{2,10},{10... | collective-permute-start | bytes 4718600 | tf_op jit(solution)/shard_map/ppermute | solution.py:394
  112.9 2.3 %copy-start.1 = (bf16[128,6144]{1,0:T(8,128)(2,1)S(1)}, bf16[128,6144]{1,0:T(8,128)(2,1)}, u32[]{:S(2)}) copy-start(bf16[128,6144]{1,0:T(8,128)(2,1)} %get-tuple-element.35.mine.refs_3_) | copy-start | bytes 4718596
  112.9 2.3 %collective-permute-start.13 = (bf16[128,3072]{1,0:T(8,128)(2,1)S(1)}, bf16[128,3072]{1,0:T(8,128)(2,1)S(1)}, u32[]{:S(2)}, u32[]{:S(2)}) collective-permute-start(bf16[128,3072]{1,0:T(8,128)(2,1)S(1)} %get-tuple-element.37), channel_id=1, source_target_pairs={{0,1},{1,0},{2,3},{3,2},{4,5},{5,4},{6,7},{7,6},{8,9},{9,8},{10,11... | collective-permute-start | bytes 2359304 | tf_op jit(solution)/shard_map/ppermute | solution.py:391
  113.5 36.2 %collective-permute-start.17 = (bf16[3,2,64,1536]{3,2,1,0:T(8,128)(2,1)S(1)}, bf16[3,2,64,1536]{3,2,1,0:T(8,128)(2,1)S(1)}, u32[]{:S(2)}, u32[]{:S(2)}) collective-permute-start(bf16[3,2,64,1536]{3,2,1,0:T(8,128)(2,1)S(1)} %shard_map.110), channel_id=1, source_target_pairs={{0,1},{1,0},{2,3},{3,2},{4,5},{5,4},{6,7},{7,6},{8,9},{9,8},{10,11... | collective-permute-start | bytes 3538952 | tf_op jit(solution)/shard_map/ppermute | solution.py:391
  115.6 36.8 %collective-permute-start.14 = (bf16[32,6144]{1,0:T(8,128)(2,1)S(1)}, bf16[32,6144]{1,0:T(8,128)(2,1)S(1)}, u32[]{:S(2)}, u32[]{:S(2)}) collective-permute-start(bf16[32,6144]{1,0:T(8,128)(2,1)S(1)} %get-tuple-element.39), channel_id=1, source_target_pairs={{0,6},{1,7},{2,0},{3,1},{4,2},{5,3},{6,4},{7,5},{8,14},{9,15},{10,... | collective-permute-start | bytes 1179656 | tf_op jit(solution)/shard_map/ppermute | solution.py:388
  117.4 34.9 %collective-permute-start.15 = (bf16[32,6144]{1,0:T(8,128)(2,1)S(1)}, bf16[32,6144]{1,0:T(8,128)(2,1)S(1)}, u32[]{:S(2)}, u32[]{:S(2)}) collective-permute-start(bf16[32,6144]{1,0:T(8,128)(2,1)S(1)} %get-tuple-element.40), channel_id=1, source_target_pairs={{0,2},{1,3},{2,4},{3,5},{4,6},{5,7},{6,0},{7,1},{8,10},{9,11},{10,... | collective-permute-start | bytes 1179656 | tf_op jit(solution)/shard_map/ppermute | solution.py:388
  146.7 20.0 %collective-permute-start.16 = (bf16[32,6144]{1,0:T(8,128)(2,1)S(1)}, bf16[32,6144]{1,0:T(8,128)(2,1)S(1)}, u32[]{:S(2)}, u32[]{:S(2)}) collective-permute-start(bf16[32,6144]{1,0:T(8,128)(2,1)S(1)} %get-tuple-element.41), channel_id=1, source_target_pairs={{0,4},{1,5},{2,6},{3,7},{4,0},{5,1},{6,2},{7,3},{8,12},{9,13},{10,... | collective-permute-start | bytes 1179656 | tf_op jit(solution)/shard_map/ppermute | solution.py:388
  148.0 1.6 copy-start.9
  148.1 35.9 %collective-permute-start.22 = (bf16[128,3072]{1,0:T(8,128)(2,1)S(1)}, bf16[128,3072]{1,0:T(8,128)(2,1)S(1)}, u32[]{:S(2)}, u32[]{:S(2)}) collective-permute-start(bf16[128,3072]{1,0:T(8,128)(2,1)S(1)} %slice.35), channel_id=1, source_target_pairs={{0,8},{8,0},{16,24},{24,16},{1,9},{9,1},{17,25},{25,17},{2,10},{10... | collective-permute-start | bytes 2359304 | tf_op jit(solution)/shard_map/ppermute | solution.py:394
  149.7 2.7 %copy-start.8 = (bf16[256,3072]{1,0:T(8,128)(2,1)}, bf16[256,3072]{1,0:T(8,128)(2,1)S(1)}, u32[]{:S(2)}) copy-start(bf16[256,3072]{1,0:T(8,128)(2,1)S(1)} %shard_map.112.refs_15_) | copy-start | bytes 4718596
  149.7 17.0 %copy-start.18 = (bf16[32,128]{1,0:T(8,128)(2,1)S(1)}, bf16[32,128]{1,0:T(8,128)(2,1)}, u32[]{:S(2)}) copy-start(bf16[32,128]{1,0:T(8,128)(2,1)} %get-tuple-element.26.sel) | copy-start | bytes 24580
  149.7 34.3 %collective-permute-start.20 = (bf16[128,3072]{1,0:T(8,128)(2,1)S(1)}, bf16[128,3072]{1,0:T(8,128)(2,1)S(1)}, u32[]{:S(2)}, u32[]{:S(2)}) collective-permute-start(bf16[128,3072]{1,0:T(8,128)(2,1)S(1)} %slice.34), channel_id=1, source_target_pairs={{0,16},{8,24},{16,0},{24,8},{1,17},{9,25},{17,1},{25,9},{2,18},{10... | collective-permute-start | bytes 2359304 | tf_op jit(solution)/shard_map/ppermute | solution.py:394
  184.0 0.9 copy-start.21
  184.0 1.2 copy-start.22

commit v3 on v2

--- a/solution.py
+++ b/solution.py
@@ -43,7 +43,7 @@
     return copies
 
 
-def pick_kernel(me, routes, probs, tokens, out_grad, sel_out, both, held, sem):
+def pick_kernel(me, routes, probs, tokens, out_grad, sel_out, both, again, held, sem):
     _, n_dp, _, width = both.shape
     copies = fetch(tokens, held.at[0], sem.at[0], n_dp) + fetch(out_grad, held.at[1], sem.at[1], n_dp)
     n = tokens.shape[0]
@@ -66,15 +66,16 @@
         cols = pl.ds(pl.multiple_of((me[0] ^ k) * width, 128), width)
         both[0, k] = mm(sel, held[0, :, cols]).astype(BF16)
         both[1, k] = (scale * mm(sel, held[1, :, cols])).astype(BF16)
+        again[:, k] = both[:, k]
 
 
 def pick(me, tokens, routes, probs, out_grad, n_dp):
     n, d = tokens.shape
     return pl.pallas_call(
         pick_kernel,
-        out_shape=(shape((CAP, n)), shape((2, n_dp, CAP, d // n_dp))),
+        out_shape=(shape((CAP, n)),) + (shape((2, n_dp, CAP, d // n_dp)),) * 2,
         in_specs=[SMEM, VMEM, VMEM, ANY, ANY],
-        out_specs=(VMEM,) * 2,
+        out_specs=(VMEM,) * 3,
         scratch_shapes=[pltpu.VMEM((2, n, d), BF16), pltpu.SemaphoreType.DMA((2, n_dp))],
         compiler_params=params(60 << 20),
         cost_estimate=cost(4 * CAP * n * d, 5 * n * d),
@@ -117,13 +118,14 @@
 def lay(blocks, whole, deps=()):
     arrays, slices, _, width = blocks[0].shape
     rows = sum(b.shape[2] for b in blocks)
-    outs = [shape((arrays, slices, rows, width))] * whole + [shape((arrays, rows, width))] * (slices - 1)
+    cut = slices - 1
+    outs = [shape((arrays, slices, rows, width))] * whole + [shape((arrays, rows, width))] * cut
     return pl.pallas_call(
         functools.partial(lay_kernel, len(blocks), len(deps), whole),
         out_shape=outs,
         in_specs=[ANY] * (len(blocks) + len(deps)),
         out_specs=[ANY] * len(outs),
-        scratch_shapes=[pltpu.SemaphoreType.DMA((len(blocks) * (whole + slices - 1),))],
+        scratch_shapes=[pltpu.SemaphoreType.DMA((len(blocks) * (whole + cut),))],
         compiler_params=params(1 << 20),
         cost_estimate=cost(0, 4 * arrays * slices * rows * width),
     )(*blocks, *deps)
@@ -176,38 +178,40 @@
             copy.wait()
 
 
-def slab_kernel(count, me, *refs):
-    parts, (gw, uw, dw, out, rows, gate, up, wide, tall, wide_sem, tall_sem) = refs[:count], refs[count:]
+def slab_kernel(count, sides, me, *refs):
+    parts, refs = refs[:count], refs[count:]
+    gw, uw, dw, out, mine, left, right, rows, gate, up, wide, tall, wide_sem, tall_sem = refs
     ff, piece = gw.shape[1], tall.shape[1]
     _, n_dp, _, width = parts[0].shape
-    sub = wide.shape[2]
-    forth = []
+    sub = 768 if width % 768 == 0 else width
+    steps = width // sub
+    forth, spans = [], []
     for k in range(n_dp):
-        for s in range(width // sub):
-            source = pl.ds(pl.multiple_of((me[0] ^ k) * width + s * sub, 128), sub)
-            slot = len(forth) % 3
+        for s in range(steps):
+            span = pl.ds(pl.multiple_of((me[0] ^ k) * width + s * sub, 128), sub)
+            slot = len(forth) % 4
+            spans.append(span)
             forth.append([
-                pltpu.make_async_copy(w.at[source], wide.at[slot, j], wide_sem.at[slot, j])
-                for j, w in enumerate((gw, uw))
+                pltpu.make_async_copy(w.at[span], wide.at[j, span], wide_sem.at[slot, j]) for j, w in enumerate((gw, uw))
             ])
     back = Stream([
         [pltpu.make_async_copy(dw.at[pl.ds(i * piece, piece)], tall.at[i % 3], tall_sem.at[i % 3])]
         for i in range(ff // piece)
     ])
     forth = Stream(forth)
-    forth.start(2)
-    total = len(forth.copies)
-    for i in range(total):
-        k, s = i // (width // sub), i % (width // sub)
+    forth.start(1)
+    gather_rows(me, 1, parts, rows)
+    forth.start(3)
+    for i, span in enumerate(spans):
+        k, s = i // steps, i % steps
         forth.take(i)
-        forth.start(i + 3)
-        if i >= total - 2:
-            back.start(i + 3 - total)
+        forth.start(i + 4)
+        if i >= len(spans) - 2:
+            back.start(i + 3 - len(spans))
         some = jnp.concatenate([p[0, k, :, s * sub : (s + 1) * sub] for p in parts])
         for acc, j in ((gate, 0), (up, 1)):
-            more = mm(some, wide[i % 3, j])
+            more = mm(some, wide[j, span])
             acc[...] = more if i == 0 else acc[...] + more
-    gather_rows(me, 1, parts, rows)
     g, u = gate[...], up[...]
     sig = jax.nn.sigmoid(g)
     act = g * sig
@@ -222,68 +226,57 @@
         grad = mm(rows[...], tall[i % 3], LAST)
         out[:, ff + at : ff + at + piece] = (grad * up[:, cols]).astype(BF16)
         out[:, 2 * ff + at : 2 * ff + at + piece] = (grad * gate[:, cols]).astype(BF16)
-
-
-def slab(me, parts, gw, uw, dw):
-    rows, (d, ff) = sum(p.shape[2] for p in parts), gw.shape
-    width = parts[0].shape[3]
-    sub = 768 if width % 768 == 0 else width
-    return pl.pallas_call(
-        functools.partial(slab_kernel, len(parts)),
-        out_shape=shape((rows, 3 * ff)),
-        in_specs=[SMEM] + [VMEM] * len(parts) + [ANY] * 3,
-        out_specs=VMEM,
+    d = wide.shape[1]
+    tile = 512
+    for i in range(d // tile):
+        cols = slice(i * tile, (i + 1) * tile)
+        half = slice(i * tile % (d // 2), i * tile % (d // 2) + tile)
+        theirs = left if i * tile < d // 2 else right
+        term = mm(out[:, ff : 2 * ff], wide[0, cols], LAST) + mm(out[:, 2 * ff :], wide[1, cols], LAST)
+        at, to = 0, [0, 0]
+        for side, size in sides:
+            some = term[at : at + size].astype(BF16)
+            if side == 0:
+                mine[to[0] : to[0] + size, cols] = some
+            else:
+                theirs[to[1] : to[1] + size, half] = some
+            at += size
+            to[side] += size
+
+
+def slab(me, parts, sides, gw, uw, dw, dep):
+    sizes = [p.shape[2] for p in parts]
+    rows, (d, ff) = sum(sizes), gw.shape
+    n = len(parts) + 3
+
+    def kernel(me, *refs):
+        slab_kernel(len(parts), tuple(zip(sides, sizes)), me, *refs[:n], *refs[n + 1 :])
+
+    return pl.pallas_call(
+        kernel,
+        out_shape=(
+            shape((rows, 3 * ff)),
+            shape((rows // 2, d)),
+            shape((rows // 2, d // 2)),
+            shape((rows // 2, d // 2)),
+        ),
+        in_specs=[SMEM] + [VMEM] * len(parts) + [ANY] * 4,
+        out_specs=(VMEM,) * 4,
         scratch_shapes=[
             pltpu.VMEM((rows, d), BF16),
             pltpu.VMEM((rows, ff), F32),
             pltpu.VMEM((rows, ff), F32),
-            pltpu.VMEM((3, 2, sub, ff), BF16),
+            pltpu.VMEM((2, d, ff), BF16),
             pltpu.VMEM((3, 256, d), BF16),
-            pltpu.SemaphoreType.DMA((3, 2)),
+            pltpu.SemaphoreType.DMA((4, 2)),
             pltpu.SemaphoreType.DMA((3,)),
         ],
-        compiler_params=params(50 << 20),
-        cost_estimate=cost(6 * rows * gw.size, 6 * gw.size, 1),
-    )(me, *parts, gw, uw, dw)
-
-
-def term_kernel(grads, gw, uw, *refs):
-    mine, left, right, held, sem = refs[-5:]
-    ff, half, width = gw.shape[1], mine.shape[0], mine.shape[1]
-    tile = held.shape[2]
-    copies = []
-    for i in range(width // tile):
-        rows, slot = pl.ds(i * tile, tile), i % 4
-        copies.append([
-            pltpu.make_async_copy(w.at[rows], held.at[slot, j], sem.at[slot, j]) for j, w in enumerate((gw, uw))
-        ])
-    stream = Stream(copies)
-    stream.start(3)
-    for i in range(width // tile):
-        cols = slice(i * tile, (i + 1) * tile)
-        stream.take(i)
-        stream.start(i + 4)
-        held_gate, held_up = held[i % 4, 0], held[i % 4, 1]
-        term = mm(grads[:, ff : 2 * ff], held_gate, LAST) + mm(grads[:, 2 * ff :], held_up, LAST)
-        mine[:, cols] = term[:half].astype(BF16)
-        theirs = left if i * tile < width // 2 else right
-        theirs[:, i * tile % (width // 2) : i * tile % (width // 2) + tile] = term[half:].astype(BF16)
-
-
-def term(grads, gw, uw, deps):
-    rows, (d, ff) = grads.shape[0], gw.shape
-    return pl.pallas_call(
-        term_kernel,
-        out_shape=(shape((rows // 2, d)), shape((rows // 2, d // 2)), shape((rows // 2, d // 2))),
-        in_specs=[VMEM, ANY, ANY] + [ANY] * len(deps),
-        out_specs=(VMEM,) * 3,
-        scratch_shapes=[pltpu.VMEM((4, 2, 512, ff), BF16), pltpu.SemaphoreType.DMA((4, 2))],
-        compiler_params=params(50 << 20),
-        cost_estimate=cost(4 * rows * gw.size, 4 * gw.size),
-    )(grads, gw, uw, *deps)
-
-
-def fold_kernel(mine, left, right, *outs):
+        compiler_params=params(46 << 20),
+        cost_estimate=cost(10 * rows * gw.size, 6 * gw.size, 1),
+    )(me, *parts, gw, uw, dw, dep)
+
+
+def fold_kernel(mine, left, right, _, *outs):
     half = left.shape[1]
     for i, out in enumerate(outs):
         rows = slice(i * CAP, (i + 1) * CAP)
@@ -291,19 +284,19 @@
             out[:, cols] = (mine[rows, cols].astype(F32) + theirs[rows].astype(F32)).astype(BF16)
 
 
-def fold(mine, left, right):
+def fold(mine, left, right, dep):
     rows, d = mine.shape
     return pl.pallas_call(
         fold_kernel,
         out_shape=[shape((CAP, d))] * (rows // CAP),
-        in_specs=[VMEM] * 3,
+        in_specs=[VMEM] * 3 + [ANY],
         out_specs=[VMEM] * (rows // CAP),
         compiler_params=params(16 << 20),
         cost_estimate=cost(0, 6 * rows * d),
-    )(mine, left, right)
-
-
-def put_kernel(groups, sel, *refs):
+    )(mine, left, right, dep)
+
+
+def put_kernel(groups, sel, _, *refs):
     *parts, out = refs
     each = len(parts) // groups
     for g in range(groups):
@@ -314,17 +307,17 @@
         out[:, g * width : (g + 1) * width] = mm(sel[...], total.astype(BF16), ROWS).astype(BF16)
 
 
-def put(sel, groups):
+def put(sel, groups, dep):
     parts = [p for group in groups for p in group]
     d = sum(group[0].shape[1] for group in groups)
     return pl.pallas_call(
         functools.partial(put_kernel, len(groups)),
         out_shape=shape((sel.shape[1], d)),
-        in_specs=[VMEM] * (1 + len(parts)),
+        in_specs=[VMEM, ANY] + [VMEM] * len(parts),
         out_specs=VMEM,
         compiler_params=params(32 << 20),
         cost_estimate=cost(2 * sel.size * d, 4 * sel.size * d),
-    )(sel, *parts)
+    )(sel, dep, *parts)
 
 
 def contract_kernel(n_slices, n_grads, n_totals, *refs):
@@ -361,9 +354,10 @@
     put_tile(2, mm(rows[:, :ff], scaled[:, cols], ROWS))
 
 
-def contract(slices, grads, totals, tile=256):
+def contract(slices, grads, totals, tile=512):
     rows = sum(b.shape[0] for b in grads)
     width, ff = slices[0].shape[-1], grads[0].shape[1] // 3
+    tile = tile if width % tile == 0 else 256
     tall = pl.BlockSpec((tile, ff), lambda i: (i, 0))
     wide = pl.BlockSpec((ff, tile), lambda i: (0, i))
     return pl.pallas_call(
@@ -397,27 +391,25 @@
     for s in range(1, chips // 2 + 1):
         offsets += [-s] if 2 * s == chips else [-s, s]
 
-    sel, both = pick(me, tokens, routes, route_probs, out_grad, n_dp)
-    blocks = {0: both, -1: move(both, 1)}
-    blocks[0] = own = after(both, blocks[-1])
+    sel, own, again = pick(me, tokens, routes, route_probs, out_grad, n_dp)
+    blocks = {0: own, -1: move(own, 1)}
     for s in range(2, chips // 2 + 1):
         blocks[-s] = move(blocks[1 - s], 1)
     for s in range(1, chips // 2):
-        blocks[s] = move(blocks[s - 1], -1)
+        blocks[s] = move(after(again, blocks[-1]) if s == 1 else blocks[s - 1], -1)
     here, beside = [own, blocks[-1]], [blocks[o] for o in offsets[2:]]
-    here_theirs = [swap(own), swap(blocks[-1])]
+    here_theirs = [swap(x) for x in here]
     near_cuts = lay(here, False, here_theirs[:1])
     near_got = [across(cut, k) for k, cut in enumerate(near_cuts, 1)]
     far, *far_cuts = lay(beside, True, near_got + here_theirs[1:])
     far_theirs = swap(far)
     far_got = [across(cut, k) for k, cut in enumerate(far_cuts, 1)]
+    near_theirs = swap(pile(near_got))
 
     parts = here + [far] + here_theirs + [far_theirs]
-    rows = slab(me, parts, gate_weight, up_weight, down_weight)
-    mine, left, right = term(rows, gate_weight, up_weight, far_got)
-    near_theirs = swap(pile(near_got, mine))
-    far_got_theirs = swap(pile(far_got, mine))
-    summed, *others = fold(mine, swap(left), swap(right))
+    rows, mine, left, right = slab(me, parts, (0, 0, 0, 1, 1, 1), gate_weight, up_weight, down_weight, near_theirs)
+    far_got_theirs = swap(pile(far_got, left))
+    summed, *others = fold(mine, swap(after(left, *far_got)), swap(right), far_got_theirs)
     slices = [parts]
     for k in range(n_dp - 1):
         slices.append([near_got[k], far_got[k], near_theirs[k], far_got_theirs[k]])
@@ -431,7 +423,7 @@
         first, last = [rows] + got[:-1], got[-1:]
     totals = contract(sum(slices[:-1], []), first, [])
     gate_grad, up_grad, down_grad = contract(slices[-1], last, totals)
-    token_grad = put(sel, [[summed] + [move(x, o) for x, o in zip(others, offsets[1:])]])
+    token_grad = put(sel, [[summed] + [move(x, o) for x, o in zip(others, offsets[1:])]], totals[2])
     return token_grad, gate_grad, up_grad, down_grad
 
 

time: 197 us -> 172 us (0.87)
  waiting for transfers between devices: 90.6 us -> 77.3 us
  Pallas kernels: 69.8 us -> 61.6 us
    ppermute x6, waiting for transfers between devices: 61.3 us -> 32.9 us  [move(): return lax.ppermute(x, 'fetch', pairs)]
    ppermute x10, waiting for transfers between devices: 28 us -> 40.7 us  [across(): return lax.ppermute(x, 'dp', [(k, k ^ bits) for k in range(n_dp)])]
    pallas_call x3 -> x2, Pallas kernels: 38.3 us -> 31.2 us  [the longest x1 26.9 us: slab(): pl.pallas_call(kernel, out_shape=(shape((rows, 3 * ff)), shape((rows // 2...]
    ppermute x7, waiting for transfers between devices: 1.35 us -> 3.67 us  [swap(): return lax.ppermute(x, 'fetch', [(k, k ^ 1) for k in range(n_fetch)])]
    unnamed x46 -> x44, local copies, waits for them, and re-layouts: 7.2 us -> 5.94 us
  transfers between devices with their start and end apart: 23 -> 23, of which waited for: 7 -> 8; matrix products, arithmetic and copies ran while one was open for 1% -> 1% of each run, Pallas kernels for 21% -> 26%
where the time goes in v3:
time: 172 us; the launch traced here: 171 us
  waiting for transfers between devices  77.3 us (45%)
  Pallas kernels  61.6 us (36%)
  starting transfers between devices  23.4 us (14%)
  local copies, waits for them, and re-layouts  8.12 us (5%)
    ppermute x10, waiting for transfers between devices, across(): return lax.ppermute(x, 'dp', [(k, k ^ bits) for k in range(n_dp)])  40.7 us
    ppermute x6, waiting for transfers between devices, move(): return lax.ppermute(x, 'fetch', pairs)  32.9 us
    pallas_call x1, Pallas kernels, slab(): pl.pallas_call(kernel, out_shape=(shape((rows, 3 * ff)), shape((rows // 2...  26.9 us
    pallas_call x2, Pallas kernels, contract(): pl.pallas_call(functools.partial(contract_kernel, len(slices), len(grads)...  25.3 us
    ppermute x10, starting transfers between devices, across(): return lax.ppermute(x, 'dp', [(k, k ^ bits) for k in range(n_dp)])  13.6 us
    ppermute x6, starting transfers between devices, move(): return lax.ppermute(x, 'fetch', pairs)  8.55 us
    unnamed x44, local copies, waits for them, and re-layouts  5.94 us
    pallas_call x1, Pallas kernels, pick(): pl.pallas_call(pick_kernel, out_shape=(shape((CAP, n)),) + (shape((2, n_d...  4.3 us
  transfers between devices with their start and end apart: 23, of which 8 were waited for; matrix products, arithmetic and copies ran while one was open for 1% of the time, Pallas kernels for 26%

profile of v3, /device:TPU:0, one launch (start us, length us, event | category | flops | bytes accessed | tf_op | source)
XLA Modules:
  0.0 171.3 jit_solution(6861921113302636053)
XLA Ops:
  0.6 4.3 %shard_map.102 = (bf16[32,128]{1,0:T(8,128)(2,1)}, bf16[2,4,32,1536]{3,2,1,0:T(8,128)(2,1)}, bf16[2,4,32,1536]{3,2,1,0:T(8,128)(2,1)}) custom-call(s32[1]{0:T(128)} %bitcast.me, s32[2,128]{1,0:T(2,128)} %bitcast.15, f32[2,128]{1,0:T(2,128)} %bitcast.16, bf16[128,6144]{1,0:T(8,128)(2,1)} %tokens.1, bf16[128,6144]{1,0:T(8,128)(2,1)} %out_grad.1), custom_call_target="tpu_custom_call" | custom-call | flops 1572864 | bytes 61440 | tf_op jit(solution)/shard_map/pallas_call | solution.py:74
  4.9 3.1 %collective-permute-start = (bf16[2,4,32,1536]{3,2,1,0:T(8,128)(2,1)}, bf16[2,4,32,1536]{3,2,1,0:T(8,128)(2,1)S(1)}, u32[]{:S(2)}, u32[]{:S(2)}) collective-permute-start(bf16[2,4,32,1536]{3,2,1,0:T(8,128)(2,1)} %get-tuple-element.29.refs_0_), channel_id=1, source_target_pairs={{0,2},{1,3},{2,4},{3,5},{4,6},{5,7},{6,0},{7,1},{8,10},{9,11},{10,... | collective-permute-start | bytes 2359304 | tf_op jit(solution)/shard_map/ppermute | solution.py:382
  8.0 19.8 %collective-permute-done.refs_1_ = bf16[2,4,32,1536]{3,2,1,0:T(8,128)(2,1)S(1)} collective-permute-done((bf16[2,4,32,1536]{3,2,1,0:T(8,128)(2,1)}, bf16[2,4,32,1536]{3,2,1,0:T(8,128)(2,1)S(1)}, u32[]{:S(2)}, u32[]{:S(2)}) %collective-permute-start) | collective-permute-done | bytes 786464 | tf_op jit(solution)/shard_map/ppermute | solution.py:382
  27.8 1.4 copy-done.12
  29.2 0.8 shard_map.104
  30.0 1.6 collective-permute-start.4
  31.6 1.7 %collective-permute-start.1 = (bf16[2,4,32,1536]{3,2,1,0:T(8,128)(2,1)S(1)}, bf16[2,4,32,1536]{3,2,1,0:T(8,128)(2,1)S(1)}, u32[]{:S(2)}, u32[]{:S(2)}) collective-permute-start(bf16[2,4,32,1536]{3,2,1,0:T(8,128)(2,1)S(1)} %shard_map.103), channel_id=1, source_target_pairs={{0,6},{1,7},{2,0},{3,1},{4,2},{5,3},{6,4},{7,5},{8,14},{9,15},{10,... | collective-permute-start | bytes 2359304 | tf_op jit(solution)/shard_map/ppermute | solution.py:382
  33.3 0.3 collective-permute-start.2
  33.6 1.5 collective-permute-start.5
  35.2 5.3 %collective-permute-done.4.refs_2_.refs_0_.refs_6_ = bf16[2,64,1536]{2,1,0:T(8,128)(2,1)S(1)} collective-permute-done((bf16[2,64,1536]{2,1,0:T(8,128)(2,1)S(1)}, bf16[2,64,1536]{2,1,0:T(8,128)(2,1)S(1)}, u32[]{:S(2)}, u32[]{:S(2)}) %collective-permute-start.4) | collective-permute-done | bytes 393248 | tf_op jit(solution)/shard_map/ppermute | solution.py:388
  40.4 2.2 %collective-permute-start.6 = (bf16[2,64,1536]{2,1,0:T(8,128)(2,1)S(1)}, bf16[2,64,1536]{2,1,0:T(8,128)(2,1)S(1)}, u32[]{:S(2)}, u32[]{:S(2)}) collective-permute-start(bf16[2,64,1536]{2,1,0:T(8,128)(2,1)S(1)} %get-tuple-element.33), channel_id=1, source_target_pairs={{0,24},{8,16},{16,8},{24,0},{1,25},{9,17},{17,9},{25,1},{2,26},{10... | collective-permute-start | bytes 1179656 | tf_op jit(solution)/shard_map/ppermute | solution.py:388
  42.6 11.0 %collective-permute-done.5.refs_3_.refs_1_.refs_10_ = bf16[2,64,1536]{2,1,0:T(8,128)(2,1)S(1)} collective-permute-done((bf16[2,64,1536]{2,1,0:T(8,128)(2,1)S(1)}, bf16[2,64,1536]{2,1,0:T(8,128)(2,1)S(1)}, u32[]{:S(2)}, u32[]{:S(2)}) %collective-permute-start.5) | collective-permute-done | bytes 393248 | tf_op jit(solution)/shard_map/ppermute | solution.py:388
  53.6 13.1 %collective-permute-done.2.refs_1_ = bf16[2,4,32,1536]{3,2,1,0:T(8,128)(2,1)S(1)} collective-permute-done((bf16[2,4,32,1536]{3,2,1,0:T(8,128)(2,1)S(1)}, bf16[2,4,32,1536]{3,2,1,0:T(8,128)(2,1)S(1)}, u32[]{:S(2)}, u32[]{:S(2)}) %collective-permute-start.2) | collective-permute-done | bytes 786464 | tf_op jit(solution)/shard_map/ppermute | solution.py:382
  66.8 0.9 shard_map.105
  67.7 0.1 collective-permute-start.8
  67.8 0.6 shard_map.106
  68.4 0.5 collective-permute-start.10
  69.0 0.8 collective-permute-start.9
  69.8 1.5 collective-permute-start.11
  71.3 1.2 collective-permute-start.12
  72.5 0.4 collective-permute-done.10.refs_9_
  72.9 1.1 copy-done.21
  74.1 26.9 %shard_map.107 = (bf16[256,3072]{1,0:T(8,128)(2,1)S(1)}, bf16[128,6144]{1,0:T(8,128)(2,1)}, bf16[128,3072]{1,0:T(8,128)(2,1)S(1)}, bf16[128,3072]{1,0:T(8,128)(2,1)S(1)}) custom-call(s32[1]{0:T(128)} %bitcast.me, bf16[2,4,32,1536]{3,2,1,0:T(8,128)(2,1)S(1)} %copy-done.13, bf16[2,4,32,1536]{3,2,1,0:T(8,128)(2,1)S(1)} %collective-permute-done.refs_1_, ...), custom_call_target="tpu_custom_call" | custom-call | flops 16106127360 | bytes 37748736 | tf_op jit(solution)/shard_map/pallas_call | solution.py:255
  101.0 0.9 collective-permute-start.14
  101.9 1.5 collective-permute-start.17
  103.5 0.6 shard_map.108
  104.1 0.1 collective-permute-start.13
  104.2 0.1 copy-done.10
  104.3 0.2 copy-done.2
  104.5 0.3 collective-permute-start.15
  104.8 0.2 collective-permute-start.16
  105.0 1.0 slice_bitcast_fusion.1
  106.0 2.1 %collective-permute-done.15.left = bf16[128,3072]{1,0:T(8,128)(2,1)S(1)} collective-permute-done((bf16[128,3072]{1,0:T(8,128)(2,1)S(1)}, bf16[128,3072]{1,0:T(8,128)(2,1)S(1)}, u32[]{:S(2)}, u32[]{:S(2)}) %collective-permute-start.15) | collective-permute-done | bytes 786464 | tf_op jit(solution)/shard_map/ppermute | solution.py:385
  108.1 1.1 collective-permute-done.16.right
  109.3 0.4 shard_map.110
  109.6 1.8 %collective-permute-start.18 = (bf16[32,6144]{1,0:T(8,128)(2,1)S(1)}, bf16[32,6144]{1,0:T(8,128)(2,1)S(1)}, u32[]{:S(2)}, u32[]{:S(2)}) collective-permute-start(bf16[32,6144]{1,0:T(8,128)(2,1)S(1)} %get-tuple-element.44), channel_id=1, source_target_pairs={{0,6},{1,7},{2,0},{3,1},{4,2},{5,3},{6,4},{7,5},{8,14},{9,15},{10,... | collective-permute-start | bytes 1179656 | tf_op jit(solution)/shard_map/ppermute | solution.py:382
  111.4 0.3 collective-permute-start.19
  111.7 1.4 collective-permute-start.20
  113.1 24.5 %collective-permute-done.14.refs_0_ = bf16[256,3072]{1,0:T(8,128)(2,1)S(1)} collective-permute-done((bf16[256,3072]{1,0:T(8,128)(2,1)S(1)}, bf16[256,3072]{1,0:T(8,128)(2,1)S(1)}, u32[]{:S(2)}, u32[]{:S(2)}) %collective-permute-start.14) | collective-permute-done | bytes 1572896 | tf_op jit(solution)/shard_map/ppermute | solution.py:388
  137.6 1.6 collective-permute-start.21
  139.3 0.9 collective-permute-start.22
  140.1 1.1 slice_bitcast_fusion
  141.2 14.8 %shard_map.113 = (bf16[1536,1024]{1,0:T(8,128)(2,1)}, bf16[1536,1024]{1,0:T(8,128)(2,1)}, bf16[1024,1536]{1,0:T(8,128)(2,1)}) custom-call(bf16[2,4,32,1536]{3,2,1,0:T(8,128)(2,1)} %get-tuple-element.29.refs_0_, bf16[2,4,32,1536]{3,2,1,0:T(8,128)(2,1)} %copy-done.5, bf16[2,4,64,1536]{3,2,1,0:T(8,128)(2,1)} %copy-done.17, bf16[2,4,32,1536]{3,2,1,0:T(8,128)(2,1)} %copy-done.14, ...), custom_call_target="tpu_custom_call" | custom-call | flops 7247757312 | bytes 28311552 | tf_op jit(solution)/shard_map/pallas_call | solution.py:363
  156.0 1.9 %copy-done = bf16[1024,1536]{1,0:T(8,128)(2,1)S(1)} copy-done((bf16[1024,1536]{1,0:T(8,128)(2,1)S(1)}, bf16[1024,1536]{1,0:T(8,128)(2,1)}, u32[]{:S(2)}) %copy-start) | copy-done | bytes 3145752
  157.9 1.7 %shard_map.114 = bf16[128,6144]{1,0:T(8,128)(2,1)} custom-call(bf16[32,128]{1,0:T(8,128)(2,1)S(1)} %copy-done.16, bf16[1024,1536]{1,0:T(8,128)(2,1)S(1)} %copy-done, bf16[32,6144]{1,0:T(8,128)(2,1)S(1)} %get-tuple-element.42.refs_1_.refs_0_, bf16[32,6144]{1,0:T(8,128)(2,1)S(1)} %collective-permute-done.18.refs_1_, ...), custom_call_target="tpu_custom_call" | custom-call | flops 786432 | bytes 1572864 | tf_op jit(solution)/shard_map/pallas_call | solution.py:313
  159.7 0.9 copy-done.19
  160.6 0.2 copy-done.20
  160.8 10.5 %shard_map.115 = (bf16[1536,1024]{1,0:T(8,128)(2,1)}, bf16[1536,1024]{1,0:T(8,128)(2,1)}, bf16[1024,1536]{1,0:T(8,128)(2,1)}) custom-call(bf16[2,64,1536]{2,1,0:T(8,128)(2,1)} %copy-done.1, bf16[2,64,1536]{2,1,0:T(8,128)(2,1)} %copy-done.2, bf16[2,64,1536]{2,1,0:T(8,128)(2,1)} %get-tuple-element.55.refs_2_, bf16[2,64,1536]{2,1,0:T(8,128)(2,1)} %get-tuple-element.52.refs_3_, ...), custom_call_target="tpu_custom_call" | custom-call | flops 2415919104 | bytes 22020096 | tf_op jit(solution)/shard_map/pallas_call | solution.py:363
  (60 shorter events, 0.2 us)
Async XLA Ops:
  4.9 22.8 %collective-permute-start = (bf16[2,4,32,1536]{3,2,1,0:T(8,128)(2,1)}, bf16[2,4,32,1536]{3,2,1,0:T(8,128)(2,1)S(1)}, u32[]{:S(2)}, u32[]{:S(2)}) collective-permute-start(bf16[2,4,32,1536]{3,2,1,0:T(8,128)(2,1)} %get-tuple-element.29.refs_0_), channel_id=1, source_target_pairs={{0,2},{1,3},{2,4},{3,5},{4,6},{5,7},{6,0},{7,1},{8,10},{9,11},{10,... | collective-permute-start | bytes 2359304 | tf_op jit(solution)/shard_map/ppermute | solution.py:382
  8.0 19.8 %collective-permute-start.3 = (bf16[2,4,32,1536]{3,2,1,0:T(8,128)(2,1)}, bf16[2,4,32,1536]{3,2,1,0:T(8,128)(2,1)S(1)}, u32[]{:S(2)}, u32[]{:S(2)}) collective-permute-start(bf16[2,4,32,1536]{3,2,1,0:T(8,128)(2,1)} %get-tuple-element.29.refs_0_), channel_id=1, source_target_pairs={{0,1},{1,0},{2,3},{3,2},{4,5},{5,4},{6,7},{7,6},{8,9},{9,8},{10,11... | collective-permute-start | bytes 2359304 | tf_op jit(solution)/shard_map/ppermute | solution.py:385
  27.8 45.1 %copy-start.5 = (bf16[2,4,32,1536]{3,2,1,0:T(8,128)(2,1)}, bf16[2,4,32,1536]{3,2,1,0:T(8,128)(2,1)S(1)}, u32[]{:S(2)}) copy-start(bf16[2,4,32,1536]{3,2,1,0:T(8,128)(2,1)S(1)} %collective-permute-done.refs_1_) | copy-start | bytes 2359300
  27.8 1.4 copy-start.12
  29.2 43.7 %copy-start.14 = (bf16[2,4,32,1536]{3,2,1,0:T(8,128)(2,1)}, bf16[2,4,32,1536]{3,2,1,0:T(8,128)(2,1)S(1)}, u32[]{:S(2)}) copy-start(bf16[2,4,32,1536]{3,2,1,0:T(8,128)(2,1)S(1)} %collective-permute-done.3.refs_2_.refs_3_) | copy-start | bytes 2359300
  29.2 2.4 %copy-start.15 = (bf16[2,4,32,1536]{3,2,1,0:T(8,128)(2,1)S(1)}, bf16[2,4,32,1536]{3,2,1,0:T(8,128)(2,1)}, u32[]{:S(2)}) copy-start(bf16[2,4,32,1536]{3,2,1,0:T(8,128)(2,1)} %get-tuple-element.30.refs_0_) | copy-start | bytes 2359300
  30.0 10.4 %collective-permute-start.4 = (bf16[2,64,1536]{2,1,0:T(8,128)(2,1)S(1)}, bf16[2,64,1536]{2,1,0:T(8,128)(2,1)S(1)}, u32[]{:S(2)}, u32[]{:S(2)}) collective-permute-start(bf16[2,64,1536]{2,1,0:T(8,128)(2,1)S(1)} %get-tuple-element.31), channel_id=1, source_target_pairs={{0,8},{8,0},{16,24},{24,16},{1,9},{9,1},{17,25},{25,17},{2,10},{10... | collective-permute-start | bytes 1179656 | tf_op jit(solution)/shard_map/ppermute | solution.py:388
  31.6 22.0 %collective-permute-start.1 = (bf16[2,4,32,1536]{3,2,1,0:T(8,128)(2,1)S(1)}, bf16[2,4,32,1536]{3,2,1,0:T(8,128)(2,1)S(1)}, u32[]{:S(2)}, u32[]{:S(2)}) collective-permute-start(bf16[2,4,32,1536]{3,2,1,0:T(8,128)(2,1)S(1)} %shard_map.103), channel_id=1, source_target_pairs={{0,6},{1,7},{2,0},{3,1},{4,2},{5,3},{6,4},{7,5},{8,14},{9,15},{10,... | collective-permute-start | bytes 2359304 | tf_op jit(solution)/shard_map/ppermute | solution.py:382
  33.3 33.4 %collective-permute-start.2 = (bf16[2,4,32,1536]{3,2,1,0:T(8,128)(2,1)S(1)}, bf16[2,4,32,1536]{3,2,1,0:T(8,128)(2,1)S(1)}, u32[]{:S(2)}, u32[]{:S(2)}) collective-permute-start(bf16[2,4,32,1536]{3,2,1,0:T(8,128)(2,1)S(1)} %collective-permute-done.refs_1_), channel_id=1, source_target_pairs={{0,2},{1,3},{2,4},{3,5},{4,6},{5,7},{6,0},{7,1},{8,10},{9,11},{10,... | collective-permute-start | bytes 2359304 | tf_op jit(solution)/shard_map/ppermute | solution.py:382
  33.6 33.1 %collective-permute-start.7 = (bf16[2,4,32,1536]{3,2,1,0:T(8,128)(2,1)S(1)}, bf16[2,4,32,1536]{3,2,1,0:T(8,128)(2,1)S(1)}, u32[]{:S(2)}, u32[]{:S(2)}) collective-permute-start(bf16[2,4,32,1536]{3,2,1,0:T(8,128)(2,1)S(1)} %collective-permute-done.refs_1_), channel_id=1, source_target_pairs={{0,1},{1,0},{2,3},{3,2},{4,5},{5,4},{6,7},{7,6},{8,9},{9,8},{10,11... | collective-permute-start | bytes 2359304 | tf_op jit(solution)/shard_map/ppermute | solution.py:385
  33.6 20.0 %collective-permute-start.5 = (bf16[2,64,1536]{2,1,0:T(8,128)(2,1)S(1)}, bf16[2,64,1536]{2,1,0:T(8,128)(2,1)S(1)}, u32[]{:S(2)}, u32[]{:S(2)}) collective-permute-start(bf16[2,64,1536]{2,1,0:T(8,128)(2,1)S(1)} %get-tuple-element.32), channel_id=1, source_target_pairs={{0,16},{8,24},{16,0},{24,8},{1,17},{9,25},{17,1},{25,9},{2,18},{10... | collective-permute-start | bytes 1179656 | tf_op jit(solution)/shard_map/ppermute | solution.py:388
  40.4 27.4 %copy-start.6 = (bf16[2,64,1536]{2,1,0:T(8,128)(2,1)}, bf16[2,64,1536]{2,1,0:T(8,128)(2,1)S(1)}, u32[]{:S(2)}) copy-start(bf16[2,64,1536]{2,1,0:T(8,128)(2,1)S(1)} %collective-permute-done.4.refs_2_.refs_0_.refs_6_) | copy-start | bytes 1179652
  40.4 13.2 %collective-permute-start.6 = (bf16[2,64,1536]{2,1,0:T(8,128)(2,1)S(1)}, bf16[2,64,1536]{2,1,0:T(8,128)(2,1)S(1)}, u32[]{:S(2)}, u32[]{:S(2)}) collective-permute-start(bf16[2,64,1536]{2,1,0:T(8,128)(2,1)S(1)} %get-tuple-element.33), channel_id=1, source_target_pairs={{0,24},{8,16},{16,8},{24,0},{1,25},{9,17},{17,9},{25,1},{2,26},{10... | collective-permute-start | bytes 1179656 | tf_op jit(solution)/shard_map/ppermute | solution.py:388
  53.6 14.2 %copy-start.7 = (bf16[2,64,1536]{2,1,0:T(8,128)(2,1)}, bf16[2,64,1536]{2,1,0:T(8,128)(2,1)S(1)}, u32[]{:S(2)}) copy-start(bf16[2,64,1536]{2,1,0:T(8,128)(2,1)S(1)} %collective-permute-done.5.refs_3_.refs_1_.refs_10_) | copy-start | bytes 1179652
  53.6 14.2 %copy-start.1 = (bf16[2,64,1536]{2,1,0:T(8,128)(2,1)}, bf16[2,64,1536]{2,1,0:T(8,128)(2,1)S(1)}, u32[]{:S(2)}) copy-start(bf16[2,64,1536]{2,1,0:T(8,128)(2,1)S(1)} %collective-permute-done.6.refs_4_.refs_2_.refs_0_) | copy-start | bytes 1179652
  66.8 6.2 %copy-start.11 = (bf16[2,4,32,1536]{3,2,1,0:T(8,128)(2,1)}, bf16[2,4,32,1536]{3,2,1,0:T(8,128)(2,1)S(1)}, u32[]{:S(2)}) copy-start(bf16[2,4,32,1536]{3,2,1,0:T(8,128)(2,1)S(1)} %collective-permute-done.7.refs_5_.refs_4_) | copy-start | bytes 2359300
  67.7 5.2 %copy-start.17 = (bf16[2,4,64,1536]{3,2,1,0:T(8,128)(2,1)}, bf16[2,4,64,1536]{3,2,1,0:T(8,128)(2,1)S(1)}, u32[]{:S(2)}) copy-start(bf16[2,4,64,1536]{3,2,1,0:T(8,128)(2,1)S(1)} %get-tuple-element.34.refs_2_) | copy-start | bytes 4718596
  67.7 6.4 %copy-start.13 = (bf16[2,4,32,1536]{3,2,1,0:T(8,128)(2,1)S(1)}, bf16[2,4,32,1536]{3,2,1,0:T(8,128)(2,1)}, u32[]{:S(2)}) copy-start(bf16[2,4,32,1536]{3,2,1,0:T(8,128)(2,1)} %get-tuple-element.29.refs_0_) | copy-start | bytes 2359300
  67.7 5.2 %collective-permute-start.8 = (bf16[2,4,64,1536]{3,2,1,0:T(8,128)(2,1)S(1)}, bf16[2,4,64,1536]{3,2,1,0:T(8,128)(2,1)S(1)}, u32[]{:S(2)}, u32[]{:S(2)}) collective-permute-start(bf16[2,4,64,1536]{3,2,1,0:T(8,128)(2,1)S(1)} %get-tuple-element.34.refs_2_), channel_id=1, source_target_pairs={{0,1},{1,0},{2,3},{3,2},{4,5},{5,4},{6,7},{7,6},{8,9},{9,8},{10,11... | collective-permute-start | bytes 4718600 | tf_op jit(solution)/shard_map/ppermute | solution.py:385
  68.4 4.5 %collective-permute-start.10 = (bf16[3,2,64,1536]{3,2,1,0:T(8,128)(2,1)S(1)}, bf16[3,2,64,1536]{3,2,1,0:T(8,128)(2,1)S(1)}, u32[]{:S(2)}, u32[]{:S(2)}) collective-permute-start(bf16[3,2,64,1536]{3,2,1,0:T(8,128)(2,1)S(1)} %shard_map.106), channel_id=1, source_target_pairs={{0,1},{1,0},{2,3},{3,2},{4,5},{5,4},{6,7},{7,6},{8,9},{9,8},{10,11... | collective-permute-start | bytes 3538952 | tf_op jit(solution)/shard_map/ppermute | solution.py:385
  69.0 34.5 %collective-permute-start.9 = (bf16[2,64,1536]{2,1,0:T(8,128)(2,1)S(1)}, bf16[2,64,1536]{2,1,0:T(8,128)(2,1)S(1)}, u32[]{:S(2)}, u32[]{:S(2)}) collective-permute-start(bf16[2,64,1536]{2,1,0:T(8,128)(2,1)S(1)} %get-tuple-element.35), channel_id=1, source_target_pairs={{0,8},{8,0},{16,24},{24,16},{1,9},{9,1},{17,25},{25,17},{2,10},{10... | collective-permute-start | bytes 1179656 | tf_op jit(solution)/shard_map/ppermute | solution.py:388
  69.8 33.7 %collective-permute-start.11 = (bf16[2,64,1536]{2,1,0:T(8,128)(2,1)S(1)}, bf16[2,64,1536]{2,1,0:T(8,128)(2,1)S(1)}, u32[]{:S(2)}, u32[]{:S(2)}) collective-permute-start(bf16[2,64,1536]{2,1,0:T(8,128)(2,1)S(1)} %get-tuple-element.36), channel_id=1, source_target_pairs={{0,16},{8,24},{16,0},{24,8},{1,17},{9,25},{17,1},{25,9},{2,18},{10... | collective-permute-start | bytes 1179656 | tf_op jit(solution)/shard_map/ppermute | solution.py:388
  71.3 32.1 %collective-permute-start.12 = (bf16[2,64,1536]{2,1,0:T(8,128)(2,1)S(1)}, bf16[2,64,1536]{2,1,0:T(8,128)(2,1)S(1)}, u32[]{:S(2)}, u32[]{:S(2)}) collective-permute-start(bf16[2,64,1536]{2,1,0:T(8,128)(2,1)S(1)} %get-tuple-element.37), channel_id=1, source_target_pairs={{0,24},{8,16},{16,8},{24,0},{1,25},{9,17},{17,9},{25,1},{2,26},{10... | collective-permute-start | bytes 1179656 | tf_op jit(solution)/shard_map/ppermute | solution.py:388
  72.9 1.1 copy-start.21
  101.0 3.1 %copy-start.18 = (bf16[256,3072]{1,0:T(8,128)(2,1)}, bf16[256,3072]{1,0:T(8,128)(2,1)S(1)}, u32[]{:S(2)}) copy-start(bf16[256,3072]{1,0:T(8,128)(2,1)S(1)} %get-tuple-element.39.refs_14_) | copy-start | bytes 4718596
  101.0 36.5 %collective-permute-start.14 = (bf16[256,3072]{1,0:T(8,128)(2,1)S(1)}, bf16[256,3072]{1,0:T(8,128)(2,1)S(1)}, u32[]{:S(2)}, u32[]{:S(2)}) collective-permute-start(bf16[256,3072]{1,0:T(8,128)(2,1)S(1)} %get-tuple-element.39.refs_14_), channel_id=1, source_target_pairs={{0,8},{8,0},{16,24},{24,16},{1,9},{9,1},{17,25},{25,17},{2,10},{10... | collective-permute-start | bytes 4718600 | tf_op jit(solution)/shard_map/ppermute | solution.py:388
  101.9 37.3 %collective-permute-start.17 = (bf16[256,3072]{1,0:T(8,128)(2,1)S(1)}, bf16[256,3072]{1,0:T(8,128)(2,1)S(1)}, u32[]{:S(2)}, u32[]{:S(2)}) collective-permute-start(bf16[256,3072]{1,0:T(8,128)(2,1)S(1)} %get-tuple-element.39.refs_14_), channel_id=1, source_target_pairs={{0,16},{8,24},{16,0},{24,8},{1,17},{9,25},{17,1},{25,9},{2,18},{10... | collective-permute-start | bytes 4718600 | tf_op jit(solution)/shard_map/ppermute | solution.py:388
  103.4 0.7 copy-start.9
  103.4 0.9 copy-start.10
  103.5 1.0 copy-start.2
  104.1 5.2 %collective-permute-start.13 = (bf16[3,2,64,1536]{3,2,1,0:T(8,128)(2,1)S(1)}, bf16[3,2,64,1536]{3,2,1,0:T(8,128)(2,1)S(1)}, u32[]{:S(2)}, u32[]{:S(2)}) collective-permute-start(bf16[3,2,64,1536]{3,2,1,0:T(8,128)(2,1)S(1)} %shard_map.108), channel_id=1, source_target_pairs={{0,1},{1,0},{2,3},{3,2},{4,5},{5,4},{6,7},{7,6},{8,9},{9,8},{10,11... | collective-permute-start | bytes 3538952 | tf_op jit(solution)/shard_map/ppermute | solution.py:385
  104.5 4.8 %copy-start.8 = (bf16[128,6144]{1,0:T(8,128)(2,1)S(1)}, bf16[128,6144]{1,0:T(8,128)(2,1)}, u32[]{:S(2)}) copy-start(bf16[128,6144]{1,0:T(8,128)(2,1)} %get-tuple-element.40.mine) | copy-start | bytes 4718596
  104.5 3.6 %collective-permute-start.15 = (bf16[128,3072]{1,0:T(8,128)(2,1)S(1)}, bf16[128,3072]{1,0:T(8,128)(2,1)S(1)}, u32[]{:S(2)}, u32[]{:S(2)}) collective-permute-start(bf16[128,3072]{1,0:T(8,128)(2,1)S(1)} %shard_map.109), channel_id=1, source_target_pairs={{0,1},{1,0},{2,3},{3,2},{4,5},{5,4},{6,7},{7,6},{8,9},{9,8},{10,11... | collective-permute-start | bytes 2359304 | tf_op jit(solution)/shard_map/ppermute | solution.py:385
  104.8 4.5 %collective-permute-start.16 = (bf16[128,3072]{1,0:T(8,128)(2,1)S(1)}, bf16[128,3072]{1,0:T(8,128)(2,1)S(1)}, u32[]{:S(2)}, u32[]{:S(2)}) collective-permute-start(bf16[128,3072]{1,0:T(8,128)(2,1)S(1)} %get-tuple-element.41), channel_id=1, source_target_pairs={{0,1},{1,0},{2,3},{3,2},{4,5},{5,4},{6,7},{7,6},{8,9},{9,8},{10,11... | collective-permute-start | bytes 2359304 | tf_op jit(solution)/shard_map/ppermute | solution.py:385
  109.6 46.4 %collective-permute-start.18 = (bf16[32,6144]{1,0:T(8,128)(2,1)S(1)}, bf16[32,6144]{1,0:T(8,128)(2,1)S(1)}, u32[]{:S(2)}, u32[]{:S(2)}) collective-permute-start(bf16[32,6144]{1,0:T(8,128)(2,1)S(1)} %get-tuple-element.44), channel_id=1, source_target_pairs={{0,6},{1,7},{2,0},{3,1},{4,2},{5,3},{6,4},{7,5},{8,14},{9,15},{10,... | collective-permute-start | bytes 1179656 | tf_op jit(solution)/shard_map/ppermute | solution.py:382
  111.4 44.6 %collective-permute-start.19 = (bf16[32,6144]{1,0:T(8,128)(2,1)S(1)}, bf16[32,6144]{1,0:T(8,128)(2,1)S(1)}, u32[]{:S(2)}, u32[]{:S(2)}) collective-permute-start(bf16[32,6144]{1,0:T(8,128)(2,1)S(1)} %get-tuple-element.45), channel_id=1, source_target_pairs={{0,2},{1,3},{2,4},{3,5},{4,6},{5,7},{6,0},{7,1},{8,10},{9,11},{10,... | collective-permute-start | bytes 1179656 | tf_op jit(solution)/shard_map/ppermute | solution.py:382
  111.7 44.3 %collective-permute-start.20 = (bf16[32,6144]{1,0:T(8,128)(2,1)S(1)}, bf16[32,6144]{1,0:T(8,128)(2,1)S(1)}, u32[]{:S(2)}, u32[]{:S(2)}) collective-permute-start(bf16[32,6144]{1,0:T(8,128)(2,1)S(1)} %get-tuple-element.46), channel_id=1, source_target_pairs={{0,4},{1,5},{2,6},{3,7},{4,0},{5,1},{6,2},{7,3},{8,12},{9,13},{10,... | collective-permute-start | bytes 1179656 | tf_op jit(solution)/shard_map/ppermute | solution.py:382
  137.5 1.7 copy-start.4
  137.6 22.1 %collective-permute-start.21 = (bf16[128,3072]{1,0:T(8,128)(2,1)S(1)}, bf16[128,3072]{1,0:T(8,128)(2,1)S(1)}, u32[]{:S(2)}, u32[]{:S(2)}) collective-permute-start(bf16[128,3072]{1,0:T(8,128)(2,1)S(1)} %slice.38), channel_id=1, source_target_pairs={{0,16},{8,24},{16,0},{24,8},{1,17},{9,25},{17,1},{25,9},{2,18},{10... | collective-permute-start | bytes 2359304 | tf_op jit(solution)/shard_map/ppermute | solution.py:388
  139.2 2.0 %copy-start.3 = (bf16[256,3072]{1,0:T(8,128)(2,1)}, bf16[256,3072]{1,0:T(8,128)(2,1)S(1)}, u32[]{:S(2)}) copy-start(bf16[256,3072]{1,0:T(8,128)(2,1)S(1)} %shard_map.112.refs_16_) | copy-start | bytes 4718596
  139.3 20.4 %collective-permute-start.22 = (bf16[128,3072]{1,0:T(8,128)(2,1)S(1)}, bf16[128,3072]{1,0:T(8,128)(2,1)S(1)}, u32[]{:S(2)}, u32[]{:S(2)}) collective-permute-start(bf16[128,3072]{1,0:T(8,128)(2,1)S(1)} %slice.39), channel_id=1, source_target_pairs={{0,8},{8,0},{16,24},{24,16},{1,9},{9,1},{17,25},{25,17},{2,10},{10... | collective-permute-start | bytes 2359304 | tf_op jit(solution)/shard_map/ppermute | solution.py:388
  141.2 14.8 %copy-start.16 = (bf16[32,128]{1,0:T(8,128)(2,1)S(1)}, bf16[32,128]{1,0:T(8,128)(2,1)}, u32[]{:S(2)}) copy-start(bf16[32,128]{1,0:T(8,128)(2,1)} %get-tuple-element.28.sel) | copy-start | bytes 24580
  156.0 1.9 %copy-start = (bf16[1024,1536]{1,0:T(8,128)(2,1)S(1)}, bf16[1024,1536]{1,0:T(8,128)(2,1)}, u32[]{:S(2)}) copy-start(bf16[1024,1536]{1,0:T(8,128)(2,1)} %get-tuple-element.43._.refs_8_) | copy-start | bytes 9437188
  159.7 0.9 copy-start.19
  159.7 1.1 copy-start.20

commit v4 on v3

--- a/solution.py
+++ b/solution.py
@@ -195,7 +195,7 @@
                 pltpu.make_async_copy(w.at[span], wide.at[j, span], wide_sem.at[slot, j]) for j, w in enumerate((gw, uw))
             ])
     back = Stream([
-        [pltpu.make_async_copy(dw.at[pl.ds(i * piece, piece)], tall.at[i % 3], tall_sem.at[i % 3])]
+        [pltpu.make_async_copy(dw.at[pl.ds(i * piece, piece)], tall.at[i % 2], tall_sem.at[i % 2])]
         for i in range(ff // piece)
     ])
     forth = Stream(forth)
@@ -222,10 +222,10 @@
         at = i * piece
         cols = slice(at, at + piece)
         back.take(i)
-        back.start(i + 3)
-        grad = mm(rows[...], tall[i % 3], LAST)
+        grad = mm(rows[...], tall[i % 2], LAST)
         out[:, ff + at : ff + at + piece] = (grad * up[:, cols]).astype(BF16)
         out[:, 2 * ff + at : 2 * ff + at + piece] = (grad * gate[:, cols]).astype(BF16)
+        back.start(i + 3)
     d = wide.shape[1]
     tile = 512
     for i in range(d // tile):
@@ -267,11 +267,11 @@
             pltpu.VMEM((rows, ff), F32),
             pltpu.VMEM((rows, ff), F32),
             pltpu.VMEM((2, d, ff), BF16),
-            pltpu.VMEM((3, 256, d), BF16),
+            pltpu.VMEM((2, 256, d), BF16),
             pltpu.SemaphoreType.DMA((4, 2)),
-            pltpu.SemaphoreType.DMA((3,)),
+            pltpu.SemaphoreType.DMA((2,)),
         ],
-        compiler_params=params(46 << 20),
+        compiler_params=params(42 << 20),
         cost_estimate=cost(10 * rows * gw.size, 6 * gw.size, 1),
     )(me, *parts, gw, uw, dw, dep)
 
@@ -324,7 +324,8 @@
     slices, refs = refs[:n_slices], refs[n_slices:]
     grads, refs = refs[:n_grads], refs[n_grads:]
     totals, refs = refs[:n_totals], refs[n_totals:]
-    outs, (picked, scaled, rows) = refs[:3], refs[3:]
+    outs, mark, (picked, scaled, rows) = refs[:3], refs[3], refs[4:]
+    mark[...] = jnp.zeros(mark.shape, F32)
 
     @pl.when(pl.program_id(0) == 0)
     def _():
@@ -358,16 +359,18 @@
     rows = sum(b.shape[0] for b in grads)
     width, ff = slices[0].shape[-1], grads[0].shape[1] // 3
     tile = tile if width % tile == 0 else 256
+    outs = (shape((width, ff)), shape((width, ff)), shape((ff, width)))
+    held = 2 * rows * (2 * width + 3 * ff)
     tall = pl.BlockSpec((tile, ff), lambda i: (i, 0))
     wide = pl.BlockSpec((ff, tile), lambda i: (0, i))
     return pl.pallas_call(
         functools.partial(contract_kernel, len(slices), len(grads), len(totals)),
-        out_shape=(shape((width, ff)), shape((width, ff)), shape((ff, width))),
+        out_shape=(list(outs) if totals else [pltpu.VMEM(o.shape, o.dtype) for o in outs]) + [shape((8, 128), F32)],
         grid=(width // tile,),
         in_specs=[VMEM] * (len(slices) + len(grads)) + [tall, tall, wide][: len(totals)],
-        out_specs=(tall, tall, wide),
+        out_specs=[tall, tall, wide, pl.BlockSpec((8, 128), lambda i: (0, 0))],
         scratch_shapes=[pltpu.VMEM((rows, width), BF16)] * 2 + [pltpu.VMEM((rows, 3 * ff), BF16)],
-        compiler_params=params(56 << 20),
+        compiler_params=params((42 if held < 16 << 20 else 56) << 20),
         cost_estimate=cost(6 * rows * width * ff, 2 * rows * (2 * width + 3 * ff) + 12 * width * ff, 1),
     )(*slices, *grads, *totals)
 
@@ -421,9 +424,9 @@
     else:
         got = [across(rows, k) for k in range(1, n_dp)]
         first, last = [rows] + got[:-1], got[-1:]
-    totals = contract(sum(slices[:-1], []), first, [])
-    gate_grad, up_grad, down_grad = contract(slices[-1], last, totals)
-    token_grad = put(sel, [[summed] + [move(x, o) for x, o in zip(others, offsets[1:])]], totals[2])
+    *totals, mark = contract(sum(slices[:-1], []), first, [])
+    gate_grad, up_grad, down_grad, _ = contract(slices[-1], last, totals)
+    token_grad = put(sel, [[summed] + [move(x, o) for x, o in zip(others, offsets[1:])]], mark)
     return token_grad, gate_grad, up_grad, down_grad
 
 

time: 172 us -> 162 us (0.942)
  Pallas kernels: 61.6 us -> 54.4 us
  local copies, waits for them, and re-layouts: 8.12 us -> 2.5 us
  waiting for transfers between devices: 77.3 us -> 80 us
    pallas_call x2, Pallas kernels: 25.3 us -> 20.1 us  [contract(): pl.pallas_call(functools.partial(contract_kernel, len(slices), len(grads)...]
    unnamed x44 -> x26, local copies, waits for them, and re-layouts: 5.94 us -> 1.47 us
    pallas_call x1, Pallas kernels: 26.9 us -> 24.6 us  [slab(): pl.pallas_call(kernel, out_shape=(shape((rows, 3 * ff)), shape((rows // 2...]
  transfers between devices with their start and end apart: 23 -> 23, of which waited for: 8 -> 10; matrix products, arithmetic and copies ran while one was open for 1% -> 1% of each run, Pallas kernels for 26% -> 26%
where the time goes in v4:
time: 162 us; the launch traced here: 161 us
  waiting for transfers between devices  80 us (49%)
  Pallas kernels  54.4 us (34%)
  starting transfers between devices  23.5 us (15%)
  local copies, waits for them, and re-layouts  2.5 us (2%)
    ppermute x10, waiting for transfers between devices, across(): return lax.ppermute(x, 'dp', [(k, k ^ bits) for k in range(n_dp)])  42.2 us
    ppermute x6, waiting for transfers between devices, move(): return lax.ppermute(x, 'fetch', pairs)  32.9 us
    pallas_call x1, Pallas kernels, slab(): pl.pallas_call(kernel, out_shape=(shape((rows, 3 * ff)), shape((rows // 2...  24.6 us
    pallas_call x2, Pallas kernels, contract(): pl.pallas_call(functools.partial(contract_kernel, len(slices), len(grads)...  20.1 us
    ppermute x10, starting transfers between devices, across(): return lax.ppermute(x, 'dp', [(k, k ^ bits) for k in range(n_dp)])  13.6 us
    ppermute x6, starting transfers between devices, move(): return lax.ppermute(x, 'fetch', pairs)  8.54 us
    ppermute x7, waiting for transfers between devices, swap(): return lax.ppermute(x, 'fetch', [(k, k ^ 1) for k in range(n_fetch)])  4.87 us
    pallas_call x1, Pallas kernels, pick(): pl.pallas_call(pick_kernel, out_shape=(shape((CAP, n)),) + (shape((2, n_d...  4.3 us
  transfers between devices with their start and end apart: 23, of which 10 were waited for; matrix products, arithmetic and copies ran while one was open for 1% of the time, Pallas kernels for 26%

profile of v4, /device:TPU:0, one launch (start us, length us, event | category | flops | bytes accessed | tf_op | source)
XLA Modules:
  0.0 161.2 jit_solution(3211921457865855742)
XLA Ops:
  0.6 4.3 %shard_map.102 = (bf16[32,128]{1,0:T(8,128)(2,1)}, bf16[2,4,32,1536]{3,2,1,0:T(8,128)(2,1)}, bf16[2,4,32,1536]{3,2,1,0:T(8,128)(2,1)}) custom-call(s32[1]{0:T(128)} %bitcast.me, s32[2,128]{1,0:T(2,128)} %bitcast.15, f32[2,128]{1,0:T(2,128)} %bitcast.16, bf16[128,6144]{1,0:T(8,128)(2,1)} %tokens.1, bf16[128,6144]{1,0:T(8,128)(2,1)} %out_grad.1), custom_call_target="tpu_custom_call" | custom-call | flops 1572864 | bytes 61440 | tf_op jit(solution)/shard_map/pallas_call | solution.py:74
  4.9 3.1 %collective-permute-start = (bf16[2,4,32,1536]{3,2,1,0:T(8,128)(2,1)}, bf16[2,4,32,1536]{3,2,1,0:T(8,128)(2,1)S(1)}, u32[]{:S(2)}, u32[]{:S(2)}) collective-permute-start(bf16[2,4,32,1536]{3,2,1,0:T(8,128)(2,1)} %get-tuple-element.30.refs_0_), channel_id=1, source_target_pairs={{0,2},{1,3},{2,4},{3,5},{4,6},{5,7},{6,0},{7,1},{8,10},{9,11},{10,... | collective-permute-start | bytes 2359304 | tf_op jit(solution)/shard_map/ppermute | solution.py:385
  8.0 19.8 %collective-permute-done.refs_1_ = bf16[2,4,32,1536]{3,2,1,0:T(8,128)(2,1)S(1)} collective-permute-done((bf16[2,4,32,1536]{3,2,1,0:T(8,128)(2,1)}, bf16[2,4,32,1536]{3,2,1,0:T(8,128)(2,1)S(1)}, u32[]{:S(2)}, u32[]{:S(2)}) %collective-permute-start) | collective-permute-done | bytes 786464 | tf_op jit(solution)/shard_map/ppermute | solution.py:385
  27.8 1.4 copy-done.5
  29.2 0.8 shard_map.104
  30.0 1.6 collective-permute-start.4
  31.6 1.7 %collective-permute-start.1 = (bf16[2,4,32,1536]{3,2,1,0:T(8,128)(2,1)S(1)}, bf16[2,4,32,1536]{3,2,1,0:T(8,128)(2,1)S(1)}, u32[]{:S(2)}, u32[]{:S(2)}) collective-permute-start(bf16[2,4,32,1536]{3,2,1,0:T(8,128)(2,1)S(1)} %shard_map.103), channel_id=1, source_target_pairs={{0,6},{1,7},{2,0},{3,1},{4,2},{5,3},{6,4},{7,5},{8,14},{9,15},{10,... | collective-permute-start | bytes 2359304 | tf_op jit(solution)/shard_map/ppermute | solution.py:385
  33.3 0.3 collective-permute-start.2
  33.6 1.5 collective-permute-start.5
  35.2 5.3 %collective-permute-done.4.refs_2_.refs_0_.refs_6_ = bf16[2,64,1536]{2,1,0:T(8,128)(2,1)S(1)} collective-permute-done((bf16[2,64,1536]{2,1,0:T(8,128)(2,1)S(1)}, bf16[2,64,1536]{2,1,0:T(8,128)(2,1)S(1)}, u32[]{:S(2)}, u32[]{:S(2)}) %collective-permute-start.4) | collective-permute-done | bytes 393248 | tf_op jit(solution)/shard_map/ppermute | solution.py:391
  40.4 2.2 %collective-permute-start.6 = (bf16[2,64,1536]{2,1,0:T(8,128)(2,1)S(1)}, bf16[2,64,1536]{2,1,0:T(8,128)(2,1)S(1)}, u32[]{:S(2)}, u32[]{:S(2)}) collective-permute-start(bf16[2,64,1536]{2,1,0:T(8,128)(2,1)S(1)} %get-tuple-element.34), channel_id=1, source_target_pairs={{0,24},{8,16},{16,8},{24,0},{1,25},{9,17},{17,9},{25,1},{2,26},{10... | collective-permute-start | bytes 1179656 | tf_op jit(solution)/shard_map/ppermute | solution.py:391
  42.6 11.0 %collective-permute-done.5.refs_3_.refs_1_.refs_10_ = bf16[2,64,1536]{2,1,0:T(8,128)(2,1)S(1)} collective-permute-done((bf16[2,64,1536]{2,1,0:T(8,128)(2,1)S(1)}, bf16[2,64,1536]{2,1,0:T(8,128)(2,1)S(1)}, u32[]{:S(2)}, u32[]{:S(2)}) %collective-permute-start.5) | collective-permute-done | bytes 393248 | tf_op jit(solution)/shard_map/ppermute | solution.py:391
  53.6 13.2 %collective-permute-done.2.refs_1_ = bf16[2,4,32,1536]{3,2,1,0:T(8,128)(2,1)S(1)} collective-permute-done((bf16[2,4,32,1536]{3,2,1,0:T(8,128)(2,1)S(1)}, bf16[2,4,32,1536]{3,2,1,0:T(8,128)(2,1)S(1)}, u32[]{:S(2)}, u32[]{:S(2)}) %collective-permute-start.2) | collective-permute-done | bytes 786464 | tf_op jit(solution)/shard_map/ppermute | solution.py:385
  66.8 0.9 shard_map.105
  67.7 0.0 copy-start.10
  67.7 0.1 collective-permute-start.8
  67.8 0.6 shard_map.106
  68.4 0.6 collective-permute-start.10
  69.0 0.8 collective-permute-start.9
  69.8 1.5 collective-permute-start.11
  71.3 1.2 collective-permute-start.12
  72.5 0.4 collective-permute-done.10.refs_9_
  72.9 24.6 %shard_map.107 = (bf16[256,3072]{1,0:T(8,128)(2,1)S(1)}, bf16[128,6144]{1,0:T(8,128)(2,1)S(1)}, bf16[128,3072]{1,0:T(8,128)(2,1)S(1)}, bf16[128,3072]{1,0:T(8,128)(2,1)S(1)}) custom-call(s32[1]{0:T(128)} %bitcast.me, bf16[2,4,32,1536]{3,2,1,0:T(8,128)(2,1)S(1)} %copy-done.6, bf16[2,4,32,1536]{3,2,1,0:T(8,128)(2,1)S(1)} %collective-permute-done.refs_1_, ...), custom_call_target="tpu_custom_call" | custom-call | flops 16106127360 | bytes 37748736 | tf_op jit(solution)/shard_map/pallas_call | solution.py:255
  97.5 0.0 copy-start.12
  97.6 0.9 collective-permute-start.14
  98.4 1.5 collective-permute-start.17
  100.0 0.6 shard_map.108
  100.6 0.1 collective-permute-start.13
  100.7 0.5 collective-permute-start.15
  101.2 0.1 collective-permute-start.16
  101.3 0.1 slice_bitcast_fusion.1
  101.3 3.3 %collective-permute-done.15.left = bf16[128,3072]{1,0:T(8,128)(2,1)S(1)} collective-permute-done((bf16[128,3072]{1,0:T(8,128)(2,1)S(1)}, bf16[128,3072]{1,0:T(8,128)(2,1)S(1)}, u32[]{:S(2)}, u32[]{:S(2)}) %collective-permute-start.15) | collective-permute-done | bytes 786464 | tf_op jit(solution)/shard_map/ppermute | solution.py:388
  104.6 1.1 collective-permute-done.16.right
  105.8 0.4 shard_map.110
  106.1 1.8 %collective-permute-start.18 = (bf16[32,6144]{1,0:T(8,128)(2,1)S(1)}, bf16[32,6144]{1,0:T(8,128)(2,1)S(1)}, u32[]{:S(2)}, u32[]{:S(2)}) collective-permute-start(bf16[32,6144]{1,0:T(8,128)(2,1)S(1)} %get-tuple-element.45), channel_id=1, source_target_pairs={{0,6},{1,7},{2,0},{3,1},{4,2},{5,3},{6,4},{7,5},{8,14},{9,15},{10,... | collective-permute-start | bytes 1179656 | tf_op jit(solution)/shard_map/ppermute | solution.py:385
  107.9 0.3 collective-permute-start.19
  108.2 1.4 collective-permute-start.20
  109.6 24.5 %collective-permute-done.14.refs_0_ = bf16[256,3072]{1,0:T(8,128)(2,1)S(1)} collective-permute-done((bf16[256,3072]{1,0:T(8,128)(2,1)S(1)}, bf16[256,3072]{1,0:T(8,128)(2,1)S(1)}, u32[]{:S(2)}, u32[]{:S(2)}) %collective-permute-start.14) | collective-permute-done | bytes 1572896 | tf_op jit(solution)/shard_map/ppermute | solution.py:391
  134.1 0.1 slice.38
  134.1 1.6 collective-permute-start.21
  135.7 0.1 slice.39
  135.8 0.9 collective-permute-start.22
  136.6 0.8 slice_bitcast_fusion
  137.5 13.1 %shard_map.113 = (bf16[1536,1024]{1,0:T(8,128)(2,1)S(1)}, bf16[1536,1024]{1,0:T(8,128)(2,1)S(1)}, bf16[1024,1536]{1,0:T(8,128)(2,1)S(1)}, f32[8,128]{1,0:T(8,128)S(1)}) custom-call(bf16[2,4,32,1536]{3,2,1,0:T(8,128)(2,1)} %get-tuple-element.30.refs_0_, bf16[2,4,32,1536]{3,2,1,0:T(8,128)(2,1)} %copy-done.3, bf16[2,4,64,1536]{3,2,1,0:T(8,128)(2,1)} %copy-done.10, ...), custom_call_target="tpu_custom_call" | custom-call | flops 7247757312 | bytes 28311552 | tf_op jit(solution)/shard_map/pallas_call | solution.py:366
  150.7 2.1 %shard_map.114 = bf16[128,6144]{1,0:T(8,128)(2,1)} custom-call(bf16[32,128]{1,0:T(8,128)(2,1)S(1)} %copy-done.9, f32[8,128]{1,0:T(8,128)S(1)} %get-tuple-element.44._, bf16[32,6144]{1,0:T(8,128)(2,1)S(1)} %get-tuple-element.43.refs_1_.refs_0_, bf16[32,6144]{1,0:T(8,128)(2,1)S(1)} %collective-permute-done.18.refs_1_, ...), custom_call_target="tpu_custom_call" | custom-call | flops 786432 | bytes 1572864 | tf_op jit(solution)/shard_map/pallas_call | solution.py:313
  152.8 0.1 collective-permute-done.21.refs_4_
  152.9 1.4 collective-permute-done.22.refs_5_
  154.3 6.9 %shard_map.115 = (bf16[1536,1024]{1,0:T(8,128)(2,1)}, bf16[1536,1024]{1,0:T(8,128)(2,1)}, bf16[1024,1536]{1,0:T(8,128)(2,1)}, f32[8,128]{1,0:T(8,128)}) custom-call(bf16[2,64,1536]{2,1,0:T(8,128)(2,1)S(1)} %collective-permute-done.6.refs_4_.refs_2_.refs_0_, bf16[2,64,1536]{2,1,0:T(8,128)(2,1)S(1)} %collective-permute-done.12.refs_2_.refs_3_.refs_1_, ...), custom_call_target="tpu_custom_call" | custom-call | flops 2415919104 | bytes 22020096 | tf_op jit(solution)/shard_map/pallas_call | solution.py:366
  (42 shorter events, 0.1 us)
Async XLA Ops:
  4.9 22.8 %collective-permute-start = (bf16[2,4,32,1536]{3,2,1,0:T(8,128)(2,1)}, bf16[2,4,32,1536]{3,2,1,0:T(8,128)(2,1)S(1)}, u32[]{:S(2)}, u32[]{:S(2)}) collective-permute-start(bf16[2,4,32,1536]{3,2,1,0:T(8,128)(2,1)} %get-tuple-element.30.refs_0_), channel_id=1, source_target_pairs={{0,2},{1,3},{2,4},{3,5},{4,6},{5,7},{6,0},{7,1},{8,10},{9,11},{10,... | collective-permute-start | bytes 2359304 | tf_op jit(solution)/shard_map/ppermute | solution.py:385
  8.0 19.8 %collective-permute-start.3 = (bf16[2,4,32,1536]{3,2,1,0:T(8,128)(2,1)}, bf16[2,4,32,1536]{3,2,1,0:T(8,128)(2,1)S(1)}, u32[]{:S(2)}, u32[]{:S(2)}) collective-permute-start(bf16[2,4,32,1536]{3,2,1,0:T(8,128)(2,1)} %get-tuple-element.30.refs_0_), channel_id=1, source_target_pairs={{0,1},{1,0},{2,3},{3,2},{4,5},{5,4},{6,7},{7,6},{8,9},{9,8},{10,11... | collective-permute-start | bytes 2359304 | tf_op jit(solution)/shard_map/ppermute | solution.py:388
  27.8 45.1 %copy-start.3 = (bf16[2,4,32,1536]{3,2,1,0:T(8,128)(2,1)}, bf16[2,4,32,1536]{3,2,1,0:T(8,128)(2,1)S(1)}, u32[]{:S(2)}) copy-start(bf16[2,4,32,1536]{3,2,1,0:T(8,128)(2,1)S(1)} %collective-permute-done.refs_1_) | copy-start | bytes 2359300
  27.8 1.4 copy-start.5
  29.2 43.7 %copy-start.7 = (bf16[2,4,32,1536]{3,2,1,0:T(8,128)(2,1)}, bf16[2,4,32,1536]{3,2,1,0:T(8,128)(2,1)S(1)}, u32[]{:S(2)}) copy-start(bf16[2,4,32,1536]{3,2,1,0:T(8,128)(2,1)S(1)} %collective-permute-done.3.refs_2_.refs_3_) | copy-start | bytes 2359300
  29.2 2.4 %copy-start.8 = (bf16[2,4,32,1536]{3,2,1,0:T(8,128)(2,1)S(1)}, bf16[2,4,32,1536]{3,2,1,0:T(8,128)(2,1)}, u32[]{:S(2)}) copy-start(bf16[2,4,32,1536]{3,2,1,0:T(8,128)(2,1)} %get-tuple-element.31.refs_0_) | copy-start | bytes 2359300
  30.0 10.4 %collective-permute-start.4 = (bf16[2,64,1536]{2,1,0:T(8,128)(2,1)S(1)}, bf16[2,64,1536]{2,1,0:T(8,128)(2,1)S(1)}, u32[]{:S(2)}, u32[]{:S(2)}) collective-permute-start(bf16[2,64,1536]{2,1,0:T(8,128)(2,1)S(1)} %get-tuple-element.32), channel_id=1, source_target_pairs={{0,8},{8,0},{16,24},{24,16},{1,9},{9,1},{17,25},{25,17},{2,10},{10... | collective-permute-start | bytes 1179656 | tf_op jit(solution)/shard_map/ppermute | solution.py:391
  31.6 22.0 %collective-permute-start.1 = (bf16[2,4,32,1536]{3,2,1,0:T(8,128)(2,1)S(1)}, bf16[2,4,32,1536]{3,2,1,0:T(8,128)(2,1)S(1)}, u32[]{:S(2)}, u32[]{:S(2)}) collective-permute-start(bf16[2,4,32,1536]{3,2,1,0:T(8,128)(2,1)S(1)} %shard_map.103), channel_id=1, source_target_pairs={{0,6},{1,7},{2,0},{3,1},{4,2},{5,3},{6,4},{7,5},{8,14},{9,15},{10,... | collective-permute-start | bytes 2359304 | tf_op jit(solution)/shard_map/ppermute | solution.py:385
  33.3 33.4 %collective-permute-start.2 = (bf16[2,4,32,1536]{3,2,1,0:T(8,128)(2,1)S(1)}, bf16[2,4,32,1536]{3,2,1,0:T(8,128)(2,1)S(1)}, u32[]{:S(2)}, u32[]{:S(2)}) collective-permute-start(bf16[2,4,32,1536]{3,2,1,0:T(8,128)(2,1)S(1)} %collective-permute-done.refs_1_), channel_id=1, source_target_pairs={{0,2},{1,3},{2,4},{3,5},{4,6},{5,7},{6,0},{7,1},{8,10},{9,11},{10,... | collective-permute-start | bytes 2359304 | tf_op jit(solution)/shard_map/ppermute | solution.py:385
  33.6 33.1 %collective-permute-start.7 = (bf16[2,4,32,1536]{3,2,1,0:T(8,128)(2,1)S(1)}, bf16[2,4,32,1536]{3,2,1,0:T(8,128)(2,1)S(1)}, u32[]{:S(2)}, u32[]{:S(2)}) collective-permute-start(bf16[2,4,32,1536]{3,2,1,0:T(8,128)(2,1)S(1)} %collective-permute-done.refs_1_), channel_id=1, source_target_pairs={{0,1},{1,0},{2,3},{3,2},{4,5},{5,4},{6,7},{7,6},{8,9},{9,8},{10,11... | collective-permute-start | bytes 2359304 | tf_op jit(solution)/shard_map/ppermute | solution.py:388
  33.6 20.0 %collective-permute-start.5 = (bf16[2,64,1536]{2,1,0:T(8,128)(2,1)S(1)}, bf16[2,64,1536]{2,1,0:T(8,128)(2,1)S(1)}, u32[]{:S(2)}, u32[]{:S(2)}) collective-permute-start(bf16[2,64,1536]{2,1,0:T(8,128)(2,1)S(1)} %get-tuple-element.33), channel_id=1, source_target_pairs={{0,16},{8,24},{16,0},{24,8},{1,17},{9,25},{17,1},{25,9},{2,18},{10... | collective-permute-start | bytes 1179656 | tf_op jit(solution)/shard_map/ppermute | solution.py:391
  40.4 13.2 %collective-permute-start.6 = (bf16[2,64,1536]{2,1,0:T(8,128)(2,1)S(1)}, bf16[2,64,1536]{2,1,0:T(8,128)(2,1)S(1)}, u32[]{:S(2)}, u32[]{:S(2)}) collective-permute-start(bf16[2,64,1536]{2,1,0:T(8,128)(2,1)S(1)} %get-tuple-element.34), channel_id=1, source_target_pairs={{0,24},{8,16},{16,8},{24,0},{1,25},{9,17},{17,9},{25,1},{2,26},{10... | collective-permute-start | bytes 1179656 | tf_op jit(solution)/shard_map/ppermute | solution.py:391
  66.8 6.2 %copy-start.4 = (bf16[2,4,32,1536]{3,2,1,0:T(8,128)(2,1)}, bf16[2,4,32,1536]{3,2,1,0:T(8,128)(2,1)S(1)}, u32[]{:S(2)}) copy-start(bf16[2,4,32,1536]{3,2,1,0:T(8,128)(2,1)S(1)} %collective-permute-done.7.refs_5_.refs_4_) | copy-start | bytes 2359300
  67.7 29.8 %copy-start.10 = (bf16[2,4,64,1536]{3,2,1,0:T(8,128)(2,1)}, bf16[2,4,64,1536]{3,2,1,0:T(8,128)(2,1)S(1)}, u32[]{:S(2)}) copy-start(bf16[2,4,64,1536]{3,2,1,0:T(8,128)(2,1)S(1)} %get-tuple-element.35.refs_2_) | copy-start | bytes 4718596
  67.7 5.2 %copy-start.6 = (bf16[2,4,32,1536]{3,2,1,0:T(8,128)(2,1)S(1)}, bf16[2,4,32,1536]{3,2,1,0:T(8,128)(2,1)}, u32[]{:S(2)}) copy-start(bf16[2,4,32,1536]{3,2,1,0:T(8,128)(2,1)} %get-tuple-element.30.refs_0_) | copy-start | bytes 2359300
  67.7 5.2 %collective-permute-start.8 = (bf16[2,4,64,1536]{3,2,1,0:T(8,128)(2,1)S(1)}, bf16[2,4,64,1536]{3,2,1,0:T(8,128)(2,1)S(1)}, u32[]{:S(2)}, u32[]{:S(2)}) collective-permute-start(bf16[2,4,64,1536]{3,2,1,0:T(8,128)(2,1)S(1)} %get-tuple-element.35.refs_2_), channel_id=1, source_target_pairs={{0,1},{1,0},{2,3},{3,2},{4,5},{5,4},{6,7},{7,6},{8,9},{9,8},{10,11... | collective-permute-start | bytes 4718600 | tf_op jit(solution)/shard_map/ppermute | solution.py:388
  68.4 4.5 %collective-permute-start.10 = (bf16[3,2,64,1536]{3,2,1,0:T(8,128)(2,1)S(1)}, bf16[3,2,64,1536]{3,2,1,0:T(8,128)(2,1)S(1)}, u32[]{:S(2)}, u32[]{:S(2)}) collective-permute-start(bf16[3,2,64,1536]{3,2,1,0:T(8,128)(2,1)S(1)} %shard_map.106), channel_id=1, source_target_pairs={{0,1},{1,0},{2,3},{3,2},{4,5},{5,4},{6,7},{7,6},{8,9},{9,8},{10,11... | collective-permute-start | bytes 3538952 | tf_op jit(solution)/shard_map/ppermute | solution.py:388
  69.0 31.0 %collective-permute-start.9 = (bf16[2,64,1536]{2,1,0:T(8,128)(2,1)S(1)}, bf16[2,64,1536]{2,1,0:T(8,128)(2,1)S(1)}, u32[]{:S(2)}, u32[]{:S(2)}) collective-permute-start(bf16[2,64,1536]{2,1,0:T(8,128)(2,1)S(1)} %get-tuple-element.36), channel_id=1, source_target_pairs={{0,8},{8,0},{16,24},{24,16},{1,9},{9,1},{17,25},{25,17},{2,10},{10... | collective-permute-start | bytes 1179656 | tf_op jit(solution)/shard_map/ppermute | solution.py:391
  69.8 30.2 %collective-permute-start.11 = (bf16[2,64,1536]{2,1,0:T(8,128)(2,1)S(1)}, bf16[2,64,1536]{2,1,0:T(8,128)(2,1)S(1)}, u32[]{:S(2)}, u32[]{:S(2)}) collective-permute-start(bf16[2,64,1536]{2,1,0:T(8,128)(2,1)S(1)} %get-tuple-element.37), channel_id=1, source_target_pairs={{0,16},{8,24},{16,0},{24,8},{1,17},{9,25},{17,1},{25,9},{2,18},{10... | collective-permute-start | bytes 1179656 | tf_op jit(solution)/shard_map/ppermute | solution.py:391
  71.3 28.7 %collective-permute-start.12 = (bf16[2,64,1536]{2,1,0:T(8,128)(2,1)S(1)}, bf16[2,64,1536]{2,1,0:T(8,128)(2,1)S(1)}, u32[]{:S(2)}, u32[]{:S(2)}) collective-permute-start(bf16[2,64,1536]{2,1,0:T(8,128)(2,1)S(1)} %get-tuple-element.38), channel_id=1, source_target_pairs={{0,24},{8,16},{16,8},{24,0},{1,25},{9,17},{17,9},{25,1},{2,26},{10... | collective-permute-start | bytes 1179656 | tf_op jit(solution)/shard_map/ppermute | solution.py:391
  72.9 24.6 %copy-start.11 = (bf16[2,4,64,1536]{3,2,1,0:T(8,128)(2,1)}, bf16[2,4,64,1536]{3,2,1,0:T(8,128)(2,1)S(1)}, u32[]{:S(2)}) copy-start(bf16[2,4,64,1536]{3,2,1,0:T(8,128)(2,1)S(1)} %collective-permute-done.8.refs_5_) | copy-start | bytes 4718596
  97.5 3.0 %copy-start.12 = (bf16[256,3072]{1,0:T(8,128)(2,1)}, bf16[256,3072]{1,0:T(8,128)(2,1)S(1)}, u32[]{:S(2)}) copy-start(bf16[256,3072]{1,0:T(8,128)(2,1)S(1)} %get-tuple-element.40.refs_14_) | copy-start | bytes 4718596
  97.6 36.5 %collective-permute-start.14 = (bf16[256,3072]{1,0:T(8,128)(2,1)S(1)}, bf16[256,3072]{1,0:T(8,128)(2,1)S(1)}, u32[]{:S(2)}, u32[]{:S(2)}) collective-permute-start(bf16[256,3072]{1,0:T(8,128)(2,1)S(1)} %get-tuple-element.40.refs_14_), channel_id=1, source_target_pairs={{0,8},{8,0},{16,24},{24,16},{1,9},{9,1},{17,25},{25,17},{2,10},{10... | collective-permute-start | bytes 4718600 | tf_op jit(solution)/shard_map/ppermute | solution.py:391
  98.4 37.3 %collective-permute-start.17 = (bf16[256,3072]{1,0:T(8,128)(2,1)S(1)}, bf16[256,3072]{1,0:T(8,128)(2,1)S(1)}, u32[]{:S(2)}, u32[]{:S(2)}) collective-permute-start(bf16[256,3072]{1,0:T(8,128)(2,1)S(1)} %get-tuple-element.40.refs_14_), channel_id=1, source_target_pairs={{0,16},{8,24},{16,0},{24,8},{1,17},{9,25},{17,1},{25,9},{2,18},{10... | collective-permute-start | bytes 4718600 | tf_op jit(solution)/shard_map/ppermute | solution.py:391
  100.6 5.2 %collective-permute-start.13 = (bf16[3,2,64,1536]{3,2,1,0:T(8,128)(2,1)S(1)}, bf16[3,2,64,1536]{3,2,1,0:T(8,128)(2,1)S(1)}, u32[]{:S(2)}, u32[]{:S(2)}) collective-permute-start(bf16[3,2,64,1536]{3,2,1,0:T(8,128)(2,1)S(1)} %shard_map.108), channel_id=1, source_target_pairs={{0,1},{1,0},{2,3},{3,2},{4,5},{5,4},{6,7},{7,6},{8,9},{9,8},{10,11... | collective-permute-start | bytes 3538952 | tf_op jit(solution)/shard_map/ppermute | solution.py:388
  100.7 3.9 %collective-permute-start.15 = (bf16[128,3072]{1,0:T(8,128)(2,1)S(1)}, bf16[128,3072]{1,0:T(8,128)(2,1)S(1)}, u32[]{:S(2)}, u32[]{:S(2)}) collective-permute-start(bf16[128,3072]{1,0:T(8,128)(2,1)S(1)} %shard_map.109), channel_id=1, source_target_pairs={{0,1},{1,0},{2,3},{3,2},{4,5},{5,4},{6,7},{7,6},{8,9},{9,8},{10,11... | collective-permute-start | bytes 2359304 | tf_op jit(solution)/shard_map/ppermute | solution.py:388
  101.2 4.6 %collective-permute-start.16 = (bf16[128,3072]{1,0:T(8,128)(2,1)S(1)}, bf16[128,3072]{1,0:T(8,128)(2,1)S(1)}, u32[]{:S(2)}, u32[]{:S(2)}) collective-permute-start(bf16[128,3072]{1,0:T(8,128)(2,1)S(1)} %get-tuple-element.42), channel_id=1, source_target_pairs={{0,1},{1,0},{2,3},{3,2},{4,5},{5,4},{6,7},{7,6},{8,9},{9,8},{10,11... | collective-permute-start | bytes 2359304 | tf_op jit(solution)/shard_map/ppermute | solution.py:388
  106.1 44.5 %collective-permute-start.18 = (bf16[32,6144]{1,0:T(8,128)(2,1)S(1)}, bf16[32,6144]{1,0:T(8,128)(2,1)S(1)}, u32[]{:S(2)}, u32[]{:S(2)}) collective-permute-start(bf16[32,6144]{1,0:T(8,128)(2,1)S(1)} %get-tuple-element.45), channel_id=1, source_target_pairs={{0,6},{1,7},{2,0},{3,1},{4,2},{5,3},{6,4},{7,5},{8,14},{9,15},{10,... | collective-permute-start | bytes 1179656 | tf_op jit(solution)/shard_map/ppermute | solution.py:385
  107.9 42.8 %collective-permute-start.19 = (bf16[32,6144]{1,0:T(8,128)(2,1)S(1)}, bf16[32,6144]{1,0:T(8,128)(2,1)S(1)}, u32[]{:S(2)}, u32[]{:S(2)}) collective-permute-start(bf16[32,6144]{1,0:T(8,128)(2,1)S(1)} %get-tuple-element.46), channel_id=1, source_target_pairs={{0,2},{1,3},{2,4},{3,5},{4,6},{5,7},{6,0},{7,1},{8,10},{9,11},{10,... | collective-permute-start | bytes 1179656 | tf_op jit(solution)/shard_map/ppermute | solution.py:385
  108.2 42.5 %collective-permute-start.20 = (bf16[32,6144]{1,0:T(8,128)(2,1)S(1)}, bf16[32,6144]{1,0:T(8,128)(2,1)S(1)}, u32[]{:S(2)}, u32[]{:S(2)}) collective-permute-start(bf16[32,6144]{1,0:T(8,128)(2,1)S(1)} %get-tuple-element.47), channel_id=1, source_target_pairs={{0,4},{1,5},{2,6},{3,7},{4,0},{5,1},{6,2},{7,3},{8,12},{9,13},{10,... | collective-permute-start | bytes 1179656 | tf_op jit(solution)/shard_map/ppermute | solution.py:385
  134.1 1.7 %copy-start.1 = (bf16[256,3072]{1,0:T(8,128)(2,1)}, bf16[256,3072]{1,0:T(8,128)(2,1)S(1)}, u32[]{:S(2)}) copy-start(bf16[256,3072]{1,0:T(8,128)(2,1)S(1)} %shard_map.111.refs_15_) | copy-start | bytes 4718596
  134.1 18.8 %collective-permute-start.21 = (bf16[128,3072]{1,0:T(8,128)(2,1)S(1)}, bf16[128,3072]{1,0:T(8,128)(2,1)S(1)}, u32[]{:S(2)}, u32[]{:S(2)}) collective-permute-start(bf16[128,3072]{1,0:T(8,128)(2,1)S(1)} %slice.38), channel_id=1, source_target_pairs={{0,16},{8,24},{16,0},{24,8},{1,17},{9,25},{17,1},{25,9},{2,18},{10... | collective-permute-start | bytes 2359304 | tf_op jit(solution)/shard_map/ppermute | solution.py:391
  135.7 1.8 %copy-start = (bf16[256,3072]{1,0:T(8,128)(2,1)}, bf16[256,3072]{1,0:T(8,128)(2,1)S(1)}, u32[]{:S(2)}) copy-start(bf16[256,3072]{1,0:T(8,128)(2,1)S(1)} %shard_map.112.refs_16_) | copy-start | bytes 4718596
  135.8 18.5 %collective-permute-start.22 = (bf16[128,3072]{1,0:T(8,128)(2,1)S(1)}, bf16[128,3072]{1,0:T(8,128)(2,1)S(1)}, u32[]{:S(2)}, u32[]{:S(2)}) collective-permute-start(bf16[128,3072]{1,0:T(8,128)(2,1)S(1)} %slice.39), channel_id=1, source_target_pairs={{0,8},{8,0},{16,24},{24,16},{1,9},{9,1},{17,25},{25,17},{2,10},{10... | collective-permute-start | bytes 2359304 | tf_op jit(solution)/shard_map/ppermute | solution.py:391
  137.5 13.2 %copy-start.9 = (bf16[32,128]{1,0:T(8,128)(2,1)S(1)}, bf16[32,128]{1,0:T(8,128)(2,1)}, u32[]{:S(2)}) copy-start(bf16[32,128]{1,0:T(8,128)(2,1)} %get-tuple-element.29.sel) | copy-start | bytes 24580
  150.6 2.2 %copy-start.2 = (bf16[1024,1536]{1,0:T(8,128)(2,1)}, bf16[1024,1536]{1,0:T(8,128)(2,1)S(1)}, u32[]{:S(2)}) copy-start(bf16[1024,1536]{1,0:T(8,128)(2,1)S(1)} %get-tuple-element.50.refs_8_) | copy-start | bytes 9437188

commit v5 on v4

--- a/solution.py
+++ b/solution.py
@@ -206,8 +206,8 @@
         k, s = i // steps, i % steps
         forth.take(i)
         forth.start(i + 4)
-        if i >= len(spans) - 2:
-            back.start(i + 3 - len(spans))
+        if i >= len(spans) - 5:
+            back.start(min(2, i + 6 - len(spans)))
         some = jnp.concatenate([p[0, k, :, s * sub : (s + 1) * sub] for p in parts])
         for acc, j in ((gate, 0), (up, 1)):
             more = mm(some, wide[j, span])

time: 162 us -> 162 us (level)
  no operation moved by 1% of the time
where the time goes in v5:
time: 162 us
  waiting for transfers between devices  80 us (49%)
  Pallas kernels  55.2 us (34%)
  starting transfers between devices  23.4 us (14%)
  local copies, waits for them, and re-layouts  2.5 us (2%)
    ppermute x10, waiting for transfers between devices, across(): return lax.ppermute(x, 'dp', [(k, k ^ bits) for k in range(n_dp)])  42.2 us
    ppermute x6, waiting for transfers between devices, move(): return lax.ppermute(x, 'fetch', pairs)  32.9 us
    pallas_call x1, Pallas kernels, slab(): pl.pallas_call(kernel, out_shape=(shape((rows, 3 * ff)), shape((rows // 2...  25.4 us
    pallas_call x2, Pallas kernels, contract(): pl.pallas_call(functools.partial(contract_kernel, len(slices), len(grads)...  20.1 us
    ppermute x10, starting transfers between devices, across(): return lax.ppermute(x, 'dp', [(k, k ^ bits) for k in range(n_dp)])  13.6 us
    ppermute x6, starting transfers between devices, move(): return lax.ppermute(x, 'fetch', pairs)  8.55 us
    ppermute x7, waiting for transfers between devices, swap(): return lax.ppermute(x, 'fetch', [(k, k ^ 1) for k in range(n_fetch)])  4.87 us
    pallas_call x1, Pallas kernels, pick(): pl.pallas_call(pick_kernel, out_shape=(shape((CAP, n)),) + (shape((2, n_d...  4.3 us
  transfers between devices with their start and end apart: 23, of which 10 were waited for; matrix products, arithmetic and copies ran while one was open for 1% of the time, Pallas kernels for 26%

profile of v5, /device:TPU:0, one launch (start us, length us, event | category | flops | bytes accessed | tf_op | source)
XLA Modules:
  0.0 162.0 jit_solution(669808631149411205)
XLA Ops:
  0.6 4.3 %shard_map.102 = (bf16[32,128]{1,0:T(8,128)(2,1)}, bf16[2,4,32,1536]{3,2,1,0:T(8,128)(2,1)}, bf16[2,4,32,1536]{3,2,1,0:T(8,128)(2,1)}) custom-call(s32[1]{0:T(128)} %bitcast.me, s32[2,128]{1,0:T(2,128)} %bitcast.15, f32[2,128]{1,0:T(2,128)} %bitcast.16, bf16[128,6144]{1,0:T(8,128)(2,1)} %tokens.1, bf16[128,6144]{1,0:T(8,128)(2,1)} %out_grad.1), custom_call_target="tpu_custom_call" | custom-call | flops 1572864 | bytes 61440 | tf_op jit(solution)/shard_map/pallas_call | solution.py:74
  4.9 3.1 %collective-permute-start = (bf16[2,4,32,1536]{3,2,1,0:T(8,128)(2,1)}, bf16[2,4,32,1536]{3,2,1,0:T(8,128)(2,1)S(1)}, u32[]{:S(2)}, u32[]{:S(2)}) collective-permute-start(bf16[2,4,32,1536]{3,2,1,0:T(8,128)(2,1)} %get-tuple-element.30.refs_0_), channel_id=1, source_target_pairs={{0,2},{1,3},{2,4},{3,5},{4,6},{5,7},{6,0},{7,1},{8,10},{9,11},{10,... | collective-permute-start | bytes 2359304 | tf_op jit(solution)/shard_map/ppermute | solution.py:385
  8.0 19.8 %collective-permute-done.refs_1_ = bf16[2,4,32,1536]{3,2,1,0:T(8,128)(2,1)S(1)} collective-permute-done((bf16[2,4,32,1536]{3,2,1,0:T(8,128)(2,1)}, bf16[2,4,32,1536]{3,2,1,0:T(8,128)(2,1)S(1)}, u32[]{:S(2)}, u32[]{:S(2)}) %collective-permute-start) | collective-permute-done | bytes 786464 | tf_op jit(solution)/shard_map/ppermute | solution.py:385
  27.8 1.4 copy-done.5
  29.2 0.8 shard_map.104
  30.0 1.6 collective-permute-start.4
  31.6 1.7 %collective-permute-start.1 = (bf16[2,4,32,1536]{3,2,1,0:T(8,128)(2,1)S(1)}, bf16[2,4,32,1536]{3,2,1,0:T(8,128)(2,1)S(1)}, u32[]{:S(2)}, u32[]{:S(2)}) collective-permute-start(bf16[2,4,32,1536]{3,2,1,0:T(8,128)(2,1)S(1)} %shard_map.103), channel_id=1, source_target_pairs={{0,6},{1,7},{2,0},{3,1},{4,2},{5,3},{6,4},{7,5},{8,14},{9,15},{10,... | collective-permute-start | bytes 2359304 | tf_op jit(solution)/shard_map/ppermute | solution.py:385
  33.3 0.3 collective-permute-start.2
  33.6 1.5 collective-permute-start.5
  35.2 5.3 %collective-permute-done.4.refs_2_.refs_0_.refs_6_ = bf16[2,64,1536]{2,1,0:T(8,128)(2,1)S(1)} collective-permute-done((bf16[2,64,1536]{2,1,0:T(8,128)(2,1)S(1)}, bf16[2,64,1536]{2,1,0:T(8,128)(2,1)S(1)}, u32[]{:S(2)}, u32[]{:S(2)}) %collective-permute-start.4) | collective-permute-done | bytes 393248 | tf_op jit(solution)/shard_map/ppermute | solution.py:391
  40.4 2.2 %collective-permute-start.6 = (bf16[2,64,1536]{2,1,0:T(8,128)(2,1)S(1)}, bf16[2,64,1536]{2,1,0:T(8,128)(2,1)S(1)}, u32[]{:S(2)}, u32[]{:S(2)}) collective-permute-start(bf16[2,64,1536]{2,1,0:T(8,128)(2,1)S(1)} %get-tuple-element.34), channel_id=1, source_target_pairs={{0,24},{8,16},{16,8},{24,0},{1,25},{9,17},{17,9},{25,1},{2,26},{10... | collective-permute-start | bytes 1179656 | tf_op jit(solution)/shard_map/ppermute | solution.py:391
  42.6 11.0 %collective-permute-done.5.refs_3_.refs_1_.refs_10_ = bf16[2,64,1536]{2,1,0:T(8,128)(2,1)S(1)} collective-permute-done((bf16[2,64,1536]{2,1,0:T(8,128)(2,1)S(1)}, bf16[2,64,1536]{2,1,0:T(8,128)(2,1)S(1)}, u32[]{:S(2)}, u32[]{:S(2)}) %collective-permute-start.5) | collective-permute-done | bytes 393248 | tf_op jit(solution)/shard_map/ppermute | solution.py:391
  53.6 13.2 %collective-permute-done.2.refs_1_ = bf16[2,4,32,1536]{3,2,1,0:T(8,128)(2,1)S(1)} collective-permute-done((bf16[2,4,32,1536]{3,2,1,0:T(8,128)(2,1)S(1)}, bf16[2,4,32,1536]{3,2,1,0:T(8,128)(2,1)S(1)}, u32[]{:S(2)}, u32[]{:S(2)}) %collective-permute-start.2) | collective-permute-done | bytes 786464 | tf_op jit(solution)/shard_map/ppermute | solution.py:385
  66.8 0.9 shard_map.105
  67.7 0.1 collective-permute-start.8
  67.8 0.6 shard_map.106
  68.4 0.6 collective-permute-start.10
  69.0 0.8 collective-permute-start.9
  69.8 1.5 collective-permute-start.11
  71.3 1.2 collective-permute-start.12
  72.5 0.4 collective-permute-done.10.refs_9_
  72.9 0.0 copy-start.11
  72.9 25.4 %shard_map.107 = (bf16[256,3072]{1,0:T(8,128)(2,1)S(1)}, bf16[128,6144]{1,0:T(8,128)(2,1)S(1)}, bf16[128,3072]{1,0:T(8,128)(2,1)S(1)}, bf16[128,3072]{1,0:T(8,128)(2,1)S(1)}) custom-call(s32[1]{0:T(128)} %bitcast.me, bf16[2,4,32,1536]{3,2,1,0:T(8,128)(2,1)S(1)} %copy-done.6, bf16[2,4,32,1536]{3,2,1,0:T(8,128)(2,1)S(1)} %collective-permute-done.refs_1_, ...), custom_call_target="tpu_custom_call" | custom-call | flops 16106127360 | bytes 37748736 | tf_op jit(solution)/shard_map/pallas_call | solution.py:255
  98.3 0.0 copy-start.12
  98.3 0.9 collective-permute-start.14
  99.2 1.5 collective-permute-start.17
  100.7 0.6 shard_map.108
  101.4 0.1 collective-permute-start.13
  101.4 0.5 collective-permute-start.15
  101.9 0.1 collective-permute-start.16
  102.0 0.1 slice_bitcast_fusion.1
  102.1 3.3 %collective-permute-done.15.left = bf16[128,3072]{1,0:T(8,128)(2,1)S(1)} collective-permute-done((bf16[128,3072]{1,0:T(8,128)(2,1)S(1)}, bf16[128,3072]{1,0:T(8,128)(2,1)S(1)}, u32[]{:S(2)}, u32[]{:S(2)}) %collective-permute-start.15) | collective-permute-done | bytes 786464 | tf_op jit(solution)/shard_map/ppermute | solution.py:388
  105.4 1.1 collective-permute-done.16.right
  106.5 0.4 shard_map.110
  106.9 1.8 %collective-permute-start.18 = (bf16[32,6144]{1,0:T(8,128)(2,1)S(1)}, bf16[32,6144]{1,0:T(8,128)(2,1)S(1)}, u32[]{:S(2)}, u32[]{:S(2)}) collective-permute-start(bf16[32,6144]{1,0:T(8,128)(2,1)S(1)} %get-tuple-element.45), channel_id=1, source_target_pairs={{0,6},{1,7},{2,0},{3,1},{4,2},{5,3},{6,4},{7,5},{8,14},{9,15},{10,... | collective-permute-start | bytes 1179656 | tf_op jit(solution)/shard_map/ppermute | solution.py:385
  108.7 0.3 collective-permute-start.19
  109.0 1.4 collective-permute-start.20
  110.3 24.5 %collective-permute-done.14.refs_0_ = bf16[256,3072]{1,0:T(8,128)(2,1)S(1)} collective-permute-done((bf16[256,3072]{1,0:T(8,128)(2,1)S(1)}, bf16[256,3072]{1,0:T(8,128)(2,1)S(1)}, u32[]{:S(2)}, u32[]{:S(2)}) %collective-permute-start.14) | collective-permute-done | bytes 1572896 | tf_op jit(solution)/shard_map/ppermute | solution.py:391
  134.8 0.1 slice.38
  134.9 1.6 collective-permute-start.21
  136.5 0.1 slice.39
  136.5 0.9 collective-permute-start.22
  137.4 0.8 slice_bitcast_fusion
  138.3 13.1 %shard_map.113 = (bf16[1536,1024]{1,0:T(8,128)(2,1)S(1)}, bf16[1536,1024]{1,0:T(8,128)(2,1)S(1)}, bf16[1024,1536]{1,0:T(8,128)(2,1)S(1)}, f32[8,128]{1,0:T(8,128)S(1)}) custom-call(bf16[2,4,32,1536]{3,2,1,0:T(8,128)(2,1)} %get-tuple-element.30.refs_0_, bf16[2,4,32,1536]{3,2,1,0:T(8,128)(2,1)} %copy-done.3, bf16[2,4,64,1536]{3,2,1,0:T(8,128)(2,1)} %copy-done.10, ...), custom_call_target="tpu_custom_call" | custom-call | flops 7247757312 | bytes 28311552 | tf_op jit(solution)/shard_map/pallas_call | solution.py:366
  151.5 2.1 %shard_map.114 = bf16[128,6144]{1,0:T(8,128)(2,1)} custom-call(bf16[32,128]{1,0:T(8,128)(2,1)S(1)} %copy-done.9, f32[8,128]{1,0:T(8,128)S(1)} %get-tuple-element.44._, bf16[32,6144]{1,0:T(8,128)(2,1)S(1)} %get-tuple-element.43.refs_1_.refs_0_, bf16[32,6144]{1,0:T(8,128)(2,1)S(1)} %collective-permute-done.18.refs_1_, ...), custom_call_target="tpu_custom_call" | custom-call | flops 786432 | bytes 1572864 | tf_op jit(solution)/shard_map/pallas_call | solution.py:313
  153.6 0.1 collective-permute-done.21.refs_4_
  153.7 1.4 collective-permute-done.22.refs_5_
  155.1 6.9 %shard_map.115 = (bf16[1536,1024]{1,0:T(8,128)(2,1)}, bf16[1536,1024]{1,0:T(8,128)(2,1)}, bf16[1024,1536]{1,0:T(8,128)(2,1)}, f32[8,128]{1,0:T(8,128)}) custom-call(bf16[2,64,1536]{2,1,0:T(8,128)(2,1)S(1)} %collective-permute-done.6.refs_4_.refs_2_.refs_0_, bf16[2,64,1536]{2,1,0:T(8,128)(2,1)S(1)} %collective-permute-done.12.refs_2_.refs_3_.refs_1_, ...), custom_call_target="tpu_custom_call" | custom-call | flops 2415919104 | bytes 22020096 | tf_op jit(solution)/shard_map/pallas_call | solution.py:366
  (42 shorter events, 0.1 us)
Async XLA Ops:
  4.9 22.8 %collective-permute-start = (bf16[2,4,32,1536]{3,2,1,0:T(8,128)(2,1)}, bf16[2,4,32,1536]{3,2,1,0:T(8,128)(2,1)S(1)}, u32[]{:S(2)}, u32[]{:S(2)}) collective-permute-start(bf16[2,4,32,1536]{3,2,1,0:T(8,128)(2,1)} %get-tuple-element.30.refs_0_), channel_id=1, source_target_pairs={{0,2},{1,3},{2,4},{3,5},{4,6},{5,7},{6,0},{7,1},{8,10},{9,11},{10,... | collective-permute-start | bytes 2359304 | tf_op jit(solution)/shard_map/ppermute | solution.py:385
  8.0 19.8 %collective-permute-start.3 = (bf16[2,4,32,1536]{3,2,1,0:T(8,128)(2,1)}, bf16[2,4,32,1536]{3,2,1,0:T(8,128)(2,1)S(1)}, u32[]{:S(2)}, u32[]{:S(2)}) collective-permute-start(bf16[2,4,32,1536]{3,2,1,0:T(8,128)(2,1)} %get-tuple-element.30.refs_0_), channel_id=1, source_target_pairs={{0,1},{1,0},{2,3},{3,2},{4,5},{5,4},{6,7},{7,6},{8,9},{9,8},{10,11... | collective-permute-start | bytes 2359304 | tf_op jit(solution)/shard_map/ppermute | solution.py:388
  27.8 45.1 %copy-start.3 = (bf16[2,4,32,1536]{3,2,1,0:T(8,128)(2,1)}, bf16[2,4,32,1536]{3,2,1,0:T(8,128)(2,1)S(1)}, u32[]{:S(2)}) copy-start(bf16[2,4,32,1536]{3,2,1,0:T(8,128)(2,1)S(1)} %collective-permute-done.refs_1_) | copy-start | bytes 2359300
  27.8 1.4 copy-start.5
  29.2 43.7 %copy-start.7 = (bf16[2,4,32,1536]{3,2,1,0:T(8,128)(2,1)}, bf16[2,4,32,1536]{3,2,1,0:T(8,128)(2,1)S(1)}, u32[]{:S(2)}) copy-start(bf16[2,4,32,1536]{3,2,1,0:T(8,128)(2,1)S(1)} %collective-permute-done.3.refs_2_.refs_3_) | copy-start | bytes 2359300
  29.2 2.4 %copy-start.8 = (bf16[2,4,32,1536]{3,2,1,0:T(8,128)(2,1)S(1)}, bf16[2,4,32,1536]{3,2,1,0:T(8,128)(2,1)}, u32[]{:S(2)}) copy-start(bf16[2,4,32,1536]{3,2,1,0:T(8,128)(2,1)} %get-tuple-element.31.refs_0_) | copy-start | bytes 2359300
  30.0 10.4 %collective-permute-start.4 = (bf16[2,64,1536]{2,1,0:T(8,128)(2,1)S(1)}, bf16[2,64,1536]{2,1,0:T(8,128)(2,1)S(1)}, u32[]{:S(2)}, u32[]{:S(2)}) collective-permute-start(bf16[2,64,1536]{2,1,0:T(8,128)(2,1)S(1)} %get-tuple-element.32), channel_id=1, source_target_pairs={{0,8},{8,0},{16,24},{24,16},{1,9},{9,1},{17,25},{25,17},{2,10},{10... | collective-permute-start | bytes 1179656 | tf_op jit(solution)/shard_map/ppermute | solution.py:391
  31.6 22.0 %collective-permute-start.1 = (bf16[2,4,32,1536]{3,2,1,0:T(8,128)(2,1)S(1)}, bf16[2,4,32,1536]{3,2,1,0:T(8,128)(2,1)S(1)}, u32[]{:S(2)}, u32[]{:S(2)}) collective-permute-start(bf16[2,4,32,1536]{3,2,1,0:T(8,128)(2,1)S(1)} %shard_map.103), channel_id=1, source_target_pairs={{0,6},{1,7},{2,0},{3,1},{4,2},{5,3},{6,4},{7,5},{8,14},{9,15},{10,... | collective-permute-start | bytes 2359304 | tf_op jit(solution)/shard_map/ppermute | solution.py:385
  33.3 33.4 %collective-permute-start.2 = (bf16[2,4,32,1536]{3,2,1,0:T(8,128)(2,1)S(1)}, bf16[2,4,32,1536]{3,2,1,0:T(8,128)(2,1)S(1)}, u32[]{:S(2)}, u32[]{:S(2)}) collective-permute-start(bf16[2,4,32,1536]{3,2,1,0:T(8,128)(2,1)S(1)} %collective-permute-done.refs_1_), channel_id=1, source_target_pairs={{0,2},{1,3},{2,4},{3,5},{4,6},{5,7},{6,0},{7,1},{8,10},{9,11},{10,... | collective-permute-start | bytes 2359304 | tf_op jit(solution)/shard_map/ppermute | solution.py:385
  33.6 33.1 %collective-permute-start.7 = (bf16[2,4,32,1536]{3,2,1,0:T(8,128)(2,1)S(1)}, bf16[2,4,32,1536]{3,2,1,0:T(8,128)(2,1)S(1)}, u32[]{:S(2)}, u32[]{:S(2)}) collective-permute-start(bf16[2,4,32,1536]{3,2,1,0:T(8,128)(2,1)S(1)} %collective-permute-done.refs_1_), channel_id=1, source_target_pairs={{0,1},{1,0},{2,3},{3,2},{4,5},{5,4},{6,7},{7,6},{8,9},{9,8},{10,11... | collective-permute-start | bytes 2359304 | tf_op jit(solution)/shard_map/ppermute | solution.py:388
  33.6 20.0 %collective-permute-start.5 = (bf16[2,64,1536]{2,1,0:T(8,128)(2,1)S(1)}, bf16[2,64,1536]{2,1,0:T(8,128)(2,1)S(1)}, u32[]{:S(2)}, u32[]{:S(2)}) collective-permute-start(bf16[2,64,1536]{2,1,0:T(8,128)(2,1)S(1)} %get-tuple-element.33), channel_id=1, source_target_pairs={{0,16},{8,24},{16,0},{24,8},{1,17},{9,25},{17,1},{25,9},{2,18},{10... | collective-permute-start | bytes 1179656 | tf_op jit(solution)/shard_map/ppermute | solution.py:391
  40.4 13.2 %collective-permute-start.6 = (bf16[2,64,1536]{2,1,0:T(8,128)(2,1)S(1)}, bf16[2,64,1536]{2,1,0:T(8,128)(2,1)S(1)}, u32[]{:S(2)}, u32[]{:S(2)}) collective-permute-start(bf16[2,64,1536]{2,1,0:T(8,128)(2,1)S(1)} %get-tuple-element.34), channel_id=1, source_target_pairs={{0,24},{8,16},{16,8},{24,0},{1,25},{9,17},{17,9},{25,1},{2,26},{10... | collective-permute-start | bytes 1179656 | tf_op jit(solution)/shard_map/ppermute | solution.py:391
  66.8 6.2 %copy-start.4 = (bf16[2,4,32,1536]{3,2,1,0:T(8,128)(2,1)}, bf16[2,4,32,1536]{3,2,1,0:T(8,128)(2,1)S(1)}, u32[]{:S(2)}) copy-start(bf16[2,4,32,1536]{3,2,1,0:T(8,128)(2,1)S(1)} %collective-permute-done.7.refs_5_.refs_4_) | copy-start | bytes 2359300
  67.7 30.6 %copy-start.10 = (bf16[2,4,64,1536]{3,2,1,0:T(8,128)(2,1)}, bf16[2,4,64,1536]{3,2,1,0:T(8,128)(2,1)S(1)}, u32[]{:S(2)}) copy-start(bf16[2,4,64,1536]{3,2,1,0:T(8,128)(2,1)S(1)} %get-tuple-element.35.refs_2_) | copy-start | bytes 4718596
  67.7 5.2 %copy-start.6 = (bf16[2,4,32,1536]{3,2,1,0:T(8,128)(2,1)S(1)}, bf16[2,4,32,1536]{3,2,1,0:T(8,128)(2,1)}, u32[]{:S(2)}) copy-start(bf16[2,4,32,1536]{3,2,1,0:T(8,128)(2,1)} %get-tuple-element.30.refs_0_) | copy-start | bytes 2359300
  67.7 5.2 %collective-permute-start.8 = (bf16[2,4,64,1536]{3,2,1,0:T(8,128)(2,1)S(1)}, bf16[2,4,64,1536]{3,2,1,0:T(8,128)(2,1)S(1)}, u32[]{:S(2)}, u32[]{:S(2)}) collective-permute-start(bf16[2,4,64,1536]{3,2,1,0:T(8,128)(2,1)S(1)} %get-tuple-element.35.refs_2_), channel_id=1, source_target_pairs={{0,1},{1,0},{2,3},{3,2},{4,5},{5,4},{6,7},{7,6},{8,9},{9,8},{10,11... | collective-permute-start | bytes 4718600 | tf_op jit(solution)/shard_map/ppermute | solution.py:388
  68.4 4.5 %collective-permute-start.10 = (bf16[3,2,64,1536]{3,2,1,0:T(8,128)(2,1)S(1)}, bf16[3,2,64,1536]{3,2,1,0:T(8,128)(2,1)S(1)}, u32[]{:S(2)}, u32[]{:S(2)}) collective-permute-start(bf16[3,2,64,1536]{3,2,1,0:T(8,128)(2,1)S(1)} %shard_map.106), channel_id=1, source_target_pairs={{0,1},{1,0},{2,3},{3,2},{4,5},{5,4},{6,7},{7,6},{8,9},{9,8},{10,11... | collective-permute-start | bytes 3538952 | tf_op jit(solution)/shard_map/ppermute | solution.py:388
  69.0 31.8 %collective-permute-start.9 = (bf16[2,64,1536]{2,1,0:T(8,128)(2,1)S(1)}, bf16[2,64,1536]{2,1,0:T(8,128)(2,1)S(1)}, u32[]{:S(2)}, u32[]{:S(2)}) collective-permute-start(bf16[2,64,1536]{2,1,0:T(8,128)(2,1)S(1)} %get-tuple-element.36), channel_id=1, source_target_pairs={{0,8},{8,0},{16,24},{24,16},{1,9},{9,1},{17,25},{25,17},{2,10},{10... | collective-permute-start | bytes 1179656 | tf_op jit(solution)/shard_map/ppermute | solution.py:391
  69.8 31.0 %collective-permute-start.11 = (bf16[2,64,1536]{2,1,0:T(8,128)(2,1)S(1)}, bf16[2,64,1536]{2,1,0:T(8,128)(2,1)S(1)}, u32[]{:S(2)}, u32[]{:S(2)}) collective-permute-start(bf16[2,64,1536]{2,1,0:T(8,128)(2,1)S(1)} %get-tuple-element.37), channel_id=1, source_target_pairs={{0,16},{8,24},{16,0},{24,8},{1,17},{9,25},{17,1},{25,9},{2,18},{10... | collective-permute-start | bytes 1179656 | tf_op jit(solution)/shard_map/ppermute | solution.py:391
  71.3 29.4 %collective-permute-start.12 = (bf16[2,64,1536]{2,1,0:T(8,128)(2,1)S(1)}, bf16[2,64,1536]{2,1,0:T(8,128)(2,1)S(1)}, u32[]{:S(2)}, u32[]{:S(2)}) collective-permute-start(bf16[2,64,1536]{2,1,0:T(8,128)(2,1)S(1)} %get-tuple-element.38), channel_id=1, source_target_pairs={{0,24},{8,16},{16,8},{24,0},{1,25},{9,17},{17,9},{25,1},{2,26},{10... | collective-permute-start | bytes 1179656 | tf_op jit(solution)/shard_map/ppermute | solution.py:391
  72.9 25.4 %copy-start.11 = (bf16[2,4,64,1536]{3,2,1,0:T(8,128)(2,1)}, bf16[2,4,64,1536]{3,2,1,0:T(8,128)(2,1)S(1)}, u32[]{:S(2)}) copy-start(bf16[2,4,64,1536]{3,2,1,0:T(8,128)(2,1)S(1)} %collective-permute-done.8.refs_5_) | copy-start | bytes 4718596
  98.3 3.0 %copy-start.12 = (bf16[256,3072]{1,0:T(8,128)(2,1)}, bf16[256,3072]{1,0:T(8,128)(2,1)S(1)}, u32[]{:S(2)}) copy-start(bf16[256,3072]{1,0:T(8,128)(2,1)S(1)} %get-tuple-element.40.refs_14_) | copy-start | bytes 4718596
  98.3 36.5 %collective-permute-start.14 = (bf16[256,3072]{1,0:T(8,128)(2,1)S(1)}, bf16[256,3072]{1,0:T(8,128)(2,1)S(1)}, u32[]{:S(2)}, u32[]{:S(2)}) collective-permute-start(bf16[256,3072]{1,0:T(8,128)(2,1)S(1)} %get-tuple-element.40.refs_14_), channel_id=1, source_target_pairs={{0,8},{8,0},{16,24},{24,16},{1,9},{9,1},{17,25},{25,17},{2,10},{10... | collective-permute-start | bytes 4718600 | tf_op jit(solution)/shard_map/ppermute | solution.py:391
  99.2 37.3 %collective-permute-start.17 = (bf16[256,3072]{1,0:T(8,128)(2,1)S(1)}, bf16[256,3072]{1,0:T(8,128)(2,1)S(1)}, u32[]{:S(2)}, u32[]{:S(2)}) collective-permute-start(bf16[256,3072]{1,0:T(8,128)(2,1)S(1)} %get-tuple-element.40.refs_14_), channel_id=1, source_target_pairs={{0,16},{8,24},{16,0},{24,8},{1,17},{9,25},{17,1},{25,9},{2,18},{10... | collective-permute-start | bytes 4718600 | tf_op jit(solution)/shard_map/ppermute | solution.py:391
  101.4 5.2 %collective-permute-start.13 = (bf16[3,2,64,1536]{3,2,1,0:T(8,128)(2,1)S(1)}, bf16[3,2,64,1536]{3,2,1,0:T(8,128)(2,1)S(1)}, u32[]{:S(2)}, u32[]{:S(2)}) collective-permute-start(bf16[3,2,64,1536]{3,2,1,0:T(8,128)(2,1)S(1)} %shard_map.108), channel_id=1, source_target_pairs={{0,1},{1,0},{2,3},{3,2},{4,5},{5,4},{6,7},{7,6},{8,9},{9,8},{10,11... | collective-permute-start | bytes 3538952 | tf_op jit(solution)/shard_map/ppermute | solution.py:388
  101.4 3.9 %collective-permute-start.15 = (bf16[128,3072]{1,0:T(8,128)(2,1)S(1)}, bf16[128,3072]{1,0:T(8,128)(2,1)S(1)}, u32[]{:S(2)}, u32[]{:S(2)}) collective-permute-start(bf16[128,3072]{1,0:T(8,128)(2,1)S(1)} %shard_map.109), channel_id=1, source_target_pairs={{0,1},{1,0},{2,3},{3,2},{4,5},{5,4},{6,7},{7,6},{8,9},{9,8},{10,11... | collective-permute-start | bytes 2359304 | tf_op jit(solution)/shard_map/ppermute | solution.py:388
  101.9 4.6 %collective-permute-start.16 = (bf16[128,3072]{1,0:T(8,128)(2,1)S(1)}, bf16[128,3072]{1,0:T(8,128)(2,1)S(1)}, u32[]{:S(2)}, u32[]{:S(2)}) collective-permute-start(bf16[128,3072]{1,0:T(8,128)(2,1)S(1)} %get-tuple-element.42), channel_id=1, source_target_pairs={{0,1},{1,0},{2,3},{3,2},{4,5},{5,4},{6,7},{7,6},{8,9},{9,8},{10,11... | collective-permute-start | bytes 2359304 | tf_op jit(solution)/shard_map/ppermute | solution.py:388
  106.9 44.6 %collective-permute-start.18 = (bf16[32,6144]{1,0:T(8,128)(2,1)S(1)}, bf16[32,6144]{1,0:T(8,128)(2,1)S(1)}, u32[]{:S(2)}, u32[]{:S(2)}) collective-permute-start(bf16[32,6144]{1,0:T(8,128)(2,1)S(1)} %get-tuple-element.45), channel_id=1, source_target_pairs={{0,6},{1,7},{2,0},{3,1},{4,2},{5,3},{6,4},{7,5},{8,14},{9,15},{10,... | collective-permute-start | bytes 1179656 | tf_op jit(solution)/shard_map/ppermute | solution.py:385
  108.7 42.8 %collective-permute-start.19 = (bf16[32,6144]{1,0:T(8,128)(2,1)S(1)}, bf16[32,6144]{1,0:T(8,128)(2,1)S(1)}, u32[]{:S(2)}, u32[]{:S(2)}) collective-permute-start(bf16[32,6144]{1,0:T(8,128)(2,1)S(1)} %get-tuple-element.46), channel_id=1, source_target_pairs={{0,2},{1,3},{2,4},{3,5},{4,6},{5,7},{6,0},{7,1},{8,10},{9,11},{10,... | collective-permute-start | bytes 1179656 | tf_op jit(solution)/shard_map/ppermute | solution.py:385
  109.0 42.5 %collective-permute-start.20 = (bf16[32,6144]{1,0:T(8,128)(2,1)S(1)}, bf16[32,6144]{1,0:T(8,128)(2,1)S(1)}, u32[]{:S(2)}, u32[]{:S(2)}) collective-permute-start(bf16[32,6144]{1,0:T(8,128)(2,1)S(1)} %get-tuple-element.47), channel_id=1, source_target_pairs={{0,4},{1,5},{2,6},{3,7},{4,0},{5,1},{6,2},{7,3},{8,12},{9,13},{10,... | collective-permute-start | bytes 1179656 | tf_op jit(solution)/shard_map/ppermute | solution.py:385
  134.8 1.6 %copy-start.1 = (bf16[256,3072]{1,0:T(8,128)(2,1)}, bf16[256,3072]{1,0:T(8,128)(2,1)S(1)}, u32[]{:S(2)}) copy-start(bf16[256,3072]{1,0:T(8,128)(2,1)S(1)} %shard_map.111.refs_15_) | copy-start | bytes 4718596
  134.9 18.8 %collective-permute-start.21 = (bf16[128,3072]{1,0:T(8,128)(2,1)S(1)}, bf16[128,3072]{1,0:T(8,128)(2,1)S(1)}, u32[]{:S(2)}, u32[]{:S(2)}) collective-permute-start(bf16[128,3072]{1,0:T(8,128)(2,1)S(1)} %slice.38), channel_id=1, source_target_pairs={{0,16},{8,24},{16,0},{24,8},{1,17},{9,25},{17,1},{25,9},{2,18},{10... | collective-permute-start | bytes 2359304 | tf_op jit(solution)/shard_map/ppermute | solution.py:391
  136.5 1.8 %copy-start = (bf16[256,3072]{1,0:T(8,128)(2,1)}, bf16[256,3072]{1,0:T(8,128)(2,1)S(1)}, u32[]{:S(2)}) copy-start(bf16[256,3072]{1,0:T(8,128)(2,1)S(1)} %shard_map.112.refs_16_) | copy-start | bytes 4718596
  136.5 18.5 %collective-permute-start.22 = (bf16[128,3072]{1,0:T(8,128)(2,1)S(1)}, bf16[128,3072]{1,0:T(8,128)(2,1)S(1)}, u32[]{:S(2)}, u32[]{:S(2)}) collective-permute-start(bf16[128,3072]{1,0:T(8,128)(2,1)S(1)} %slice.39), channel_id=1, source_target_pairs={{0,8},{8,0},{16,24},{24,16},{1,9},{9,1},{17,25},{25,17},{2,10},{10... | collective-permute-start | bytes 2359304 | tf_op jit(solution)/shard_map/ppermute | solution.py:391
  138.3 13.2 %copy-start.9 = (bf16[32,128]{1,0:T(8,128)(2,1)S(1)}, bf16[32,128]{1,0:T(8,128)(2,1)}, u32[]{:S(2)}) copy-start(bf16[32,128]{1,0:T(8,128)(2,1)} %get-tuple-element.29.sel) | copy-start | bytes 24580
  151.4 2.2 %copy-start.2 = (bf16[1024,1536]{1,0:T(8,128)(2,1)}, bf16[1024,1536]{1,0:T(8,128)(2,1)S(1)}, u32[]{:S(2)}) copy-start(bf16[1024,1536]{1,0:T(8,128)(2,1)S(1)} %get-tuple-element.50.refs_8_) | copy-start | bytes 9437188
